TPU v7x, 128 devices: a whole 4x4x4 slice. The times are simulated.
128 devices in a mesh: section: 4 (over y_lo, core), dp: 32 (over z, x, y_hi).
Axes of the slice: x: 4, y: 4 (y_hi: 2, y_lo: 2; y = y_hi * 2 + y_lo), z: 4, core: 2. Of those that a mesh axis runs over, the one named last changes fastest.
Arguments:
- inputs: bfloat16 [2, 64, 160, 768], P(None, 'dp'), may hold values from -6 to 6
- cotangent: bfloat16 [2, 64, 160, 768], P(None, 'dp'), may hold values from -6 to 6
- lengths: int32 [2, 64], P(None, 'dp'), may hold values from 80 to 160, as said below
- cdr_spans: int32 [2, 64, 2], P(None, 'dp'), may hold values from 0 to 160, as said below
- mask_vector: bfloat16 [768], replicated, may hold values from -6 to 6
- w_qkv: bfloat16 [1536, 2304], P('section'), may hold values from -0.21875 to 0.21875
- qv_bias: bfloat16 [3072], P('section'), may hold values from -2 to 2
- w_out: bfloat16 [1536, 768], P('section'), may hold values from -1.75 to 1.75
- b_out: bfloat16 [1536], P('section'), may hold values from -2 to 2
- norm1_gain: bfloat16 [1536], P('section'), may hold values from 0.5 to 1.5
- norm1_bias: bfloat16 [1536], P('section'), may hold values from -2 to 2
- w_up: bfloat16 [1536, 3072], P('section'), may hold values from -0.21875 to 0.21875
- b_up: bfloat16 [6144], P('section'), may hold values from -2 to 2
- w_down: bfloat16 [6144, 768], P('section'), may hold values from -0.15625 to 0.15625
- b_down: bfloat16 [1536], P('section'), may hold values from -2 to 2
- norm2_gain: bfloat16 [1536], P('section'), may hold values from 0.5 to 1.5
- norm2_bias: bfloat16 [1536], P('section'), may hold values from -2 to 2
Outputs:
- layer_outputs: bfloat16 [4, 64, 160, 768], P('section', 'dp')
- input_grads: bfloat16 [4, 64, 160, 768], P('section', 'dp')
- mask_grad: float32 [768], replicated
- grad_w_qkv: float32 [1536, 2304], P('section')
- grad_qv_bias: float32 [3072], P('section')
- grad_w_out: float32 [1536, 768], P('section')
- grad_b_out: float32 [1536], P('section')
- grad_norm1_gain: float32 [1536], P('section')
- grad_norm1_bias: float32 [1536], P('section')
- grad_w_up: float32 [1536, 3072], P('section')
- grad_b_up: float32 [6144], P('section')
- grad_w_down: float32 [6144, 768], P('section')
- grad_b_down: float32 [1536], P('section')
- grad_norm2_gain: float32 [1536], P('section')
- grad_norm2_bias: float32 [1536], P('section')
Inputs may be any that keep to these rules, and one draw needn't show every extreme that they name: `lengths`: positions from a chain's length to 159 are padding. `cdr_spans`: start < end <= the chain's length and end - start <= 12.
All inputs are finite; a program needn't handle non-finite values.
Results may differ from a plain program's by a relative error of at most 0.03.
Values may be sent and summed in bfloat16 or wider, within the bound.
No kernel may reach another device: no remote copies, remote signals or barrier semaphores. Data moves between devices by JAX's collectives and lax.ppermute only.
A program may use at most 256 MiB of HBM per device.

v0:
```python
import math

import jax
import jax.numpy as jnp
from jax import lax
from jax.sharding import PartitionSpec as P

HEADS = 12
MICRO = 2


EPSILON = 1e-05


def partner(x, axis, bit):
    return lax.ppermute(x, axis, [(i, i ^ 1 << bit) for i in range(lax.axis_size(axis))])


def shifted(value, axis, steps):
    count = lax.axis_size(axis)
    leading, last = (max(0, -steps), min(count, count - steps))
    return lax.ppermute(value, axis, [(source, source + steps) for source in range(leading, last)])


def norm_rows(values, norm_gain, norm_shift):
    center = values - jnp.mean(values, axis=-1, keepdims=True)
    spread = jnp.mean(center * center, axis=-1, keepdims=True)
    return center * lax.rsqrt(spread + EPSILON) * norm_gain + norm_shift


def gelu_exact(values):
    return jax.nn.gelu(values, approximate=False)


def contract_rows(left_side, right_side):
    return lax.dot_general(
        left_side, right_side, (((0,), (0,)), ((), ())), preferred_element_type=jnp.float32
    )


def contract_cols(left_side, right_side):
    return lax.dot_general(
        left_side, right_side, (((1,), (1,)), ((), ())), preferred_element_type=jnp.float32
    )


def assemble(own_part, partner_part, pair_half):
    lower = jnp.where(pair_half == 0, own_part, partner_part)
    upper = jnp.where(pair_half == 0, partner_part, own_part)
    return jnp.concatenate([lower, upper], axis=0)


def take_half(tensor, which_half):
    half_rows = tensor.shape[0] // 2
    return lax.dynamic_slice_in_dim(tensor, which_half * half_rows, half_rows, 0)


def clamp_pick(sequence, micro_no):
    return sequence[min(max(micro_no, 0), len(sequence) - 1)]


def forward_parts(layer_in, params, key_valid):
    (
        w_qkv,
        qv_bias,
        w_out,
        b_out,
        norm1_gain,
        norm1_bias,
        w_up,
        b_up,
        w_down,
        b_down,
        norm2_gain,
        norm2_bias,
    ) = params
    chains, length, model_width = layer_in.shape
    head_dim = model_width // HEADS
    scale = 1.0 / math.sqrt(head_dim)
    rows_in = layer_in.reshape(-1, model_width)
    full_bias = jnp.concatenate(
        [
            qv_bias[:model_width].astype(jnp.float32),
            jnp.zeros((model_width,), jnp.float32),
            qv_bias[model_width:].astype(jnp.float32),
        ]
    )
    projected = (jnp.dot(rows_in, w_qkv, preferred_element_type=jnp.float32) + full_bias).astype(
        jnp.bfloat16
    )
    projected = projected.reshape(chains, length, 3, HEADS, head_dim)
    queries = projected[:, :, 0]
    key_heads = projected[:, :, 1]
    value_heads = projected[:, :, 2]
    scores = (
        jnp.einsum("clhe,cmhe->chlm", queries, key_heads, preferred_element_type=jnp.float32)
        * scale
    )
    scores = jnp.where(key_valid[:, None, None, :], scores, -1000000000.0)
    top_score = jnp.max(scores, axis=-1, keepdims=True)
    log_total = top_score + jnp.log(jnp.sum(jnp.exp(scores - top_score), axis=-1, keepdims=True))
    softmax_w = jnp.exp(scores - log_total)
    weights_low = softmax_w.astype(jnp.bfloat16)
    attended = jnp.einsum(
        "chlm,cmhe->clhe", weights_low, value_heads, preferred_element_type=jnp.float32
    )
    attended = attended.reshape(-1, model_width).astype(jnp.bfloat16)
    branch = jnp.dot(attended, w_out, preferred_element_type=jnp.float32) + b_out.astype(
        jnp.float32
    )
    residual_one = rows_in.astype(jnp.float32) + branch
    normed_low = norm_rows(
        residual_one, norm1_gain.astype(jnp.float32), norm1_bias.astype(jnp.float32)
    ).astype(jnp.bfloat16)
    hidden_pre = jnp.dot(normed_low, w_up, preferred_element_type=jnp.float32) + b_up.astype(
        jnp.float32
    )
    active_low = gelu_exact(hidden_pre).astype(jnp.bfloat16)
    second = jnp.dot(active_low, w_down, preferred_element_type=jnp.float32) + b_down.astype(
        jnp.float32
    )
    residual_two = normed_low.astype(jnp.float32) + second
    output = norm_rows(residual_two, norm2_gain.astype(jnp.float32), norm2_bias.astype(jnp.float32))
    kept_parts = (
        rows_in,
        queries,
        key_heads,
        value_heads,
        softmax_w,
        weights_low,
        attended,
        residual_one,
        normed_low,
        hidden_pre,
        active_low,
        residual_two,
    )
    return (output.reshape(chains, length, model_width), kept_parts)


def layer_backward(layer_in, params, key_valid, upstream):
    (
        w_qkv,
        qv_bias,
        w_out,
        b_out,
        norm1_gain,
        norm1_bias,
        w_up,
        b_up,
        w_down,
        b_down,
        norm2_gain,
        norm2_bias,
    ) = params
    chains, length, model_width = layer_in.shape
    head_dim = model_width // HEADS
    scale = 1.0 / math.sqrt(head_dim)
    output, kept_parts = forward_parts(layer_in, params, key_valid)
    (
        rows_in,
        queries,
        key_heads,
        value_heads,
        softmax_w,
        weights_low,
        attended,
        residual_one,
        normed_low,
        hidden_pre,
        active_low,
        residual_two,
    ) = kept_parts
    primal_two, norm_two_pull = jax.vjp(
        norm_rows, residual_two, norm2_gain.astype(jnp.float32), norm2_bias.astype(jnp.float32)
    )
    d_res_two, d_norm2_gain, d_norm2_bias = norm_two_pull(upstream.reshape(-1, model_width))
    d_second = d_res_two.astype(jnp.bfloat16)
    d_w_down = contract_rows(active_low, d_second)
    d_b_down = jnp.sum(d_second.astype(jnp.float32), axis=0)
    d_active = contract_cols(d_second, w_down)
    primal_gelu, gelu_pull = jax.vjp(gelu_exact, hidden_pre)
    d_hidden = gelu_pull(d_active)[0].astype(jnp.bfloat16)
    d_w_up = contract_rows(normed_low, d_hidden)
    d_b_up = jnp.sum(d_hidden.astype(jnp.float32), axis=0)
    d_normed = d_res_two + contract_cols(d_hidden, w_up)
    primal_one, norm_one_pull = jax.vjp(
        norm_rows, residual_one, norm1_gain.astype(jnp.float32), norm1_bias.astype(jnp.float32)
    )
    d_res_one, d_norm1_gain, d_norm1_bias = norm_one_pull(d_normed)
    d_branch = d_res_one.astype(jnp.bfloat16)
    d_w_out = contract_rows(attended, d_branch)
    d_b_out = jnp.sum(d_branch.astype(jnp.float32), axis=0)
    d_attended = (
        contract_cols(d_branch, w_out).astype(jnp.bfloat16).reshape(chains, length, HEADS, head_dim)
    )
    d_weights = jnp.einsum(
        "clhe,cmhe->chlm", d_attended, value_heads, preferred_element_type=jnp.float32
    )
    row_term = jnp.sum(softmax_w * d_weights, axis=-1, keepdims=True)
    d_scores = (softmax_w * (d_weights - row_term)).astype(jnp.bfloat16)
    d_queries = (
        jnp.einsum("chlm,cmhe->clhe", d_scores, key_heads, preferred_element_type=jnp.float32)
        * scale
    )
    d_keys = (
        jnp.einsum("chlm,clhe->cmhe", d_scores, queries, preferred_element_type=jnp.float32) * scale
    )
    d_values = jnp.einsum(
        "chlm,clhe->cmhe", weights_low, d_attended, preferred_element_type=jnp.float32
    )
    d_projected = (
        jnp.stack([d_queries, d_keys, d_values], axis=2)
        .reshape(-1, 3 * model_width)
        .astype(jnp.bfloat16)
    )
    d_w_qkv = contract_rows(rows_in, d_projected)
    column_sums = jnp.sum(d_projected.astype(jnp.float32), axis=0)
    d_qv_bias = jnp.concatenate([column_sums[:model_width], column_sums[2 * model_width :]])
    d_input = d_res_one + contract_cols(d_projected, w_qkv)
    layer_grads = (
        d_w_qkv,
        d_qv_bias,
        d_w_out,
        d_b_out,
        d_norm1_gain,
        d_norm1_bias,
        d_w_up,
        d_b_up,
        d_w_down,
        d_b_down,
        d_norm2_gain,
        d_norm2_bias,
    )
    return (d_input.reshape(chains, length, model_width), layer_grads)


def per_device(
    inputs,
    cotangent,
    lengths,
    cdr_spans,
    mask_vector,
    w_qkv,
    qv_bias,
    w_out,
    b_out,
    norm1_gain,
    norm1_bias,
    w_up,
    b_up,
    w_down,
    b_down,
    norm2_gain,
    norm2_bias,
):
    section_index = lax.axis_index("section")
    is_first = section_index < 2
    pair_half = section_index % 2
    own_params = (
        w_qkv,
        qv_bias,
        w_out,
        b_out,
        norm1_gain,
        norm1_bias,
        w_up,
        b_up,
        w_down,
        b_down,
        norm2_gain,
        norm2_bias,
    )
    partner_params = partner(
        (
            w_qkv,
            qv_bias,
            w_out,
            b_out,
            norm1_gain,
            norm1_bias,
            w_up,
            b_up,
            w_down,
            b_down,
            norm2_gain,
            norm2_bias,
        ),
        "section",
        0,
    )
    params = tuple(
        (
            assemble(own_part, partner_part, pair_half)
            for own_part, partner_part in zip(own_params, partner_params)
        )
    )
    my_inputs = lax.dynamic_index_in_dim(inputs, pair_half, 0, keepdims=False)
    my_cotangent = lax.dynamic_index_in_dim(cotangent, pair_half, 0, keepdims=False)
    my_lengths = lax.dynamic_index_in_dim(lengths, pair_half, 0, keepdims=False)
    my_spans = lax.dynamic_index_in_dim(cdr_spans, pair_half, 0, keepdims=False)
    chain_rows, seq_len, model_width = my_inputs.shape
    positions = jnp.arange(seq_len, dtype=jnp.int32)
    key_valid = positions[None, :] < my_lengths[:, None]
    masked = (positions[None, :] >= my_spans[:, 0:1]) & (positions[None, :] < my_spans[:, 1:2])
    entered = jnp.where(masked[:, :, None], mask_vector[None, None, :], my_inputs)
    per_micro = chain_rows // MICRO

    def micro_of(tensor, micro_no):
        clamped = min(max(micro_no, 0), MICRO - 1)
        return tensor[clamped * per_micro : (clamped + 1) * per_micro]

    blank_block = jnp.zeros((per_micro, seq_len, model_width), jnp.bfloat16)
    received = blank_block
    tick_inputs = []
    tick_outputs = []
    for tick_no in range(MICRO + 1):
        fresh = micro_of(entered, tick_no) if tick_no < MICRO else blank_block
        layer_in = jnp.where(is_first, fresh, received)
        valid_now = jnp.where(
            is_first, micro_of(key_valid, tick_no), micro_of(key_valid, tick_no - 1)
        )
        output, kept_parts = forward_parts(layer_in, params, valid_now)
        sent = output.astype(jnp.bfloat16)
        tick_inputs.append(layer_in)
        tick_outputs.append(sent)
        if tick_no < MICRO:
            received = shifted(sent, "section", 2)
    section_inputs = [
        jnp.where(is_first, tick_inputs[micro_no], tick_inputs[micro_no + 1])
        for micro_no in range(MICRO)
    ]
    section_outputs = [
        jnp.where(is_first, tick_outputs[micro_no], tick_outputs[micro_no + 1])
        for micro_no in range(MICRO)
    ]
    layer_outputs = jnp.concatenate(section_outputs, axis=0)[None]
    grad_totals = tuple((jnp.zeros(tensor.shape, jnp.float32) for tensor in params))
    returned = blank_block
    tick_grads = []
    for tick_no in range(MICRO + 1):
        from_loss = micro_of(my_cotangent, tick_no) if tick_no < MICRO else blank_block
        upstream = jnp.where(is_first, returned, from_loss).astype(jnp.float32)
        saved_in = jnp.where(
            is_first, clamp_pick(section_inputs, tick_no - 1), clamp_pick(section_inputs, tick_no)
        )
        valid_now = jnp.where(
            is_first, micro_of(key_valid, tick_no - 1), micro_of(key_valid, tick_no)
        )
        down_grad, layer_grads = layer_backward(saved_in, params, valid_now, upstream)
        grad_totals = tuple(
            (total + fresh_grad for total, fresh_grad in zip(grad_totals, layer_grads))
        )
        sent_back = down_grad.astype(jnp.bfloat16)
        tick_grads.append(down_grad)
        if tick_no < MICRO:
            returned = shifted(sent_back, "section", -2)
    all_grads = jnp.concatenate(
        [
            jnp.where(is_first, tick_grads[micro_no + 1], tick_grads[micro_no])
            for micro_no in range(MICRO)
        ],
        axis=0,
    )
    dropped = masked[:, :, None] & is_first
    input_grads = jnp.where(dropped, 0.0, all_grads).astype(jnp.bfloat16)[None]
    mask_term = jnp.sum(jnp.where(dropped, all_grads, 0.0), axis=(0, 1))
    mask_grad = lax.psum(mask_term, ("section", "dp"))
    summed = (
        lax.psum(grad_totals[0].astype(jnp.bfloat16), "dp").astype(jnp.float32),
        lax.psum(grad_totals[1].astype(jnp.bfloat16), "dp").astype(jnp.float32),
        lax.psum(grad_totals[2].astype(jnp.bfloat16), "dp").astype(jnp.float32),
        lax.psum(grad_totals[3].astype(jnp.bfloat16), "dp").astype(jnp.float32),
        lax.psum(grad_totals[4].astype(jnp.bfloat16), "dp").astype(jnp.float32),
        lax.psum(grad_totals[5].astype(jnp.bfloat16), "dp").astype(jnp.float32),
        lax.psum(grad_totals[6].astype(jnp.bfloat16), "dp").astype(jnp.float32),
        lax.psum(grad_totals[7].astype(jnp.bfloat16), "dp").astype(jnp.float32),
        lax.psum(grad_totals[8].astype(jnp.bfloat16), "dp").astype(jnp.float32),
        lax.psum(grad_totals[9].astype(jnp.bfloat16), "dp").astype(jnp.float32),
        lax.psum(grad_totals[10].astype(jnp.bfloat16), "dp").astype(jnp.float32),
        lax.psum(grad_totals[11].astype(jnp.bfloat16), "dp").astype(jnp.float32),
    )
    outgoing = tuple((take_half(tensor, 1 - pair_half) for tensor in summed))
    incoming = (
        partner(outgoing[0].astype(jnp.bfloat16), "section", 0).astype(jnp.float32),
        partner(outgoing[1].astype(jnp.bfloat16), "section", 0).astype(jnp.float32),
        partner(outgoing[2].astype(jnp.bfloat16), "section", 0).astype(jnp.float32),
        partner(outgoing[3].astype(jnp.bfloat16), "section", 0).astype(jnp.float32),
        partner(outgoing[4].astype(jnp.bfloat16), "section", 0).astype(jnp.float32),
        partner(outgoing[5].astype(jnp.bfloat16), "section", 0).astype(jnp.float32),
        partner(outgoing[6].astype(jnp.bfloat16), "section", 0).astype(jnp.float32),
        partner(outgoing[7].astype(jnp.bfloat16), "section", 0).astype(jnp.float32),
        partner(outgoing[8].astype(jnp.bfloat16), "section", 0).astype(jnp.float32),
        partner(outgoing[9].astype(jnp.bfloat16), "section", 0).astype(jnp.float32),
        partner(outgoing[10].astype(jnp.bfloat16), "section", 0).astype(jnp.float32),
        partner(outgoing[11].astype(jnp.bfloat16), "section", 0).astype(jnp.float32),
    )
    reduced = tuple(
        (take_half(tensor, pair_half) + other_part for tensor, other_part in zip(summed, incoming))
    )
    return (layer_outputs, input_grads, mask_grad) + tuple(reduced)


def solution(mesh):
    in_specs = (
        P(None, "dp", None, None),
        P(None, "dp", None, None),
        P(None, "dp"),
        P(None, "dp", None),
        P(),
        P("section", None),
        P("section"),
        P("section", None),
        P("section"),
        P("section"),
        P("section"),
        P("section", None),
        P("section"),
        P("section", None),
        P("section"),
        P("section"),
        P("section"),
    )
    out_specs = (
        P("section", "dp", None, None),
        P("section", "dp", None, None),
        P(),
        P("section", None),
        P("section"),
        P("section", None),
        P("section"),
        P("section"),
        P("section"),
        P("section", None),
        P("section"),
        P("section", None),
        P("section"),
        P("section"),
        P("section"),
    )
    return jax.shard_map(
        per_device, mesh=mesh, in_specs=in_specs, out_specs=out_specs, check_vma=False
    )
```

profile of v0, /device:TPU:0, one launch (start us, length us, event | category | flops | bytes accessed | tf_op | source)
XLA Modules:
  0.0 947.3 jit_solution(13258252334719306996)
XLA Ops:
  15.6 1.7 collective-permute-done.1
  19.1 2.0 broadcast_select_fusion.7
  27.9 3.6 broadcast_select_fusion.1
  31.5 5.0 broadcast_select_fusion.3
  36.5 9.2 fusion.365
  46.1 4.0 collective-permute-start.12
  50.0 5.5 collective-permute-done.12
  56.2 3.1 fusion.1
  59.4 2.3 copy.73
  61.6 1.7 fusion.366
  66.8 9.9 %fusion.368 = (f32[160]{0:T(256)S(1)}, f32[160,768]{1,0:T(8,128)}) fusion(f32[768]{0:T(1024)S(1)} %maximum_convert_fusion.7, bf16[1536,768]{1,0:T(8,128)(2,1)} %get-tuple-element.94, bf16[1536,768]{1,0:T(8,128)(2,1)S(1)} %get-tuple-element.93, f32[3072]{0:T(1024)S(1)} %maximum_convert_fusion.3, f32[160,768]{1,0:T(8,128)} %copy-done.129, ...), kind=kOutput, calls=%fused_computation.698 | convolution fusion | flops 1562984320 | bytes 10443648 | tf_op jit(solution)/shard_map/dot_general | solution.py:119
  78.1 2.0 select_bitcast_fusion
  80.1 4.9 collective-permute-start.13
  84.9 4.4 collective-permute-done.13
  89.4 1.8 broadcast_select_fusion.9
  91.2 2.4 fusion.4
  103.7 1.6 fusion.3
  105.3 2.3 copy.77
  107.6 1.7 fusion.374
  109.7 2.2 convolution_convert_fusion.2
  115.0 6.3 multiply_convert_fusion.5
  121.3 1.7 fusion.378
  125.2 6.1 convert_reduce_fusion.5
  131.3 2.4 multiply_reduce_fusion.5
  138.6 2.1 convolution_bitcast_fusion.2
  147.7 4.0 fusion.210
  151.7 1.9 fusion.381
  153.6 5.1 fusion.383
  158.7 5.1 fusion.385
  163.8 6.3 multiply_convert_fusion.3
  171.5 1.9 fusion.379
  173.7 6.2 multiply_convert_fusion.1
  179.9 1.6 fusion.380
  182.3 1.6 convert_reduce_fusion.7
  185.9 6.0 convert_reduce_fusion.4
  191.9 2.4 multiply_reduce_fusion.4
  198.6 2.1 convolution_bitcast_fusion.1
  207.7 4.0 fusion.207
  211.7 5.0 fusion.384
  216.8 5.1 fusion.386
  224.2 1.9 fusion.382
  226.1 5.3 collective-permute-done.15
  233.4 6.1 convert_reduce_fusion.3
  239.6 2.4 multiply_reduce_fusion.3
  246.9 2.0 convolution_bitcast_fusion
  253.6 11.3 %add_convert_fusion.1 = bf16[768,3072]{1,0:T(8,128)(2,1)} fusion(f32[768,3072]{1,0:T(8,128)} %fusion.383, f32[768,3072]{1,0:T(8,128)} %fusion.384, bf16[160,768]{1,0:T(8,128)(2,1)S(1)} %copy-done.104, bf16[160,3072]{1,0:T(8,128)(2,1)} %copy-done.99), kind=kOutput, calls=%fused_computation.1 | convolution fusion | flops 762052608 | bytes 24821760 | tf_op jit(solution)/shard_map/dot_general | solution.py:36
  266.8 3.6 add_convert_fusion
  271.4 8.1 add_convert_fusion.2
  279.5 1.7 convert_reduce_fusion.8
  281.3 3.1 fusion.2
  284.4 1.7 copy.75
  291.4 10.5 %fusion.371 = (f32[160]{0:T(256)}, f32[160,768]{1,0:T(8,128)}) fusion(f32[768]{0:T(1024)} %copy-done.191, bf16[1536,768]{1,0:T(8,128)(2,1)} %get-tuple-element.94, bf16[1536,768]{1,0:T(8,128)(2,1)S(1)} %copy-done.28, f32[3072]{0:T(1024)} %copy-done.159, f32[160,768]{1,0:T(8,128)} %copy-done.128, f32[160]{0:T(256)} %add_rsqrt_fusion.1, f32[160]{0:T(256)} %copy-done.184, ...), kind=kOutput, calls=%fused_computation.701 | convolution fusion | flops 1562984320 | bytes 10443648 | tf_op jit(solution)/shard_map/dot_general | solution.py:119
  305.6 1.8 maximum_bitcast_fusion
  308.1 187.0 %all-reduce = (bf16[1536]{0:T(1024)(128)(2,1)S(1)}, bf16[768]{0:T(1024)(128)(2,1)S(1)}, bf16[768]{0:T(1024)(128)(2,1)S(1)}, bf16[768]{0:T(1024)(128)(2,1)S(1)}, ...) all-reduce(bf16[1536]{0:T(1024)(128)(2,1)S(1)} %fusion.245, ...), channel_id=1, replica_groups=mesh['section'=4,'dp'=32] {'dp'}, use_global_device_ids=true, to_apply=%region_57.58 | all-reduce | flops 9216 | bytes 36864 | tf_op jit(solution)/shard_map/psum | solution.py:371
  496.9 3.4 fusion.64
  501.4 212.0 %psum.91 = f32[768]{0:T(1024)} all-reduce(f32[768]{0:T(1024)S(1)} %fusion.75), channel_id=1, replica_groups=mesh['section'=4,'dp'=32] {'section','dp'}, use_global_device_ids=true, to_apply=%region_52.53 | all-reduce | flops 768 | bytes 6144 | tf_op jit(solution)/shard_map/psum | solution.py:368
  716.7 195.7 %all-reduce.4.cloned.1.call-done = (bf16[768,2304]{1,0:T(8,128)(2,1)}, bf16[768,768]{1,0:T(8,128)(2,1)}, bf16[768,3072]{1,0:T(8,128)(2,1)}, bf16[3072,768]{1,0:T(8,128)(2,1)}) async-done(((bf16[768,2304]{1,0:T(8,128)(2,1)}, bf16[768,768]{1,0:T(8,128)(2,1)}, bf16[768,3072]{1,0:T(8,128)(2,1)}, bf16[3072,768]{1,0:T(8,128)(2,1)}), (bf16[768,2304]{1,0:T(8,128)(2,1)}, bf16[768,768]{1,0:T(8,128)(2,1)}, ...) | async-done | bytes 14155792 | tf_op jit(solution)/shard_map/psum | solution.py:370
  912.4 2.7 convert_element_type.762
  917.7 1.7 dynamic-slice_convert_fusion.1
  921.6 3.1 convert_element_type.803
  926.9 2.2 convert_add_fusion.3
  929.1 3.7 convert_add_fusion.2
  932.8 4.5 convert_add_fusion.1
  937.3 2.7 convert_add_fusion
  (672 shorter events, 103.8 us)
Async XLA Ops:
  7.2 13.9 %copy-start.49 = (bf16[384,2304]{1,0:T(8,128)(2,1)S(1)}, bf16[384,2304]{1,0:T(8,128)(2,1)}, u32[]{:S(2)}) copy-start(bf16[384,2304]{1,0:T(8,128)(2,1)} %param.22) | copy-start | bytes 5308420
  7.2 905.2 %all-reduce.4.cloned.1.call-start = ((), (), s32[]{:S(2)}) async-start(), calls=%async_computation | async-start | bytes 28311552 | tf_op jit(solution)/shard_map/psum | solution.py:370
  7.3 4.4 collective-permute-start.11
  7.3 4.8 collective-permute-start.10
  7.8 5.1 collective-permute-start.9
  7.9 5.5 collective-permute-start.5
  8.4 19.0 %collective-permute-start.8 = (bf16[1536,768]{1,0:T(8,128)(2,1)}, bf16[1536,768]{1,0:T(8,128)(2,1)}, u32[]{:S(2)}, u32[]{:S(2)}) collective-permute-start(bf16[1536,768]{1,0:T(8,128)(2,1)} %param.30), channel_id=1, source_target_pairs={{0,32},{32,0},{64,96},{96,64},{1,33},{33,1},{65,97},{97,65},{2,34}... | collective-permute-start | bytes 7077896 | tf_op jit(solution)/shard_map/ppermute | solution.py:16
  11.7 12.7 %copy-start.198 = (pred[160]{0:T(512)(128)(4,1)}, pred[160]{0:T(512)(128)(4,1)S(1)}, u32[]{:S(2)}) copy-start(pred[160]{0:T(512)(128)(4,1)S(1)} %get-tuple-element.32) | copy-start | bytes 484
  11.7 6.7 collective-permute-start.7
  12.1 2.2 collective-permute-start.4
  12.9 1.9 collective-permute-start.3
  13.4 7.7 collective-permute-start
  14.2 63.8 %copy-start.142 = (f32[768]{0:T(1024)}, f32[768]{0:T(1024)S(1)}, u32[]{:S(2)}) copy-start(f32[768]{0:T(1024)S(1)} %maximum_convert_fusion.9) | copy-start | bytes 9220
  14.3 107.0 %copy-start.191 = (f32[768]{0:T(1024)}, f32[768]{0:T(1024)S(1)}, u32[]{:S(2)}) copy-start(f32[768]{0:T(1024)S(1)} %maximum_convert_fusion.7) | copy-start | bytes 9220
  14.3 3.0 collective-permute-start.1
  14.8 4.3 collective-permute-start.2
  15.6 85.6 %copy-start.193 = (f32[768]{0:T(1024)}, f32[768]{0:T(1024)S(1)}, u32[]{:S(2)}) copy-start(f32[768]{0:T(1024)S(1)} %maximum_convert_fusion.4) | copy-start | bytes 9220
  15.6 97.1 %copy-start.156 = (f32[768]{0:T(1024)}, f32[768]{0:T(1024)S(1)}, u32[]{:S(2)}) copy-start(f32[768]{0:T(1024)S(1)} %maximum_convert_fusion.6) | copy-start | bytes 9220
  17.3 14.2 %collective-permute-start.6 = (bf16[384,3072]{1,0:T(8,128)(2,1)}, bf16[384,3072]{1,0:T(8,128)(2,1)}, u32[]{:S(2)}, u32[]{:S(2)}) collective-permute-start(bf16[384,3072]{1,0:T(8,128)(2,1)} %param.28), channel_id=1, source_target_pairs={{0,32},{32,0},{64,96},{96,64},{1,33},{33,1},{65,97},{97,65},{2,34}... | collective-permute-start | bytes 7077896 | tf_op jit(solution)/shard_map/ppermute | solution.py:16
  18.3 84.9 %copy-start.161 = (f32[2304]{0:T(1024)}, f32[2304]{0:T(1024)S(1)}, u32[]{:S(2)}) copy-start(f32[2304]{0:T(1024)S(1)} %pad_maximum_fusion.4) | copy-start | bytes 27652
  19.1 95.2 %copy-start.159 = (f32[3072]{0:T(1024)}, f32[3072]{0:T(1024)S(1)}, u32[]{:S(2)}) copy-start(f32[3072]{0:T(1024)S(1)} %maximum_convert_fusion.3) | copy-start | bytes 36868
  31.5 35.3 %copy-start.24 = (bf16[1536,768]{1,0:T(8,128)(2,1)}, bf16[1536,768]{1,0:T(8,128)(2,1)S(1)}, u32[]{:S(2)}) copy-start(bf16[1536,768]{1,0:T(8,128)(2,1)S(1)} %get-tuple-element.93) | copy-start | bytes 7077892
  45.7 10.6 %copy-start.51 = (bf16[384,2304]{1,0:T(8,128)(2,1)S(1)}, bf16[384,2304]{1,0:T(8,128)(2,1)}, u32[]{:S(2)}) copy-start(bf16[384,2304]{1,0:T(8,128)(2,1)} %copy-done.50) | copy-start | bytes 5308420
  46.1 9.4 collective-permute-start.12
  76.7 14.5 %copy-start.52 = (bf16[384,2304]{1,0:T(8,128)(2,1)S(1)}, bf16[384,2304]{1,0:T(8,128)(2,1)}, u32[]{:S(2)}) copy-start(bf16[384,2304]{1,0:T(8,128)(2,1)} %copy-done.50) | copy-start | bytes 5308420
  80.1 9.3 collective-permute-start.13
  98.3 14.4 %copy-start.168 = (f32[160]{0:T(256)}, f32[160]{0:T(256)S(1)}, u32[]{:S(2)}) copy-start(f32[160]{0:T(256)S(1)} %fusion.249) | copy-start | bytes 1924
  103.3 9.5 copy-start.166
  147.6 22.5 %copy-start.17 = (f32[160,768]{1,0:T(8,128)}, f32[160,768]{1,0:T(8,128)S(1)}, u32[]{:S(2)}) copy-start(f32[160,768]{1,0:T(8,128)S(1)} %convolution_add_fusion.16) | copy-start | bytes 1474564
  163.8 7.7 copy-start.26
  170.2 12.1 %collective-permute-start.14 = (bf16[1,160,768]{2,1,0:T(8,128)(2,1)S(1)}, bf16[1,160,768]{2,1,0:T(8,128)(2,1)S(1)}, u32[]{:S(2)}, u32[]{:S(2)}) collective-permute-start(bf16[1,160,768]{2,1,0:T(8,128)(2,1)S(1)} %convert_bitcast_fusion.4), channel_id=1, source_target_pairs={{64,0},{96,32},{65,1},{97,33},{66,2},{98,34},{67,3},{99,35},{68,4}... | collective-permute-start | bytes 737288 | tf_op jit(solution)/shard_map/ppermute | solution.py:22
  181.8 10.1 %copy-start.175 = (f32[160]{0:T(256)}, f32[160]{0:T(256)S(1)}, u32[]{:S(2)}) copy-start(f32[160]{0:T(256)S(1)} %multiply_reduce_fusion.7) | copy-start | bytes 1924
  207.7 14.3 %copy-start.41 = (f32[160,768]{1,0:T(8,128)}, f32[160,768]{1,0:T(8,128)S(1)}, u32[]{:S(2)}) copy-start(f32[160,768]{1,0:T(8,128)S(1)} %convolution_add_fusion.14) | copy-start | bytes 1474564
  216.8 16.6 %copy-start.200 = (f32[160,3072]{1,0:T(8,128)S(1)}, f32[160,3072]{1,0:T(8,128)}, u32[]{:S(2)}) copy-start(f32[160,3072]{1,0:T(8,128)} %get-tuple-element.73) | copy-start | bytes 5898244
  216.8 16.6 %copy-start.201 = (f32[160,3072]{1,0:T(8,128)S(1)}, f32[160,3072]{1,0:T(8,128)}, u32[]{:S(2)}) copy-start(f32[160,3072]{1,0:T(8,128)} %get-tuple-element.170) | copy-start | bytes 5898244
  221.9 9.5 %copy-start.21 = (f32[160,768]{1,0:T(8,128)S(1)}, f32[160,768]{1,0:T(8,128)}, u32[]{:S(2)}) copy-start(f32[160,768]{1,0:T(8,128)} %copy-done.20) | copy-start | bytes 1474564
  221.9 9.5 %copy-start.145 = (f32[160]{0:T(256)S(1)}, f32[160]{0:T(256)}, u32[]{:S(2)}) copy-start(f32[160]{0:T(256)} %copy-done.144) | copy-start | bytes 1924
  221.9 9.5 %copy-start.170 = (f32[160]{0:T(256)S(1)}, f32[160]{0:T(256)}, u32[]{:S(2)}) copy-start(f32[160]{0:T(256)} %fusion.252) | copy-start | bytes 1924
  222.8 9.5 %copy-start.176 = (f32[160]{0:T(256)S(1)}, f32[160]{0:T(256)}, u32[]{:S(2)}) copy-start(f32[160]{0:T(256)} %copy-done.175) | copy-start | bytes 1924
  222.8 8.6 collective-permute-start.15
  224.2 9.1 copy-start.31
  252.1 12.8 %slice-start = ((s8[9437184]{0:T(1024)(128)(4,1)}), s8[4194304]{0:T(1024)(128)(4,1)S(1)}, s32[]{:S(2)}) async-start(s8[9437184]{0:T(1024)(128)(4,1)} %bitcast.359), calls=%async_computation.1 | async-start | bytes 8388608
  252.1 12.8 %slice-start.3 = ((s8[9437184]{0:T(1024)(128)(4,1)}), s8[4194304]{0:T(1024)(128)(4,1)S(1)}, s32[]{:S(2)}) async-start(s8[9437184]{0:T(1024)(128)(4,1)} %bitcast.361), calls=%async_computation.4 | async-start | bytes 8388608
  253.6 11.3 %slice-start.1 = ((s8[9437184]{0:T(1024)(128)(4,1)}), s8[4194304]{0:T(1024)(128)(4,1)S(1)}, s32[]{:S(2)}) async-start(s8[9437184]{0:T(1024)(128)(4,1)} %bitcast.359), calls=%async_computation.2 | async-start | bytes 8388608
  253.6 11.3 %slice-start.2 = ((s8[9437184]{0:T(1024)(128)(4,1)}), s8[1048576]{0:T(1024)(128)(4,1)S(1)}, s32[]{:S(2)}) async-start(s8[9437184]{0:T(1024)(128)(4,1)} %bitcast.359), calls=%async_computation.3 | async-start | bytes 2097152
  253.6 12.7 %slice-start.4 = ((s8[9437184]{0:T(1024)(128)(4,1)}), s8[4194304]{0:T(1024)(128)(4,1)S(1)}, s32[]{:S(2)}) async-start(s8[9437184]{0:T(1024)(128)(4,1)} %bitcast.361), calls=%async_computation.5 | async-start | bytes 8388608
  253.6 12.9 %slice-start.5 = ((s8[9437184]{0:T(1024)(128)(4,1)}), s8[1048576]{0:T(1024)(128)(4,1)S(1)}, s32[]{:S(2)}) async-start(s8[9437184]{0:T(1024)(128)(4,1)} %bitcast.361), calls=%async_computation.6 | async-start | bytes 2097152
  253.6 13.1 %copy-start.98 = (bf16[160,3072]{1,0:T(8,128)(2,1)S(1)}, bf16[160,3072]{1,0:T(8,128)(2,1)}, u32[]{:S(2)}) copy-start(bf16[160,3072]{1,0:T(8,128)(2,1)} %copy-done.97) | copy-start | bytes 2949124
  253.6 13.1 %copy-start.110 = (bf16[160,768]{1,0:T(8,128)(2,1)S(1)}, bf16[160,768]{1,0:T(8,128)(2,1)}, u32[]{:S(2)}) copy-start(bf16[160,768]{1,0:T(8,128)(2,1)} %copy-done.109) | copy-start | bytes 737284
  291.4 12.8 %copy-start.143 = (f32[768]{0:T(1024)S(1)}, f32[768]{0:T(1024)}, u32[]{:S(2)}) copy-start(f32[768]{0:T(1024)} %copy-done.142) | copy-start | bytes 9220
  304.2 192.7 %copy-start.44 = (f32[160,768]{1,0:T(8,128)S(1)}, f32[160,768]{1,0:T(8,128)}, u32[]{:S(2)}) copy-start(f32[160,768]{1,0:T(8,128)} %copy-done.43) | copy-start | bytes 1474564
  304.2 192.7 %copy-start.179 = (f32[160]{0:T(256)S(1)}, f32[160]{0:T(256)}, u32[]{:S(2)}) copy-start(f32[160]{0:T(256)} %copy-done.178) | copy-start | bytes 1924
  495.6 429.3 %collective-permute-start.17 = (bf16[768]{0:T(1024)(128)(2,1)S(1)}, bf16[768]{0:T(1024)(128)(2,1)S(1)}, u32[]{:S(2)}, u32[]{:S(2)}) collective-permute-start(bf16[768]{0:T(1024)(128)(2,1)S(1)} %dynamic_slice.147), channel_id=1, source_target_pairs={{0,32},{32,0},{64,96},{96,64},{1,33},{33,1},{65,97},{97,65},{2,34}... | collective-permute-start | bytes 4616 | tf_op jit(solution)/shard_map/ppermute | solution.py:16
  495.7 217.8 %collective-permute-start.19 = (bf16[384]{0:T(512)(128)(2,1)S(1)}, bf16[384]{0:T(512)(128)(2,1)S(1)}, u32[]{:S(2)}, u32[]{:S(2)}) collective-permute-start(bf16[384]{0:T(512)(128)(2,1)S(1)} %dynamic_slice.153), channel_id=1, source_target_pairs={{0,32},{32,0},{64,96},{96,64},{1,33},{33,1},{65,97},{97,65},{2,34}... | collective-permute-start | bytes 2312 | tf_op jit(solution)/shard_map/ppermute | solution.py:16
  496.2 218.0 %collective-permute-start.20 = (bf16[384]{0:T(512)(128)(2,1)S(1)}, bf16[384]{0:T(512)(128)(2,1)S(1)}, u32[]{:S(2)}, u32[]{:S(2)}) collective-permute-start(bf16[384]{0:T(512)(128)(2,1)S(1)} %dynamic_slice.152), channel_id=1, source_target_pairs={{0,32},{32,0},{64,96},{96,64},{1,33},{33,1},{65,97},{97,65},{2,34}... | collective-permute-start | bytes 2312 | tf_op jit(solution)/shard_map/ppermute | solution.py:16
  496.3 219.1 %collective-permute-start.21 = (bf16[384]{0:T(512)(128)(2,1)S(1)}, bf16[384]{0:T(512)(128)(2,1)S(1)}, u32[]{:S(2)}, u32[]{:S(2)}) collective-permute-start(bf16[384]{0:T(512)(128)(2,1)S(1)} %dynamic_slice.151), channel_id=1, source_target_pairs={{0,32},{32,0},{64,96},{96,64},{1,33},{33,1},{65,97},{97,65},{2,34}... | collective-permute-start | bytes 2312 | tf_op jit(solution)/shard_map/ppermute | solution.py:16
  496.8 429.5 %collective-permute-start.23 = (bf16[1536]{0:T(1024)(128)(2,1)S(1)}, bf16[1536]{0:T(1024)(128)(2,1)S(1)}, u32[]{:S(2)}, u32[]{:S(2)}) collective-permute-start(bf16[1536]{0:T(1024)(128)(2,1)S(1)} %dynamic_slice.146), channel_id=1, source_target_pairs={{0,32},{32,0},{64,96},{96,64},{1,33},{33,1},{65,97},{97,65},{2,34}... | collective-permute-start | bytes 9224 | tf_op jit(solution)/shard_map/ppermute | solution.py:16
  713.5 2.6 collective-permute-start.25
  714.2 205.3 %collective-permute-start.26 = (bf16[384]{0:T(512)(128)(2,1)S(1)}, bf16[384]{0:T(512)(128)(2,1)S(1)}, u32[]{:S(2)}, u32[]{:S(2)}) collective-permute-start(bf16[384]{0:T(512)(128)(2,1)S(1)} %dynamic_slice.149), channel_id=1, source_target_pairs={{0,32},{32,0},{64,96},{96,64},{1,33},{33,1},{65,97},{97,65},{2,34}... | collective-permute-start | bytes 2312 | tf_op jit(solution)/shard_map/ppermute | solution.py:16
  715.4 205.3 %collective-permute-start.27 = (bf16[384]{0:T(512)(128)(2,1)S(1)}, bf16[384]{0:T(512)(128)(2,1)S(1)}, u32[]{:S(2)}, u32[]{:S(2)}) collective-permute-start(bf16[384]{0:T(512)(128)(2,1)S(1)} %dynamic_slice.148), channel_id=1, source_target_pairs={{0,32},{32,0},{64,96},{96,64},{1,33},{33,1},{65,97},{97,65},{2,34}... | collective-permute-start | bytes 2312 | tf_op jit(solution)/shard_map/ppermute | solution.py:16
  916.4 12.7 %collective-permute-start.16 = (bf16[384,2304]{1,0:T(8,128)(2,1)}, bf16[384,2304]{1,0:T(8,128)(2,1)}, u32[]{:S(2)}, u32[]{:S(2)}) collective-permute-start(bf16[384,2304]{1,0:T(8,128)(2,1)} %dynamic-slice_convert_fusion.2), channel_id=1, source_target_pairs={{0,32},{32,0},{64,96},{96,64},{1,33},{33,1},{65,97},{97,65},{2,34}... | collective-permute-start | bytes 5308424 | tf_op jit(solution)/shard_map/ppermute | solution.py:16
  919.5 13.3 %collective-permute-start.22 = (bf16[384,3072]{1,0:T(8,128)(2,1)}, bf16[384,3072]{1,0:T(8,128)(2,1)}, u32[]{:S(2)}, u32[]{:S(2)}) collective-permute-start(bf16[384,3072]{1,0:T(8,128)(2,1)} %dynamic-slice_convert_fusion.1), channel_id=1, source_target_pairs={{0,32},{32,0},{64,96},{96,64},{1,33},{33,1},{65,97},{97,65},{2,34}... | collective-permute-start | bytes 7077896 | tf_op jit(solution)/shard_map/ppermute | solution.py:16
  921.6 5.4 collective-permute-start.18
  925.0 12.3 %collective-permute-start.24 = (bf16[1536,768]{1,0:T(8,128)(2,1)S(1)}, bf16[1536,768]{1,0:T(8,128)(2,1)S(1)}, u32[]{:S(2)}, u32[]{:S(2)}) collective-permute-start(bf16[1536,768]{1,0:T(8,128)(2,1)S(1)} %dynamic-slice_convert_fusion), channel_id=1, source_target_pairs={{0,32},{32,0},{64,96},{96,64},{1,33},{33,1},{65,97},{97,65},{2,34}... | collective-permute-start | bytes 7077896 | tf_op jit(solution)/shard_map/ppermute | solution.py:16
  (175 other events, 550.9 us)
Sparse Core Ops, SparseCore 0:
  279.6 632.6 all-reduce.3
where the time goes:
time: 961 us; the launch traced here: 947 us
  blocking collectives  399 us (42%)
  waiting for transfers between devices  213 us (22%)
  matrix products  184 us (19%)
  other arithmetic  77 us (8%)
  local copies, waits for them, and re-layouts  40 us (4%)
  starting transfers between devices  17.7 us (2%)
  between operations  17.3 us (2%)
    psum x1, blocking collectives, per_device(): mask_grad = lax.psum(mask_term, ('section', 'dp'))  212 us
    psum x1, waiting for transfers between devices, per_device(): lax.psum(grad_totals[0].astype(jnp.bfloat16), 'dp').astype(jnp.float32)  196 us
    psum x1, blocking collectives, per_device(): lax.psum(grad_totals[1].astype(jnp.bfloat16), 'dp').astype(jnp.float32)  187 us
    dot_general x12, matrix products, contract_rows(): lax.dot_general(left_side, right_side, (((0,), (0,)), ((), ())), preferre...  56.5 us
    dot_general x12, matrix products, contract_cols(): lax.dot_general(left_side, right_side, (((1,), (1,)), ((), ())), preferre...  35.4 us
    dot_general x6, matrix products, forward_parts(): jnp.dot(active_low, w_down, preferred_element_type=jnp.float32)  34.7 us
    unnamed x420, local copies, waits for them, and re-layouts  22.1 us
  transfers between devices with their start and end apart: 29, of which 5 were waited for; matrix products, arithmetic and copies ran while one was open for 9% of the time, Pallas kernels for 0%

commit v1 on v0

--- a/solution.py
+++ b/solution.py
@@ -6,7 +6,6 @@
 from jax.sharding import PartitionSpec as P
 
 HEADS = 12
-MICRO = 2
 
 
 EPSILON = 1e-05
@@ -14,12 +13,6 @@
 
 def partner(x, axis, bit):
     return lax.ppermute(x, axis, [(i, i ^ 1 << bit) for i in range(lax.axis_size(axis))])
-
-
-def shifted(value, axis, steps):
-    count = lax.axis_size(axis)
-    leading, last = (max(0, -steps), min(count, count - steps))
-    return lax.ppermute(value, axis, [(source, source + steps) for source in range(leading, last)])
 
 
 def norm_rows(values, norm_gain, norm_shift):
@@ -53,10 +46,6 @@
 def take_half(tensor, which_half):
     half_rows = tensor.shape[0] // 2
     return lax.dynamic_slice_in_dim(tensor, which_half * half_rows, half_rows, 0)
-
-
-def clamp_pick(sequence, micro_no):
-    return sequence[min(max(micro_no, 0), len(sequence) - 1)]
 
 
 def forward_parts(layer_in, params, key_valid):
@@ -138,7 +127,7 @@
     return (output.reshape(chains, length, model_width), kept_parts)
 
 
-def layer_backward(layer_in, params, key_valid, upstream):
+def layer_backward(layer_in, params, kept_parts, upstream):
     (
         w_qkv,
         qv_bias,
@@ -156,7 +145,6 @@
     chains, length, model_width = layer_in.shape
     head_dim = model_width // HEADS
     scale = 1.0 / math.sqrt(head_dim)
-    output, kept_parts = forward_parts(layer_in, params, key_valid)
     (
         rows_in,
         queries,
@@ -233,6 +221,104 @@
         d_norm2_bias,
     )
     return (d_input.reshape(chains, length, model_width), layer_grads)
+
+
+BITS = ("zw", "zu", "xw", "xu", "y")
+ORDERS = (
+    (("zw", "zu", "xw", "xu"), ("zu", "zw", "xu", "xw")),
+    (("xw", "xu", "zw", "zu"), ("xu", "xw", "zu", "zw")),
+)
+
+
+def flip_dp(index, bit):
+    z, x, y = index // 8, index // 2 % 4, index % 2
+    if bit == "zw":
+        z ^= 1
+    elif bit == "zu":
+        z ^= 3
+    elif bit == "xw":
+        x ^= 1
+    elif bit == "xu":
+        x ^= 3
+    else:
+        y ^= 1
+    return z * 8 + x * 2 + y
+
+
+def flip_pairs(bit_of_core):
+    pairs = []
+    for section in range(4):
+        for index in range(32):
+            pairs.append(
+                (section * 32 + index, section * 32 + flip_dp(index, bit_of_core[section % 2]))
+            )
+    return pairs
+
+
+def exchange(value, bit_of_core):
+    return lax.ppermute(value, ("section", "dp"), flip_pairs(bit_of_core))
+
+
+def own_bits():
+    index = lax.axis_index("dp")
+    z, x, y = index // 8, index // 2 % 4, index % 2
+    return {
+        "zu": z // 2,
+        "zw": (z // 2) ^ (z % 2),
+        "xu": x // 2,
+        "xw": (x // 2) ^ (x % 2),
+        "y": y,
+    }
+
+
+def own_bit(bits, core, part, step):
+    return jnp.where(core == 0, bits[ORDERS[0][part][step]], bits[ORDERS[1][part][step]])
+
+
+def add_low(left_side, right_side):
+    return (left_side.astype(jnp.float32) + right_side.astype(jnp.float32)).astype(jnp.bfloat16)
+
+
+def reduce_rows(pack, extra, bits, core):
+    half = pack.shape[0] // 2
+    parts = [pack[:half], pack[half:]]
+    for step in range(4):
+        for part in range(2):
+            bit = own_bit(bits, core, part, step)
+            rows = parts[part].shape[0] // 2
+            keep = lax.dynamic_slice_in_dim(parts[part], bit * rows, rows, 0)
+            send = lax.dynamic_slice_in_dim(parts[part], (1 - bit) * rows, rows, 0)
+            flips = (ORDERS[0][part][step], ORDERS[1][part][step])
+            if part == 0 and extra is not None:
+                got = exchange(jnp.concatenate([send, extra], axis=0), flips)
+                extra = add_low(extra, got[rows:])
+                got = got[:rows]
+            else:
+                got = exchange(send, flips)
+            parts[part] = add_low(keep, got)
+    rows = parts[0].shape[0]
+    both = jnp.concatenate(parts + ([extra] if extra is not None else []), axis=0)
+    both = add_low(both, exchange(both, ("y", "y")))
+    parts = [both[:rows], both[rows : 2 * rows]]
+    if extra is not None:
+        extra = both[2 * rows :]
+    for step in reversed(range(4)):
+        for part in range(2):
+            bit = own_bit(bits, core, part, step)
+            flips = (ORDERS[0][part][step], ORDERS[1][part][step])
+            got = exchange(parts[part], flips)
+            parts[part] = assemble(parts[part], got, bit)
+    return jnp.concatenate(parts, axis=0), extra
+
+
+def fold(tensor):
+    return jnp.concatenate(
+        [tensor[:, at : at + 768] for at in range(0, tensor.shape[1], 768)], axis=0
+    )
+
+
+def unfold(rows, count):
+    return jnp.concatenate(jnp.split(rows, count, axis=0), axis=1)
 
 
 def per_device(
@@ -257,7 +343,26 @@
     section_index = lax.axis_index("section")
     is_first = section_index < 2
     pair_half = section_index % 2
-    own_params = (
+    big = (w_qkv, w_out, w_up, w_down)
+    small = jnp.concatenate(
+        [qv_bias, b_out, norm1_gain, norm1_bias, b_up, b_down, norm2_gain, norm2_bias]
+    )
+    partner_big = partner(big, "section", 0)
+    partner_small = partner(small, "section", 0)
+    w_qkv, w_out, w_up, w_down = (
+        assemble(own_part, partner_part, pair_half)
+        for own_part, partner_part in zip(big, partner_big)
+    )
+    low_small = jnp.where(pair_half == 0, small, partner_small)
+    high_small = jnp.where(pair_half == 0, partner_small, small)
+    sizes = (768, 384, 384, 384, 1536, 384, 384, 384)
+    smalls = []
+    at = 0
+    for size in sizes:
+        smalls.append(jnp.concatenate([low_small[at : at + size], high_small[at : at + size]]))
+        at += size
+    qv_bias, b_out, norm1_gain, norm1_bias, b_up, b_down, norm2_gain, norm2_bias = smalls
+    params = (
         w_qkv,
         qv_bias,
         w_out,
@@ -271,30 +376,6 @@
         norm2_gain,
         norm2_bias,
     )
-    partner_params = partner(
-        (
-            w_qkv,
-            qv_bias,
-            w_out,
-            b_out,
-            norm1_gain,
-            norm1_bias,
-            w_up,
-            b_up,
-            w_down,
-            b_down,
-            norm2_gain,
-            norm2_bias,
-        ),
-        "section",
-        0,
-    )
-    params = tuple(
-        (
-            assemble(own_part, partner_part, pair_half)
-            for own_part, partner_part in zip(own_params, partner_params)
-        )
-    )
     my_inputs = lax.dynamic_index_in_dim(inputs, pair_half, 0, keepdims=False)
     my_cotangent = lax.dynamic_index_in_dim(cotangent, pair_half, 0, keepdims=False)
     my_lengths = lax.dynamic_index_in_dim(lengths, pair_half, 0, keepdims=False)
@@ -304,101 +385,102 @@
     key_valid = positions[None, :] < my_lengths[:, None]
     masked = (positions[None, :] >= my_spans[:, 0:1]) & (positions[None, :] < my_spans[:, 1:2])
     entered = jnp.where(masked[:, :, None], mask_vector[None, None, :], my_inputs)
-    per_micro = chain_rows // MICRO
-
-    def micro_of(tensor, micro_no):
-        clamped = min(max(micro_no, 0), MICRO - 1)
-        return tensor[clamped * per_micro : (clamped + 1) * per_micro]
-
-    blank_block = jnp.zeros((per_micro, seq_len, model_width), jnp.bfloat16)
-    received = blank_block
-    tick_inputs = []
-    tick_outputs = []
-    for tick_no in range(MICRO + 1):
-        fresh = micro_of(entered, tick_no) if tick_no < MICRO else blank_block
-        layer_in = jnp.where(is_first, fresh, received)
-        valid_now = jnp.where(
-            is_first, micro_of(key_valid, tick_no), micro_of(key_valid, tick_no - 1)
-        )
-        output, kept_parts = forward_parts(layer_in, params, valid_now)
-        sent = output.astype(jnp.bfloat16)
-        tick_inputs.append(layer_in)
-        tick_outputs.append(sent)
-        if tick_no < MICRO:
-            received = shifted(sent, "section", 2)
-    section_inputs = [
-        jnp.where(is_first, tick_inputs[micro_no], tick_inputs[micro_no + 1])
-        for micro_no in range(MICRO)
-    ]
-    section_outputs = [
-        jnp.where(is_first, tick_outputs[micro_no], tick_outputs[micro_no + 1])
-        for micro_no in range(MICRO)
-    ]
-    layer_outputs = jnp.concatenate(section_outputs, axis=0)[None]
-    grad_totals = tuple((jnp.zeros(tensor.shape, jnp.float32) for tensor in params))
-    returned = blank_block
-    tick_grads = []
-    for tick_no in range(MICRO + 1):
-        from_loss = micro_of(my_cotangent, tick_no) if tick_no < MICRO else blank_block
-        upstream = jnp.where(is_first, returned, from_loss).astype(jnp.float32)
-        saved_in = jnp.where(
-            is_first, clamp_pick(section_inputs, tick_no - 1), clamp_pick(section_inputs, tick_no)
-        )
-        valid_now = jnp.where(
-            is_first, micro_of(key_valid, tick_no - 1), micro_of(key_valid, tick_no)
-        )
-        down_grad, layer_grads = layer_backward(saved_in, params, valid_now, upstream)
-        grad_totals = tuple(
-            (total + fresh_grad for total, fresh_grad in zip(grad_totals, layer_grads))
-        )
-        sent_back = down_grad.astype(jnp.bfloat16)
-        tick_grads.append(down_grad)
-        if tick_no < MICRO:
-            returned = shifted(sent_back, "section", -2)
-    all_grads = jnp.concatenate(
-        [
-            jnp.where(is_first, tick_grads[micro_no + 1], tick_grads[micro_no])
-            for micro_no in range(MICRO)
-        ],
-        axis=0,
-    )
+
+    first_out, _ = forward_parts(entered, params, key_valid)
+    received = lax.ppermute(first_out.astype(jnp.bfloat16), "section", [(0, 2), (1, 3)])
+    layer_in = jnp.where(is_first, entered, received)
+    output, kept_parts = forward_parts(layer_in, params, key_valid)
+    layer_outputs = output.astype(jnp.bfloat16)[None]
+    upper_grad, _ = layer_backward(layer_in, params, kept_parts, my_cotangent.astype(jnp.float32))
+    returned = lax.ppermute(upper_grad.astype(jnp.bfloat16), "section", [(2, 0), (3, 1)])
+    upstream = jnp.where(is_first, returned, my_cotangent).astype(jnp.float32)
+    all_grads, layer_grads = layer_backward(layer_in, params, kept_parts, upstream)
     dropped = masked[:, :, None] & is_first
     input_grads = jnp.where(dropped, 0.0, all_grads).astype(jnp.bfloat16)[None]
     mask_term = jnp.sum(jnp.where(dropped, all_grads, 0.0), axis=(0, 1))
-    mask_grad = lax.psum(mask_term, ("section", "dp"))
-    summed = (
-        lax.psum(grad_totals[0].astype(jnp.bfloat16), "dp").astype(jnp.float32),
-        lax.psum(grad_totals[1].astype(jnp.bfloat16), "dp").astype(jnp.float32),
-        lax.psum(grad_totals[2].astype(jnp.bfloat16), "dp").astype(jnp.float32),
-        lax.psum(grad_totals[3].astype(jnp.bfloat16), "dp").astype(jnp.float32),
-        lax.psum(grad_totals[4].astype(jnp.bfloat16), "dp").astype(jnp.float32),
-        lax.psum(grad_totals[5].astype(jnp.bfloat16), "dp").astype(jnp.float32),
-        lax.psum(grad_totals[6].astype(jnp.bfloat16), "dp").astype(jnp.float32),
-        lax.psum(grad_totals[7].astype(jnp.bfloat16), "dp").astype(jnp.float32),
-        lax.psum(grad_totals[8].astype(jnp.bfloat16), "dp").astype(jnp.float32),
-        lax.psum(grad_totals[9].astype(jnp.bfloat16), "dp").astype(jnp.float32),
-        lax.psum(grad_totals[10].astype(jnp.bfloat16), "dp").astype(jnp.float32),
-        lax.psum(grad_totals[11].astype(jnp.bfloat16), "dp").astype(jnp.float32),
-    )
-    outgoing = tuple((take_half(tensor, 1 - pair_half) for tensor in summed))
-    incoming = (
-        partner(outgoing[0].astype(jnp.bfloat16), "section", 0).astype(jnp.float32),
-        partner(outgoing[1].astype(jnp.bfloat16), "section", 0).astype(jnp.float32),
-        partner(outgoing[2].astype(jnp.bfloat16), "section", 0).astype(jnp.float32),
-        partner(outgoing[3].astype(jnp.bfloat16), "section", 0).astype(jnp.float32),
-        partner(outgoing[4].astype(jnp.bfloat16), "section", 0).astype(jnp.float32),
-        partner(outgoing[5].astype(jnp.bfloat16), "section", 0).astype(jnp.float32),
-        partner(outgoing[6].astype(jnp.bfloat16), "section", 0).astype(jnp.float32),
-        partner(outgoing[7].astype(jnp.bfloat16), "section", 0).astype(jnp.float32),
-        partner(outgoing[8].astype(jnp.bfloat16), "section", 0).astype(jnp.float32),
-        partner(outgoing[9].astype(jnp.bfloat16), "section", 0).astype(jnp.float32),
-        partner(outgoing[10].astype(jnp.bfloat16), "section", 0).astype(jnp.float32),
-        partner(outgoing[11].astype(jnp.bfloat16), "section", 0).astype(jnp.float32),
-    )
-    reduced = tuple(
-        (take_half(tensor, pair_half) + other_part for tensor, other_part in zip(summed, incoming))
-    )
-    return (layer_outputs, input_grads, mask_grad) + tuple(reduced)
+
+    (
+        d_w_qkv,
+        d_qv_bias,
+        d_w_out,
+        d_b_out,
+        d_norm1_gain,
+        d_norm1_bias,
+        d_w_up,
+        d_b_up,
+        d_w_down,
+        d_b_down,
+        d_norm2_gain,
+        d_norm2_bias,
+    ) = layer_grads
+
+    def pair_sum(tensor):
+        low = tensor.astype(jnp.bfloat16)
+        got = partner(take_half(low, 1 - pair_half), "section", 0)
+        return add_low(take_half(low, pair_half), got)
+
+    bits = own_bits()
+    early = jnp.concatenate([pair_sum(d_w_down), fold(pair_sum(d_w_up))], axis=0)
+    grads_small = (
+        d_qv_bias,
+        d_b_out,
+        d_norm1_gain,
+        d_norm1_bias,
+        d_b_up,
+        d_b_down,
+        d_norm2_gain,
+        d_norm2_bias,
+    )
+    own_small = jnp.concatenate([take_half(t, pair_half) for t in grads_small])
+    other_small = jnp.concatenate([take_half(t, 1 - pair_half) for t in grads_small])
+    summed_small = own_small + partner(other_small.astype(jnp.bfloat16), "section", 0).astype(
+        jnp.float32
+    )
+    extra = jnp.concatenate(
+        [
+            summed_small.astype(jnp.bfloat16).reshape(6, 768),
+            mask_term.astype(jnp.bfloat16)[None],
+            jnp.zeros((9, 768), jnp.bfloat16),
+        ],
+        axis=0,
+    )
+    late = jnp.concatenate([pair_sum(d_w_out), fold(pair_sum(d_w_qkv))], axis=0)
+    early, _ = reduce_rows(early, None, bits, pair_half)
+    late, extra = reduce_rows(late, extra, bits, pair_half)
+    mask_row = extra[6:7]
+    mask_row = mask_row.astype(jnp.float32) + partner(mask_row, "section", 0).astype(jnp.float32)
+    mask_low = mask_row.astype(jnp.bfloat16)
+    mask_row = mask_row + partner(mask_low, "section", 1).astype(jnp.float32)
+    mask_grad = mask_row.astype(jnp.bfloat16).astype(jnp.float32)[0]
+
+    flat_small = extra[:6].reshape(-1).astype(jnp.float32)
+    out_small = []
+    at = 0
+    for size in sizes:
+        out_small.append(flat_small[at : at + size])
+        at += size
+    g_qv, g_bo, g_n1g, g_n1b, g_bu, g_bd, g_n2g, g_n2b = out_small
+    g_down = early[:1536].astype(jnp.float32)
+    g_up = unfold(early[1536:], 4).astype(jnp.float32)
+    g_out = late[:384].astype(jnp.float32)
+    g_qkv = unfold(late[384:], 3).astype(jnp.float32)
+    return (
+        layer_outputs,
+        input_grads,
+        mask_grad,
+        g_qkv,
+        g_qv,
+        g_out,
+        g_bo,
+        g_n1g,
+        g_n1b,
+        g_up,
+        g_bu,
+        g_down,
+        g_bd,
+        g_n2g,
+        g_n2b,
+    )
 
 
 def solution(mesh):

time: 961 us -> 460 us (0.48); the launches traced: 947 us -> 457 us
  blocking collectives: 399 us -> 0 us
  waiting for transfers between devices: 213 us -> 113 us
  matrix products: 184 us -> 111 us
  local copies, waits for them, and re-layouts: 40 us -> 102 us
  starting transfers between devices: 17.7 us -> 62.2 us
  between operations: 17.3 us -> 3.13 us
  other arithmetic: 77 us -> 66 us
    psum x2 -> x0, blocking collectives: 399 us -> none  [the longest x1 212 us: per_device(): mask_grad = lax.psum(mask_term, ('section', 'dp'))]
    psum x1 -> x0, waiting for transfers between devices: 196 us -> none  [per_device(): lax.psum(grad_totals[0].astype(jnp.bfloat16), 'dp').astype(jnp.float32)]
    ppermute x4 -> x36, waiting for transfers between devices: 15.2 us -> 110 us  [the longest x34 88 us: exchange(): return lax.ppermute(value, ('section', 'dp'), flip_pairs(bit_of_core))]
    ppermute x4 -> x36, starting transfers between devices: 11.5 us -> 59.2 us  [the longest x34 54 us: exchange(): return lax.ppermute(value, ('section', 'dp'), flip_pairs(bit_of_core))]
    dot_general x12 -> x4, matrix products: 56.5 us -> 13 us  [contract_rows(): lax.dot_general(left_side, right_side, (((0,), (0,)), ((), ())), preferre...]
    add x12 -> x0, other arithmetic: 18.4 us -> none  [per_device(): take_half(tensor, pair_half) + other_part]
    reshape x0 -> x7, local copies, waits for them, and re-layouts: none -> 17.8 us  [the longest x4 8.92 us: layer_backward(): contract_cols(d_branch, w_out).astype(jnp.bfloat16)]
    convert_element_type x23 -> x36, other arithmetic: 8.13 us -> 23.5 us  [the longest x26 13.2 us: add_low(): (left_side.astype(jnp.float32) + right_side.astype(jnp.float32)).astype(j...]
  transfers between devices with their start and end apart: 29 -> 48, of which waited for: 5 -> 23; matrix products, arithmetic and copies ran while one was open for 9% -> 18% of each run, Pallas kernels for 0% -> 0%
where the time goes in v1:
time: 460 us; the launch traced here: 457 us
  waiting for transfers between devices  113 us (25%)
  matrix products  111 us (24%)
  local copies, waits for them, and re-layouts  102 us (22%)
  other arithmetic  66 us (14%)
  starting transfers between devices  62.2 us (14%)
    ppermute x34, waiting for transfers between devices, exchange(): return lax.ppermute(value, ('section', 'dp'), flip_pairs(bit_of_core))  88 us
    ppermute x34, starting transfers between devices, exchange(): return lax.ppermute(value, ('section', 'dp'), flip_pairs(bit_of_core))  54 us
    unnamed x184, local copies, waits for them, and re-layouts  37 us
    dot_general x7, matrix products, contract_cols(): lax.dot_general(left_side, right_side, (((1,), (1,)), ((), ())), preferre...  31.2 us
    dot_general x2, matrix products, forward_parts(): jnp.dot(active_low, w_down, preferred_element_type=jnp.float32)  28 us
    select_n x17, other arithmetic, assemble(): lower = jnp.where(pair_half == 0, own_part, partner_part)  14 us
    convert_element_type x26, other arithmetic, add_low(): (left_side.astype(jnp.float32) + right_side.astype(jnp.float32)).astype(j...  13.2 us
    dot_general x4, matrix products, contract_rows(): lax.dot_general(left_side, right_side, (((0,), (0,)), ((), ())), preferre...  13 us
  transfers between devices with their start and end apart: 48, of which 23 were waited for; matrix products, arithmetic and copies ran while one was open for 18% of the time, Pallas kernels for 0%

profile of v1, /device:TPU:0, one launch (start us, length us, event | category | flops | bytes accessed | tf_op | source)
XLA Modules:
  0.0 457.0 jit_solution(5697574264997616599)
XLA Ops:
  21.3 4.1 reshape.498
  25.3 3.9 fusion.131
  32.9 2.2 fusion.19
  39.4 3.2 fusion.39
  44.7 2.3 fusion.142
  47.9 4.4 broadcast_select_fusion.1
  52.3 3.5 broadcast_select_fusion.3
  55.7 26.2 %fusion.143 = (f32[320]{0:T(512)S(1)}, f32[320,768]{1,0:T(8,128)S(1)}) fusion(f32[768]{0:T(1024)S(1)} %maximum_convert_fusion.8, bf16[1536,768]{1,0:T(8,128)(2,1)} %get-tuple-element.41, bf16[1536,768]{1,0:T(8,128)(2,1)} %get-tuple-element.40, f32[3072]{0:T(1024)S(1)} %maximum_convert_fusion.4, f32[320,768]{1,0:T(8,128)} %copy-done.48, ...), kind=kOutput, calls=%fused_computation.405 | convolution fusion | flops 3107094272 | bytes 11428608 | tf_op jit(solution)/shard_map/dot_general | solution.py:108
  82.5 3.7 collective-permute-start.5
  87.3 9.9 %collective-permute-done.5 = bf16[2,160,768]{2,1,0:T(8,128)(2,1)S(1)} collective-permute-done((bf16[2,160,768]{2,1,0:T(8,128)(2,1)S(1)}, bf16[2,160,768]{2,1,0:T(8,128)(2,1)S(1)}, u32[]{:S(2)}, u32[]{:S(2)}) %collective-permute-start.5) | collective-permute-done | bytes 491552 | tf_op jit(solution)/shard_map/ppermute | solution.py:390
  100.5 4.1 reshape.499
  104.5 4.4 fusion.130
  119.1 3.1 convert_element_type.553
  122.2 2.3 fusion.67
  126.9 11.9 %multiply_convert_fusion.2 = (bf16[320,3072]{1,0:T(8,128)(2,1)S(1)}, f32[320,3072]{1,0:T(8,128)}, f32[320,3072]{1,0:T(8,128)}) fusion(f32[3072]{0:T(1024)S(1)} %maximum_convert_fusion.4, bf16[320,768]{1,0:T(8,128)(2,1)S(1)} %add_convert_fusion.18, bf16[384,3072]{1,0:T(8,128)(2,1)S(1)} %copy-done.27, bf16[384,3072]{1,0:T(8,128)(2,1)S(1)} %copy-done.25), kind=kOutput, calls=%fused_computation.28 | convolution fusion | flops 1584267264 | bytes 15052800 | tf_op jit(solution)/shard_map/dot_general | solution.py:104
  144.2 11.1 %multiply_reduce_fusion.5 = (f32[320]{0:T(512)S(1)}, f32[320,768]{1,0:T(8,128)}) fusion(f32[320,768]{1,0:T(8,128)S(1)} %fusion.66, f32[768]{0:T(1024)S(1)} %maximum_convert_fusion.6, bf16[384,3072]{1,0:T(8,128)(2,1)} %get-tuple-element.39, bf16[384,3072]{1,0:T(8,128)(2,1)} %copy-done.24, f32[320,3072]{1,0:T(8,128)} %get-tuple-element.37, ...), kind=kOutput, calls=%fused_computation.156 | convolution fusion | flops 3054255872 | bytes 20256256 | tf_op jit(solution)/shard_map/dot_general | solution.py:35
  161.5 3.1 copy.63
  166.7 4.0 multiply_reduce_fusion.1
  174.2 3.9 copy.68
  178.2 6.3 %convert_element_type.566 = bf16[320,2304]{0,1:T(8,128)(2,1)} reshape(bf16[2,160,3,12,64]{1,0,4,3,2:T(2,128)(2,1)} %copy.68) | data formatting | bytes 2949120 | tf_op jit(solution)/shard_map/convert_element_type | solution.py:203
  184.4 5.2 %fusion.45 = bf16[320,768]{1,0:T(8,128)(2,1)} fusion(bf16[320,2304]{0,1:T(8,128)(2,1)} %convert_element_type.566, f32[320,768]{1,0:T(8,128)} %copy-done.47, f32[320]{0:T(512)S(1)} %negate_multiply_fusion.4, bf16[384,2304]{1,0:T(8,128)(2,1)} %copy-done.41, bf16[384,2304]{1,0:T(8,128)(2,1)} %copy-done.38), kind=kOutput, calls=%fused_computation.126 | convolution fusion | flops 1140277248 | bytes 6489344 | tf_op jit(solution)/shard_map/dot_general | solution.py:35
  192.1 12.5 %collective-permute-done.6 = bf16[2,160,768]{2,1,0:T(8,128)(2,1)S(1)} collective-permute-done((bf16[2,160,768]{2,1,0:T(8,128)(2,1)}, bf16[2,160,768]{2,1,0:T(8,128)(2,1)S(1)}, u32[]{:S(2)}, u32[]{:S(2)}) %collective-permute-start.6) | collective-permute-done | bytes 491552 | tf_op jit(solution)/shard_map/ppermute | solution.py:395
  212.3 8.2 %convert_reduce_fusion.1 = (f32[3072]{0:T(1024)}, bf16[320,3072]{1,0:T(8,128)(2,1)S(1)}) fusion(f32[320,3072]{1,0:T(8,128)} %get-tuple-element.37, f32[320,3072]{1,0:T(8,128)} %get-tuple-element.141, bf16[320,768]{1,0:T(8,128)(2,1)S(1)} %get-tuple-element.27, bf16[1536,768]{1,0:T(8,128)(2,1)} %get-tuple-element.41, bf16[1536,768]{1,0:T(8,128)(2,1)} %get-tuple-element.40), kind=kOutput, calls=%fused_computation.21 | convolution fusion | flops 1535112192 | bytes 15052800 | tf_op jit(solution)/shard_map/dot_general | solution.py:35
  220.5 2.6 multiply_reduce_fusion.2
  230.6 4.0 multiply_reduce_fusion
  237.9 4.3 convolution_convert_fusion.1
  242.2 4.3 convolution_convert_fusion.2
  247.2 2.5 copy.75
  249.7 2.6 convert_element_type.576
  264.7 3.7 convolution_convert_fusion
  268.9 3.2 constant_dynamic-slice_fusion.4
  281.7 4.0 collective-permute-start.14
  289.2 4.6 %collective-permute-done.14 = bf16[384,768]{1,0:T(8,128)(2,1)S(1)} collective-permute-done((bf16[384,768]{1,0:T(8,128)(2,1)}, bf16[384,768]{1,0:T(8,128)(2,1)S(1)}, u32[]{:S(2)}, u32[]{:S(2)}) %collective-permute-start.14) | collective-permute-done | bytes 589856 | tf_op jit(solution)/shard_map/ppermute | solution.py:259
  294.7 3.3 add_convert_fusion
  299.5 3.4 collective-permute-start.35
  304.0 2.8 collective-permute-start.16
  306.8 15.5 %collective-permute-done.11 = bf16[208,768]{1,0:T(8,128)(2,1)S(1)} collective-permute-done((bf16[208,768]{1,0:T(8,128)(2,1)S(1)}, bf16[208,768]{1,0:T(8,128)(2,1)S(1)}, u32[]{:S(2)}, u32[]{:S(2)}) %collective-permute-start.11) | collective-permute-done | bytes 319520 | tf_op jit(solution)/shard_map/ppermute | solution.py:259
  324.7 3.2 collective-permute-done.12
  328.0 2.8 collective-permute-start.13
  330.9 3.0 collective-permute-done.13
  334.0 3.0 collective-permute-start.18
  337.0 2.3 add_convert_fusion.1
  344.4 2.8 collective-permute-start.21
  347.7 2.2 collective-permute-done.21
  349.9 2.4 collective-permute-done.25
  354.7 3.0 collective-permute-done.30
  359.3 3.3 collective-permute-start.31
  362.6 2.8 collective-permute-start.26
  366.1 2.4 collective-permute-start.37
  368.5 5.1 %collective-permute-done.31 = bf16[384,768]{1,0:T(8,128)(2,1)S(1)} collective-permute-done((bf16[384,768]{1,0:T(8,128)(2,1)S(1)}, bf16[384,768]{1,0:T(8,128)(2,1)S(1)}, u32[]{:S(2)}, u32[]{:S(2)}) %collective-permute-start.31) | collective-permute-done | bytes 589856 | tf_op jit(solution)/shard_map/ppermute | solution.py:259
  376.1 4.5 collective-permute-done.32
  380.7 2.8 collective-permute-start.33
  383.6 3.5 collective-permute-done.33
  388.9 6.6 %collective-permute-done.39 = bf16[192,768]{1,0:T(8,128)(2,1)S(1)} collective-permute-done((bf16[192,768]{1,0:T(8,128)(2,1)S(1)}, bf16[192,768]{1,0:T(8,128)(2,1)S(1)}, u32[]{:S(2)}, u32[]{:S(2)}) %collective-permute-start.39) | collective-permute-done | bytes 294944 | tf_op jit(solution)/shard_map/ppermute | solution.py:259
  395.7 2.8 collective-permute-start.44
  398.6 3.1 collective-permute-start.23
  406.8 2.8 collective-permute-start.28
  409.7 6.8 %collective-permute-done.41 = bf16[192,768]{1,0:T(8,128)(2,1)S(1)} collective-permute-done((bf16[192,768]{1,0:T(8,128)(2,1)S(1)}, bf16[192,768]{1,0:T(8,128)(2,1)S(1)}, u32[]{:S(2)}, u32[]{:S(2)}) %collective-permute-start.41) | collective-permute-done | bytes 294944 | tf_op jit(solution)/shard_map/ppermute | solution.py:259
  420.7 6.1 %collective-permute-done.42 = bf16[384,768]{1,0:T(8,128)(2,1)S(1)} collective-permute-done((bf16[384,768]{1,0:T(8,128)(2,1)S(1)}, bf16[384,768]{1,0:T(8,128)(2,1)S(1)}, u32[]{:S(2)}, u32[]{:S(2)}) %collective-permute-start.42) | collective-permute-done | bytes 589856 | tf_op jit(solution)/shard_map/ppermute | solution.py:259
  428.7 4.4 collective-permute-done.24
  437.1 7.5 %collective-permute-done.43 = bf16[768,768]{1,0:T(8,128)(2,1)S(1)} collective-permute-done((bf16[768,768]{1,0:T(8,128)(2,1)S(1)}, bf16[768,768]{1,0:T(8,128)(2,1)S(1)}, u32[]{:S(2)}, u32[]{:S(2)}) %collective-permute-start.43) | collective-permute-done | bytes 1179680 | tf_op jit(solution)/shard_map/ppermute | solution.py:259
  445.3 5.6 %collective-permute-done.47 = bf16[768,768]{1,0:T(8,128)(2,1)S(1)} collective-permute-done((bf16[768,768]{1,0:T(8,128)(2,1)S(1)}, bf16[768,768]{1,0:T(8,128)(2,1)S(1)}, u32[]{:S(2)}, u32[]{:S(2)}) %collective-permute-start.47) | collective-permute-done | bytes 1179680 | tf_op jit(solution)/shard_map/ppermute | solution.py:259
  451.5 2.5 maximum_convert_fusion.2
  454.0 2.8 maximum_convert_fusion.1
  (455 shorter events, 149.6 us)
Async XLA Ops:
  0.7 15.8 %copy-start.37 = (bf16[384,2304]{1,0:T(8,128)(2,1)S(1)}, bf16[384,2304]{1,0:T(8,128)(2,1)}, u32[]{:S(2)}) copy-start(bf16[384,2304]{1,0:T(8,128)(2,1)} %param.22) | copy-start | bytes 5308420
  7.7 4.7 %collective-permute-start.1 = (bf16[4608]{0:T(1024)(128)(2,1)S(1)}, bf16[4608]{0:T(1024)(128)(2,1)S(1)}, u32[]{:S(2)}, u32[]{:S(2)}) collective-permute-start(bf16[4608]{0:T(1024)(128)(2,1)S(1)} %dynamic-update-slice.25), channel_id=1, source_target_pairs={{0,32},{32,0},{64,96},{96,64},{1,33},{33,1},{65,97},{97,65},{2,34}... | collective-permute-start | bytes 27656 | tf_op jit(solution)/shard_map/ppermute | solution.py:15
  7.7 40.2 %collective-permute-start.4 = (bf16[1536,768]{1,0:T(8,128)(2,1)}, bf16[1536,768]{1,0:T(8,128)(2,1)}, u32[]{:S(2)}, u32[]{:S(2)}) collective-permute-start(bf16[1536,768]{1,0:T(8,128)(2,1)} %param.30), channel_id=1, source_target_pairs={{0,32},{32,0},{64,96},{96,64},{1,33},{33,1},{65,97},{97,65},{2,34}... | collective-permute-start | bytes 7077896 | tf_op jit(solution)/shard_map/ppermute | solution.py:15
  8.2 8.2 %collective-permute-start = (bf16[384,2304]{1,0:T(8,128)(2,1)}, bf16[384,2304]{1,0:T(8,128)(2,1)}, u32[]{:S(2)}, u32[]{:S(2)}) collective-permute-start(bf16[384,2304]{1,0:T(8,128)(2,1)} %param.22), channel_id=1, source_target_pairs={{0,32},{32,0},{64,96},{96,64},{1,33},{33,1},{65,97},{97,65},{2,34}... | collective-permute-start | bytes 5308424 | tf_op jit(solution)/shard_map/ppermute | solution.py:15
  8.3 6.0 %collective-permute-start.2 = (bf16[384,768]{1,0:T(8,128)(2,1)}, bf16[384,768]{1,0:T(8,128)(2,1)S(1)}, u32[]{:S(2)}, u32[]{:S(2)}) collective-permute-start(bf16[384,768]{1,0:T(8,128)(2,1)} %param.24), channel_id=1, source_target_pairs={{0,32},{32,0},{64,96},{96,64},{1,33},{33,1},{65,97},{97,65},{2,34}... | collective-permute-start | bytes 1769480 | tf_op jit(solution)/shard_map/ppermute | solution.py:15
  8.7 43.5 %collective-permute-start.3 = (bf16[384,3072]{1,0:T(8,128)(2,1)}, bf16[384,3072]{1,0:T(8,128)(2,1)}, u32[]{:S(2)}, u32[]{:S(2)}) collective-permute-start(bf16[384,3072]{1,0:T(8,128)(2,1)} %param.28), channel_id=1, source_target_pairs={{0,32},{32,0},{64,96},{96,64},{1,33},{33,1},{65,97},{97,65},{2,34}... | collective-permute-start | bytes 7077896 | tf_op jit(solution)/shard_map/ppermute | solution.py:15
  55.7 26.2 %copy-start.24 = (bf16[384,3072]{1,0:T(8,128)(2,1)}, bf16[384,3072]{1,0:T(8,128)(2,1)S(1)}, u32[]{:S(2)}) copy-start(bf16[384,3072]{1,0:T(8,128)(2,1)S(1)} %get-tuple-element.38) | copy-start | bytes 7077892
  55.7 41.5 %copy-start.60 = (bf16[768]{0:T(1024)(128)(2,1)S(1)}, bf16[768]{0:T(1024)(128)(2,1)}, u32[]{:S(2)}) copy-start(bf16[768]{0:T(1024)(128)(2,1)} %param.21) | copy-start | bytes 4612
  81.9 17.2 %copy-start.39 = (bf16[384,2304]{1,0:T(8,128)(2,1)S(1)}, bf16[384,2304]{1,0:T(8,128)(2,1)}, u32[]{:S(2)}) copy-start(bf16[384,2304]{1,0:T(8,128)(2,1)} %copy-done.38) | copy-start | bytes 5308420
  81.9 17.2 %copy-start.42 = (bf16[384,2304]{1,0:T(8,128)(2,1)S(1)}, bf16[384,2304]{1,0:T(8,128)(2,1)}, u32[]{:S(2)}) copy-start(bf16[384,2304]{1,0:T(8,128)(2,1)} %copy-done.41) | copy-start | bytes 5308420
  82.5 14.7 %collective-permute-start.5 = (bf16[2,160,768]{2,1,0:T(8,128)(2,1)S(1)}, bf16[2,160,768]{2,1,0:T(8,128)(2,1)S(1)}, u32[]{:S(2)}, u32[]{:S(2)}) collective-permute-start(bf16[2,160,768]{2,1,0:T(8,128)(2,1)S(1)} %bitcast.147), channel_id=1, source_target_pairs={{0,64},{32,96},{1,65},{33,97},{2,66},{34,98},{3,67},{35,99},{4,68}... | collective-permute-start | bytes 1474568 | tf_op jit(solution)/shard_map/ppermute | solution.py:390
  114.0 56.6 %copy-start.45 = (f32[2,12,160]{2,1,0:T(8,128)}, f32[2,12,160]{2,1,0:T(8,128)S(1)}, u32[]{:S(2)}) copy-start(f32[2,12,160]{2,1,0:T(8,128)S(1)} %log_add_fusion) | copy-start | bytes 46084
  126.9 11.9 %copy-start.52 = (bf16[320,768]{1,0:T(8,128)(2,1)}, bf16[320,768]{1,0:T(8,128)(2,1)S(1)}, u32[]{:S(2)}) copy-start(bf16[320,768]{1,0:T(8,128)(2,1)S(1)} %add_convert_fusion.18) | copy-start | bytes 1474564
  126.9 11.9 %copy-start.29 = (bf16[1536,768]{1,0:T(8,128)(2,1)S(1)}, bf16[1536,768]{1,0:T(8,128)(2,1)}, u32[]{:S(2)}) copy-start(bf16[1536,768]{1,0:T(8,128)(2,1)} %get-tuple-element.40) | copy-start | bytes 7077892
  126.9 11.9 %copy-start.30 = (bf16[1536,768]{1,0:T(8,128)(2,1)S(1)}, bf16[1536,768]{1,0:T(8,128)(2,1)}, u32[]{:S(2)}) copy-start(bf16[1536,768]{1,0:T(8,128)(2,1)} %get-tuple-element.41) | copy-start | bytes 7077892
  189.7 14.9 %collective-permute-start.6 = (bf16[2,160,768]{2,1,0:T(8,128)(2,1)}, bf16[2,160,768]{2,1,0:T(8,128)(2,1)S(1)}, u32[]{:S(2)}, u32[]{:S(2)}) collective-permute-start(bf16[2,160,768]{2,1,0:T(8,128)(2,1)} %bitcast.22), channel_id=1, source_target_pairs={{64,0},{96,32},{65,1},{97,33},{66,2},{98,34},{67,3},{99,35},{68,4}... | collective-permute-start | bytes 1474568 | tf_op jit(solution)/shard_map/ppermute | solution.py:395
  191.5 15.9 %copy-start.7 = (f32[320,768]{1,0:T(8,128)S(1)}, f32[320,768]{1,0:T(8,128)}, u32[]{:S(2)}) copy-start(f32[320,768]{1,0:T(8,128)} %copy-done.6) | copy-start | bytes 2949124
  247.1 11.5 %copy-start.59 = (f32[3072]{0:T(1024)S(1)}, f32[3072]{0:T(1024)}, u32[]{:S(2)}) copy-start(f32[3072]{0:T(1024)} %get-tuple-element.153) | copy-start | bytes 36868
  247.1 17.5 %copy-start.34 = (bf16[2,160,768]{2,1,0:T(8,128)(2,1)S(1)}, bf16[2,160,768]{2,1,0:T(8,128)(2,1)}, u32[]{:S(2)}) copy-start(bf16[2,160,768]{2,1,0:T(8,128)(2,1)} %copy-done.32) | copy-start | bytes 1474564
  249.6 22.9 %slice-start = ((s8[4718592]{0:T(1024)(128)(4,1)}), s8[524288]{0:T(1024)(128)(4,1)S(1)}, s32[]{:S(2)}) async-start(s8[4718592]{0:T(1024)(128)(4,1)} %bitcast.137), calls=%async_computation | async-start | bytes 1048576
  264.3 21.5 %collective-permute-start.9 = (bf16[4608]{0:T(1024)(128)(2,1)}, bf16[4608]{0:T(1024)(128)(2,1)S(1)}, u32[]{:S(2)}, u32[]{:S(2)}) collective-permute-start(bf16[4608]{0:T(1024)(128)(2,1)} %dynamic-update-slice.7), channel_id=1, source_target_pairs={{0,32},{32,0},{64,96},{96,64},{1,33},{33,1},{65,97},{97,65},{2,34}... | collective-permute-start | bytes 27656 | tf_op jit(solution)/shard_map/ppermute | solution.py:15
  268.6 11.1 %collective-permute-start.8 = (bf16[384,2304]{1,0:T(8,128)(2,1)S(1)}, bf16[384,2304]{1,0:T(8,128)(2,1)S(1)}, u32[]{:S(2)}, u32[]{:S(2)}) collective-permute-start(bf16[384,2304]{1,0:T(8,128)(2,1)S(1)} %constant_dynamic-slice_fusion.16), channel_id=1, source_target_pairs={{0,32},{32,0},{64,96},{96,64},{1,33},{33,1},{65,97},{97,65},{2,34}... | collective-permute-start | bytes 5308424 | tf_op jit(solution)/shard_map/ppermute | solution.py:15
  272.2 22.6 %collective-permute-start.34 = (bf16[384,3072]{1,0:T(8,128)(2,1)}, bf16[384,3072]{1,0:T(8,128)(2,1)}, u32[]{:S(2)}, u32[]{:S(2)}) collective-permute-start(bf16[384,3072]{1,0:T(8,128)(2,1)} %constant_dynamic-slice_fusion.4), channel_id=1, source_target_pairs={{0,32},{32,0},{64,96},{96,64},{1,33},{33,1},{65,97},{97,65},{2,34}... | collective-permute-start | bytes 7077896 | tf_op jit(solution)/shard_map/ppermute | solution.py:15
  274.1 62.9 %collective-permute-start.29 = (bf16[1536,768]{1,0:T(8,128)(2,1)}, bf16[1536,768]{1,0:T(8,128)(2,1)}, u32[]{:S(2)}, u32[]{:S(2)}) collective-permute-start(bf16[1536,768]{1,0:T(8,128)(2,1)} %constant_dynamic-slice_fusion.9), channel_id=1, source_target_pairs={{0,32},{32,0},{64,96},{96,64},{1,33},{33,1},{65,97},{97,65},{2,34}... | collective-permute-start | bytes 7077896 | tf_op jit(solution)/shard_map/ppermute | solution.py:15
  279.3 7.8 %collective-permute-start.7 = (bf16[384,768]{1,0:T(8,128)(2,1)}, bf16[384,768]{1,0:T(8,128)(2,1)}, u32[]{:S(2)}, u32[]{:S(2)}) collective-permute-start(bf16[384,768]{1,0:T(8,128)(2,1)} %constant_dynamic-slice_fusion.17), channel_id=1, source_target_pairs={{0,32},{32,0},{64,96},{96,64},{1,33},{33,1},{65,97},{97,65},{2,34}... | collective-permute-start | bytes 1769480 | tf_op jit(solution)/shard_map/ppermute | solution.py:15
  281.7 12.1 %collective-permute-start.14 = (bf16[384,768]{1,0:T(8,128)(2,1)}, bf16[384,768]{1,0:T(8,128)(2,1)S(1)}, u32[]{:S(2)}, u32[]{:S(2)}) collective-permute-start(bf16[384,768]{1,0:T(8,128)(2,1)} %fusion.68), channel_id=1, source_target_pairs={{0,24},{1,25},{2,26},{3,27},{4,28},{5,29},{6,30},{7,31},{8,16},{9,... | collective-permute-start | bytes 1769480 | tf_op jit(solution)/shard_map/ppermute | solution.py:259
  289.1 13.7 %collective-permute-start.10 = (bf16[400,768]{1,0:T(8,128)(2,1)S(1)}, bf16[400,768]{1,0:T(8,128)(2,1)S(1)}, u32[]{:S(2)}, u32[]{:S(2)}) collective-permute-start(bf16[400,768]{1,0:T(8,128)(2,1)S(1)} %pad_maximum_fusion.8), channel_id=1, source_target_pairs={{0,8},{1,9},{2,10},{3,11},{4,12},{5,13},{6,14},{7,15},{8,0},{9,1},... | collective-permute-start | bytes 1843208 | tf_op jit(solution)/shard_map/ppermute | solution.py:259
  294.6 9.2 %collective-permute-start.15 = (bf16[192,768]{1,0:T(8,128)(2,1)S(1)}, bf16[192,768]{1,0:T(8,128)(2,1)S(1)}, u32[]{:S(2)}, u32[]{:S(2)}) collective-permute-start(bf16[192,768]{1,0:T(8,128)(2,1)S(1)} %constant_dynamic-slice_fusion.12), channel_id=1, source_target_pairs={{0,8},{1,9},{2,10},{3,11},{4,12},{5,13},{6,14},{7,15},{8,0},{9,1},... | collective-permute-start | bytes 884744 | tf_op jit(solution)/shard_map/ppermute | solution.py:259
  298.2 38.8 %slice-start.2 = ((s8[4718592]{0:T(1024)(128)(4,1)}), s8[4194304]{0:T(1024)(128)(4,1)S(1)}, s32[]{:S(2)}) async-start(s8[4718592]{0:T(1024)(128)(4,1)} %bitcast.139), calls=%async_computation.2 | async-start | bytes 8388608
  298.4 24.0 %copy-start.17 = (bf16[1536,768]{1,0:T(8,128)(2,1)}, bf16[1536,768]{1,0:T(8,128)(2,1)S(1)}, u32[]{:S(2)}) copy-start(bf16[1536,768]{1,0:T(8,128)(2,1)S(1)} %pad_maximum_fusion.4) | copy-start | bytes 7077892
  299.5 37.5 %slice-start.3 = ((s8[4718592]{0:T(1024)(128)(4,1)}), s8[524288]{0:T(1024)(128)(4,1)S(1)}, s32[]{:S(2)}) async-start(s8[4718592]{0:T(1024)(128)(4,1)} %bitcast.139), calls=%async_computation.3 | async-start | bytes 1048576
  299.5 52.9 %collective-permute-start.35 = (bf16[768,768]{1,0:T(8,128)(2,1)}, bf16[768,768]{1,0:T(8,128)(2,1)}, u32[]{:S(2)}, u32[]{:S(2)}) collective-permute-start(bf16[768,768]{1,0:T(8,128)(2,1)} %constant_dynamic-slice_fusion.3), channel_id=1, source_target_pairs={{0,24},{1,25},{2,26},{3,27},{4,28},{5,29},{6,30},{7,31},{8,16},{9,... | collective-permute-start | bytes 3538952 | tf_op jit(solution)/shard_map/ppermute | solution.py:259
  303.7 18.5 %collective-permute-start.11 = (bf16[208,768]{1,0:T(8,128)(2,1)S(1)}, bf16[208,768]{1,0:T(8,128)(2,1)S(1)}, u32[]{:S(2)}, u32[]{:S(2)}) collective-permute-start(bf16[208,768]{1,0:T(8,128)(2,1)S(1)} %pad_maximum_fusion.13), channel_id=1, source_target_pairs={{0,24},{1,25},{2,26},{3,27},{4,28},{5,29},{6,30},{7,31},{8,16},{9,... | collective-permute-start | bytes 958472 | tf_op jit(solution)/shard_map/ppermute | solution.py:259
  304.0 20.0 %collective-permute-start.16 = (bf16[96,768]{1,0:T(8,128)(2,1)S(1)}, bf16[96,768]{1,0:T(8,128)(2,1)S(1)}, u32[]{:S(2)}, u32[]{:S(2)}) collective-permute-start(bf16[96,768]{1,0:T(8,128)(2,1)S(1)} %constant_dynamic-slice_fusion.11), channel_id=1, source_target_pairs={{0,6},{1,7},{2,4},{3,5},{4,2},{5,3},{6,0},{7,1},{8,14},{9,15},{10,... | collective-permute-start | bytes 442376 | tf_op jit(solution)/shard_map/ppermute | solution.py:259
  322.4 5.5 %collective-permute-start.12 = (bf16[112,768]{1,0:T(8,128)(2,1)S(1)}, bf16[112,768]{1,0:T(8,128)(2,1)S(1)}, u32[]{:S(2)}, u32[]{:S(2)}) collective-permute-start(bf16[112,768]{1,0:T(8,128)(2,1)S(1)} %pad_maximum_fusion.19), channel_id=1, source_target_pairs={{0,2},{1,3},{2,0},{3,1},{4,6},{5,7},{6,4},{7,5},{8,10},{9,11},{10,... | collective-permute-start | bytes 516104 | tf_op jit(solution)/shard_map/ppermute | solution.py:259
  324.0 6.8 %collective-permute-start.17 = (bf16[48,768]{1,0:T(8,128)(2,1)S(1)}, bf16[48,768]{1,0:T(8,128)(2,1)S(1)}, u32[]{:S(2)}, u32[]{:S(2)}) collective-permute-start(bf16[48,768]{1,0:T(8,128)(2,1)S(1)} %constant_dynamic-slice_fusion.10), channel_id=1, source_target_pairs={{0,2},{1,3},{2,0},{3,1},{4,6},{5,7},{6,4},{7,5},{8,10},{9,11},{10,... | collective-permute-start | bytes 221192 | tf_op jit(solution)/shard_map/ppermute | solution.py:259
  328.0 5.9 %collective-permute-start.13 = (bf16[64,768]{1,0:T(8,128)(2,1)S(1)}, bf16[64,768]{1,0:T(8,128)(2,1)S(1)}, u32[]{:S(2)}, u32[]{:S(2)}) collective-permute-start(bf16[64,768]{1,0:T(8,128)(2,1)S(1)} %pad_maximum_fusion.23), channel_id=1, source_target_pairs={{0,6},{1,7},{2,4},{3,5},{4,2},{5,3},{6,0},{7,1},{8,14},{9,15},{10,... | collective-permute-start | bytes 294920 | tf_op jit(solution)/shard_map/ppermute | solution.py:259
  334.0 7.8 %collective-permute-start.18 = (bf16[112,768]{1,0:T(8,128)(2,1)S(1)}, bf16[112,768]{1,0:T(8,128)(2,1)S(1)}, u32[]{:S(2)}, u32[]{:S(2)}) collective-permute-start(bf16[112,768]{1,0:T(8,128)(2,1)S(1)} %pad_maximum_fusion.20), channel_id=1, source_target_pairs={{0,1},{1,0},{2,3},{3,2},{4,5},{5,4},{6,7},{7,6},{8,9},{9,8},{10,11... | collective-permute-start | bytes 516104 | tf_op jit(solution)/shard_map/ppermute | solution.py:259
  340.3 17.3 %collective-permute-start.30 = (bf16[768,768]{1,0:T(8,128)(2,1)}, bf16[768,768]{1,0:T(8,128)(2,1)}, u32[]{:S(2)}, u32[]{:S(2)}) collective-permute-start(bf16[768,768]{1,0:T(8,128)(2,1)} %constant_dynamic-slice_fusion.8), channel_id=1, source_target_pairs={{0,8},{1,9},{2,10},{3,11},{4,12},{5,13},{6,14},{7,15},{8,0},{9,1},... | collective-permute-start | bytes 3538952 | tf_op jit(solution)/shard_map/ppermute | solution.py:259
  341.8 1.2 collective-permute-start.19
  343.1 4.1 collective-permute-start.20
  344.4 5.6 %collective-permute-start.21 = (bf16[48,768]{1,0:T(8,128)(2,1)S(1)}, bf16[48,768]{1,0:T(8,128)(2,1)S(1)}, u32[]{:S(2)}, u32[]{:S(2)}) collective-permute-start(bf16[48,768]{1,0:T(8,128)(2,1)S(1)} %get-tuple-element.103), channel_id=1, source_target_pairs={{0,6},{1,7},{2,4},{3,5},{4,2},{5,3},{6,0},{7,1},{8,14},{9,15},{10,... | collective-permute-start | bytes 221192 | tf_op jit(solution)/shard_map/ppermute | solution.py:259
  347.1 5.2 %collective-permute-start.25 = (bf16[48,768]{1,0:T(8,128)(2,1)S(1)}, bf16[48,768]{1,0:T(8,128)(2,1)S(1)}, u32[]{:S(2)}, u32[]{:S(2)}) collective-permute-start(bf16[48,768]{1,0:T(8,128)(2,1)S(1)} %get-tuple-element.104), channel_id=1, source_target_pairs={{0,2},{1,3},{2,0},{3,1},{4,6},{5,7},{6,4},{7,5},{8,10},{9,11},{10,... | collective-permute-start | bytes 221192 | tf_op jit(solution)/shard_map/ppermute | solution.py:259
  354.4 11.5 %collective-permute-start.36 = (bf16[384,768]{1,0:T(8,128)(2,1)S(1)}, bf16[384,768]{1,0:T(8,128)(2,1)S(1)}, u32[]{:S(2)}, u32[]{:S(2)}) collective-permute-start(bf16[384,768]{1,0:T(8,128)(2,1)S(1)} %constant_dynamic-slice_fusion.2), channel_id=1, source_target_pairs={{0,8},{1,9},{2,10},{3,11},{4,12},{5,13},{6,14},{7,15},{8,0},{9,1},... | collective-permute-start | bytes 1769480 | tf_op jit(solution)/shard_map/ppermute | solution.py:259
  359.3 14.3 %collective-permute-start.31 = (bf16[384,768]{1,0:T(8,128)(2,1)S(1)}, bf16[384,768]{1,0:T(8,128)(2,1)S(1)}, u32[]{:S(2)}, u32[]{:S(2)}) collective-permute-start(bf16[384,768]{1,0:T(8,128)(2,1)S(1)} %constant_dynamic-slice_fusion.7), channel_id=1, source_target_pairs={{0,24},{1,25},{2,26},{3,27},{4,28},{5,29},{6,30},{7,31},{8,16},{9,... | collective-permute-start | bytes 1769480 | tf_op jit(solution)/shard_map/ppermute | solution.py:259
  362.6 26.2 %collective-permute-start.26 = (bf16[96,768]{1,0:T(8,128)(2,1)S(1)}, bf16[96,768]{1,0:T(8,128)(2,1)S(1)}, u32[]{:S(2)}, u32[]{:S(2)}) collective-permute-start(bf16[96,768]{1,0:T(8,128)(2,1)S(1)} %pad_maximum_fusion.22), channel_id=1, source_target_pairs={{0,6},{1,7},{2,4},{3,5},{4,2},{5,3},{6,0},{7,1},{8,14},{9,15},{10,... | collective-permute-start | bytes 442376 | tf_op jit(solution)/shard_map/ppermute | solution.py:259
  365.5 33.0 %collective-permute-start.22 = (bf16[96,768]{1,0:T(8,128)(2,1)S(1)}, bf16[96,768]{1,0:T(8,128)(2,1)S(1)}, u32[]{:S(2)}, u32[]{:S(2)}) collective-permute-start(bf16[96,768]{1,0:T(8,128)(2,1)S(1)} %pad_maximum_fusion.21), channel_id=1, source_target_pairs={{0,2},{1,3},{2,0},{3,1},{4,6},{5,7},{6,4},{7,5},{8,10},{9,11},{10,... | collective-permute-start | bytes 442376 | tf_op jit(solution)/shard_map/ppermute | solution.py:259
  366.1 8.1 %collective-permute-start.37 = (bf16[192,768]{1,0:T(8,128)(2,1)S(1)}, bf16[192,768]{1,0:T(8,128)(2,1)S(1)}, u32[]{:S(2)}, u32[]{:S(2)}) collective-permute-start(bf16[192,768]{1,0:T(8,128)(2,1)S(1)} %constant_dynamic-slice_fusion.1), channel_id=1, source_target_pairs={{0,6},{1,7},{2,4},{3,5},{4,2},{5,3},{6,0},{7,1},{8,14},{9,15},{10,... | collective-permute-start | bytes 884744 | tf_op jit(solution)/shard_map/ppermute | solution.py:259
  373.8 6.8 %collective-permute-start.32 = (bf16[192,768]{1,0:T(8,128)(2,1)S(1)}, bf16[192,768]{1,0:T(8,128)(2,1)S(1)}, u32[]{:S(2)}, u32[]{:S(2)}) collective-permute-start(bf16[192,768]{1,0:T(8,128)(2,1)S(1)} %constant_dynamic-slice_fusion.6), channel_id=1, source_target_pairs={{0,2},{1,3},{2,0},{3,1},{4,6},{5,7},{6,4},{7,5},{8,10},{9,11},{10,... | collective-permute-start | bytes 884744 | tf_op jit(solution)/shard_map/ppermute | solution.py:259
  374.3 9.3 %collective-permute-start.38 = (bf16[96,768]{1,0:T(8,128)(2,1)S(1)}, bf16[96,768]{1,0:T(8,128)(2,1)S(1)}, u32[]{:S(2)}, u32[]{:S(2)}) collective-permute-start(bf16[96,768]{1,0:T(8,128)(2,1)S(1)} %constant_dynamic-slice_fusion), channel_id=1, source_target_pairs={{0,2},{1,3},{2,0},{3,1},{4,6},{5,7},{6,4},{7,5},{8,10},{9,11},{10,... | collective-permute-start | bytes 442376 | tf_op jit(solution)/shard_map/ppermute | solution.py:259
  380.7 6.4 %collective-permute-start.33 = (bf16[96,768]{1,0:T(8,128)(2,1)S(1)}, bf16[96,768]{1,0:T(8,128)(2,1)S(1)}, u32[]{:S(2)}, u32[]{:S(2)}) collective-permute-start(bf16[96,768]{1,0:T(8,128)(2,1)S(1)} %constant_dynamic-slice_fusion.5), channel_id=1, source_target_pairs={{0,6},{1,7},{2,4},{3,5},{4,2},{5,3},{6,0},{7,1},{8,14},{9,15},{10,... | collective-permute-start | bytes 442376 | tf_op jit(solution)/shard_map/ppermute | solution.py:259
  387.2 8.3 %collective-permute-start.39 = (bf16[192,768]{1,0:T(8,128)(2,1)S(1)}, bf16[192,768]{1,0:T(8,128)(2,1)S(1)}, u32[]{:S(2)}, u32[]{:S(2)}) collective-permute-start(bf16[192,768]{1,0:T(8,128)(2,1)S(1)} %pad_maximum_fusion.16), channel_id=1, source_target_pairs={{0,1},{1,0},{2,3},{3,2},{4,5},{5,4},{6,7},{7,6},{8,9},{9,8},{10,11... | collective-permute-start | bytes 884744 | tf_op jit(solution)/shard_map/ppermute | solution.py:259
  388.8 17.8 %collective-permute-start.27 = (bf16[192,768]{1,0:T(8,128)(2,1)S(1)}, bf16[192,768]{1,0:T(8,128)(2,1)S(1)}, u32[]{:S(2)}, u32[]{:S(2)}) collective-permute-start(bf16[192,768]{1,0:T(8,128)(2,1)S(1)} %pad_maximum_fusion.15), channel_id=1, source_target_pairs={{0,8},{1,9},{2,10},{3,11},{4,12},{5,13},{6,14},{7,15},{8,0},{9,1},... | collective-permute-start | bytes 884744 | tf_op jit(solution)/shard_map/ppermute | solution.py:259
  395.7 8.1 %collective-permute-start.44 = (bf16[96,768]{1,0:T(8,128)(2,1)S(1)}, bf16[96,768]{1,0:T(8,128)(2,1)S(1)}, u32[]{:S(2)}, u32[]{:S(2)}) collective-permute-start(bf16[96,768]{1,0:T(8,128)(2,1)S(1)} %get-tuple-element.91), channel_id=1, source_target_pairs={{0,6},{1,7},{2,4},{3,5},{4,2},{5,3},{6,0},{7,1},{8,14},{9,15},{10,... | collective-permute-start | bytes 442376 | tf_op jit(solution)/shard_map/ppermute | solution.py:259
  398.5 6.7 %collective-permute-start.40 = (bf16[96,768]{1,0:T(8,128)(2,1)S(1)}, bf16[96,768]{1,0:T(8,128)(2,1)S(1)}, u32[]{:S(2)}, u32[]{:S(2)}) collective-permute-start(bf16[96,768]{1,0:T(8,128)(2,1)S(1)} %get-tuple-element.92), channel_id=1, source_target_pairs={{0,2},{1,3},{2,0},{3,1},{4,6},{5,7},{6,4},{7,5},{8,10},{9,11},{10,... | collective-permute-start | bytes 442376 | tf_op jit(solution)/shard_map/ppermute | solution.py:259
  398.6 18.7 %collective-permute-start.23 = (bf16[192,768]{1,0:T(8,128)(2,1)S(1)}, bf16[192,768]{1,0:T(8,128)(2,1)S(1)}, u32[]{:S(2)}, u32[]{:S(2)}) collective-permute-start(bf16[192,768]{1,0:T(8,128)(2,1)S(1)} %pad_maximum_fusion.14), channel_id=1, source_target_pairs={{0,24},{1,25},{2,26},{3,27},{4,28},{5,29},{6,30},{7,31},{8,16},{9,... | collective-permute-start | bytes 884744 | tf_op jit(solution)/shard_map/ppermute | solution.py:259
  405.3 11.2 %collective-permute-start.41 = (bf16[192,768]{1,0:T(8,128)(2,1)S(1)}, bf16[192,768]{1,0:T(8,128)(2,1)S(1)}, u32[]{:S(2)}, u32[]{:S(2)}) collective-permute-start(bf16[192,768]{1,0:T(8,128)(2,1)S(1)} %pad_maximum_fusion.17), channel_id=1, source_target_pairs={{0,6},{1,7},{2,4},{3,5},{4,2},{5,3},{6,0},{7,1},{8,14},{9,15},{10,... | collective-permute-start | bytes 884744 | tf_op jit(solution)/shard_map/ppermute | solution.py:259
  406.8 21.7 %collective-permute-start.28 = (bf16[384,768]{1,0:T(8,128)(2,1)S(1)}, bf16[384,768]{1,0:T(8,128)(2,1)S(1)}, u32[]{:S(2)}, u32[]{:S(2)}) collective-permute-start(bf16[384,768]{1,0:T(8,128)(2,1)S(1)} %pad_maximum_fusion.10), channel_id=1, source_target_pairs={{0,24},{1,25},{2,26},{3,27},{4,28},{5,29},{6,30},{7,31},{8,16},{9,... | collective-permute-start | bytes 1769480 | tf_op jit(solution)/shard_map/ppermute | solution.py:259
  409.6 9.6 %collective-permute-start.45 = (bf16[192,768]{1,0:T(8,128)(2,1)S(1)}, bf16[192,768]{1,0:T(8,128)(2,1)S(1)}, u32[]{:S(2)}, u32[]{:S(2)}) collective-permute-start(bf16[192,768]{1,0:T(8,128)(2,1)S(1)} %pad_maximum_fusion.18), channel_id=1, source_target_pairs={{0,2},{1,3},{2,0},{3,1},{4,6},{5,7},{6,4},{7,5},{8,10},{9,11},{10,... | collective-permute-start | bytes 884744 | tf_op jit(solution)/shard_map/ppermute | solution.py:259
  416.7 10.2 %collective-permute-start.42 = (bf16[384,768]{1,0:T(8,128)(2,1)S(1)}, bf16[384,768]{1,0:T(8,128)(2,1)S(1)}, u32[]{:S(2)}, u32[]{:S(2)}) collective-permute-start(bf16[384,768]{1,0:T(8,128)(2,1)S(1)} %pad_maximum_fusion.11), channel_id=1, source_target_pairs={{0,8},{1,9},{2,10},{3,11},{4,12},{5,13},{6,14},{7,15},{8,0},{9,1},... | collective-permute-start | bytes 1769480 | tf_op jit(solution)/shard_map/ppermute | solution.py:259
  417.5 15.7 %collective-permute-start.24 = (bf16[384,768]{1,0:T(8,128)(2,1)S(1)}, bf16[384,768]{1,0:T(8,128)(2,1)S(1)}, u32[]{:S(2)}, u32[]{:S(2)}) collective-permute-start(bf16[384,768]{1,0:T(8,128)(2,1)S(1)} %pad_maximum_fusion.9), channel_id=1, source_target_pairs={{0,8},{1,9},{2,10},{3,11},{4,12},{5,13},{6,14},{7,15},{8,0},{9,1},... | collective-permute-start | bytes 1769480 | tf_op jit(solution)/shard_map/ppermute | solution.py:259
  419.4 15.0 %collective-permute-start.46 = (bf16[384,768]{1,0:T(8,128)(2,1)S(1)}, bf16[384,768]{1,0:T(8,128)(2,1)S(1)}, u32[]{:S(2)}, u32[]{:S(2)}) collective-permute-start(bf16[384,768]{1,0:T(8,128)(2,1)S(1)} %pad_maximum_fusion.12), channel_id=1, source_target_pairs={{0,24},{1,25},{2,26},{3,27},{4,28},{5,29},{6,30},{7,31},{8,16},{9,... | collective-permute-start | bytes 1769480 | tf_op jit(solution)/shard_map/ppermute | solution.py:259
  427.2 17.5 %collective-permute-start.43 = (bf16[768,768]{1,0:T(8,128)(2,1)S(1)}, bf16[768,768]{1,0:T(8,128)(2,1)S(1)}, u32[]{:S(2)}, u32[]{:S(2)}) collective-permute-start(bf16[768,768]{1,0:T(8,128)(2,1)S(1)} %pad_maximum_fusion.6), channel_id=1, source_target_pairs={{0,24},{1,25},{2,26},{3,27},{4,28},{5,29},{6,30},{7,31},{8,16},{9,... | collective-permute-start | bytes 3538952 | tf_op jit(solution)/shard_map/ppermute | solution.py:259
  434.7 16.3 %collective-permute-start.47 = (bf16[768,768]{1,0:T(8,128)(2,1)S(1)}, bf16[768,768]{1,0:T(8,128)(2,1)S(1)}, u32[]{:S(2)}, u32[]{:S(2)}) collective-permute-start(bf16[768,768]{1,0:T(8,128)(2,1)S(1)} %pad_maximum_fusion.7), channel_id=1, source_target_pairs={{0,8},{1,9},{2,10},{3,11},{4,12},{5,13},{6,14},{7,15},{8,0},{9,1},... | collective-permute-start | bytes 3538952 | tf_op jit(solution)/shard_map/ppermute | solution.py:259
  (62 other events, 237.3 us)

commit v2 on v1

v2 whole, which is shorter than its diff:
```python
import functools
import math

import jax
import jax.numpy as jnp
from jax import lax
from jax.experimental import pallas as pl
from jax.experimental.pallas import tpu as pltpu
from jax.sharding import PartitionSpec as P

EPSILON = 1e-05
F32 = jnp.float32
LOW = jnp.bfloat16
WIDTH = 768
LENGTH = 160
ROWS = 320
HIDDEN = 3072
PAIRS = 6
TILE = 256
SCALE = 0.125
SIZES = (768, 384, 384, 384, 1536, 384, 384, 384)
QV, B_OUT, N1G, N1B, B_UP, B_DOWN, N2G, N2B = (sum(SIZES[:at]) for at in range(8))
SMALL = sum(SIZES)
VMEM_LIMIT = 56 * 1024 * 1024


def dot_nn(left_side, right_side):
    return jnp.dot(left_side, right_side, preferred_element_type=F32)


def dot_nt(left_side, right_side):
    return lax.dot_general(
        left_side, right_side, (((1,), (1,)), ((), ())), preferred_element_type=F32
    )


def dot_tn(left_side, right_side):
    return lax.dot_general(
        left_side, right_side, (((0,), (0,)), ((), ())), preferred_element_type=F32
    )


def columns(tile, width=TILE):
    return pl.ds(pl.multiple_of(tile * width, width), width)


def fetch(half, own, other, dest, sems):
    rows = own.shape[0]
    copies = (
        pltpu.make_async_copy(own, dest.at[pl.ds(half * rows, rows)], sems.at[0]),
        pltpu.make_async_copy(other, dest.at[pl.ds((1 - half) * rows, rows)], sems.at[1]),
    )
    for copy in copies:
        copy.start()
    return copies


def wait_all(copies):
    for copy in copies:
        copy.wait()


def whole(smalls, at, size):
    return jnp.concatenate([smalls[0:1, at : at + size], smalls[1:2, at : at + size]], axis=1)


def split_heads(tensor):
    lane = lax.broadcasted_iota(jnp.int32, tensor.shape, 1)
    zero = jnp.zeros_like(tensor)
    return jnp.concatenate(
        [jnp.where(lane < 64, tensor, zero), jnp.where(lane < 64, zero, tensor)], axis=0
    )


def join_heads(tensor):
    lane = lax.broadcasted_iota(jnp.int32, (LENGTH, 128), 1)
    return jnp.where(lane < 64, tensor[:LENGTH], tensor[LENGTH:])


def normalize(values):
    center = values - jnp.mean(values, axis=-1, keepdims=True)
    spread = jnp.mean(center * center, axis=-1, keepdims=True)
    inverse = lax.rsqrt(spread + EPSILON)
    return center * inverse, inverse


def normalize_back(upstream, gain, normal, inverse):
    scaled = upstream * gain
    first = jnp.mean(scaled, axis=-1, keepdims=True)
    second = jnp.mean(scaled * normal, axis=-1, keepdims=True)
    return inverse * (scaled - first - normal * second)


def gelu_parts(values):
    size = jnp.abs(values)
    below = 1.0 + (0.3275911 * math.sqrt(0.5)) * size
    t = pl.reciprocal(below, approx=True)
    t = t * (2.0 - below * t)
    series = t * (
        0.5 * 0.254829592
        + t
        * (
            0.5 * -0.284496736
            + t * (0.5 * 1.421413741 + t * (0.5 * -1.453152027 + t * (0.5 * 1.061405429)))
        )
    )
    bell = jnp.exp(-0.5 * values * values)
    tail = series * bell
    share = jnp.where(values >= 0.0, 1.0 - tail, tail)
    return values * share, share + values * bell * (1.0 / math.sqrt(2.0 * math.pi))


def attend_body(h, wqkv, wout, smalls, lens, qkv, probs, mixed, normal1, inverse1, u):
    x = h[...]
    for block, bias in ((0, smalls[0:1, QV : QV + 768]), (1, None), (2, smalls[1:2, QV : QV + 768])):
        for tile in range(3):
            at = block * WIDTH + tile * TILE
            part = dot_nn(x, wqkv[:, at : at + TILE])
            if bias is not None:
                part = part + bias[:, tile * TILE : (tile + 1) * TILE]
            qkv[:, at : at + TILE] = part.astype(LOW)

    def heads(index, carry):
        chain = index // PAIRS
        pair = index % PAIRS
        rows = pl.ds(pl.multiple_of(chain * LENGTH, LENGTH), LENGTH)
        q = qkv[rows, columns(pair, 128)]
        k = qkv[rows, columns(pair + PAIRS, 128)]
        v = qkv[rows, columns(pair + 2 * PAIRS, 128)]
        scores = dot_nt(split_heads(q), k) * SCALE
        key = lax.broadcasted_iota(jnp.int32, scores.shape, 1)
        scores = jnp.where(key < lens[chain], scores, -1000000000.0)
        grown = jnp.exp(scores - jnp.max(scores, axis=-1, keepdims=True))
        weights = (grown / jnp.sum(grown, axis=-1, keepdims=True)).astype(LOW)
        if probs is not None:
            probs[index] = weights
        mixed[rows, columns(pair, 128)] = join_heads(dot_nn(weights, v)).astype(LOW)
        return carry

    lax.fori_loop(0, 2 * PAIRS, heads, 0)
    branch = dot_nn(mixed[...], wout[...]) + whole(smalls, B_OUT, 384)
    normal, inverse = normalize(x.astype(F32) + branch)
    if normal1 is not None:
        normal1[...] = normal
        inverse1[...] = inverse
    u[...] = (normal * whole(smalls, N1G, 384) + whole(smalls, N1B, 384)).astype(LOW)


def feed_body(u, wup, wdown, smalls, slope, active, normal2, inverse2, y, total):
    x = u[...]
    total[...] = x.astype(F32) + whole(smalls, B_DOWN, 384)

    def step(tile, carry):
        place = columns(tile)
        bias = smalls[
            pl.ds(tile // 6, 1), pl.ds(pl.multiple_of(B_UP + (tile % 6) * TILE, 128), TILE)
        ]
        grown, tangent = gelu_parts(dot_nn(x, wup[:, place]) + bias)
        f = grown.astype(LOW)
        if slope is not None:
            slope[:, place] = tangent.astype(LOW)
            active[:, place] = f
        total[...] += dot_nn(f, wdown[place, :])
        return carry

    lax.fori_loop(0, HIDDEN // TILE, step, 0)
    normal, inverse = normalize(total[...])
    if normal2 is not None:
        normal2[...] = normal
        inverse2[...] = inverse
    y[...] = (normal * whole(smalls, N2G, 384) + whole(smalls, N2B, 384)).astype(LOW)


def put_halves(target, at, row):
    size = row.shape[1] // 2
    target[0:1, at : at + size] = row[:, :size]
    target[1:2, at : at + size] = row[:, size:]


def column_sum(values):
    return jnp.sum(values, axis=0, keepdims=True)


def feed_back_body(
    gy, wup, wdown, smalls, slope, normal1, inverse1, normal2, inverse2, gz, ga, gr1, gb, gsmall, total
):
    up = gy[...].astype(F32)
    normal = normal2[...]
    put_halves(gsmall, N2G, column_sum(up * normal))
    put_halves(gsmall, N2B, column_sum(up))
    grad = normalize_back(up, whole(smalls, N2G, 384), normal, inverse2[...])
    z = grad.astype(LOW)
    gz[...] = z
    put_halves(gsmall, B_DOWN, column_sum(z.astype(F32)))
    total[...] = grad

    def step(tile, carry):
        place = columns(tile)
        inner = dot_nt(z, wdown[place, :]) * slope[:, place].astype(F32)
        a = inner.astype(LOW)
        ga[:, place] = a
        gsmall[pl.ds(tile // 6, 1), pl.ds(pl.multiple_of(B_UP + (tile % 6) * TILE, 128), TILE)] = (
            column_sum(a.astype(F32))
        )
        total[...] += dot_nt(a, wup[:, place])
        return carry

    lax.fori_loop(0, HIDDEN // TILE, step, 0)
    up = total[...]
    normal = normal1[...]
    put_halves(gsmall, N1G, column_sum(up * normal))
    put_halves(gsmall, N1B, column_sum(up))
    grad = normalize_back(up, whole(smalls, N1G, 384), normal, inverse1[...])
    gr1[...] = grad
    b = grad.astype(LOW)
    gb[...] = b
    put_halves(gsmall, B_OUT, column_sum(b.astype(F32)))


def attend_back_body(gb, gr1, wqkv, wout, spans, first, qkv, probs, gqkv, gh, gqv, gmask, go):
    go[...] = dot_nt(gb[...], wout[...]).astype(LOW)

    def heads(index, carry):
        chain = index // PAIRS
        pair = index % PAIRS
        rows = pl.ds(pl.multiple_of(chain * LENGTH, LENGTH), LENGTH)
        q = split_heads(qkv[rows, columns(pair, 128)])
        k = qkv[rows, columns(pair + PAIRS, 128)]
        v = qkv[rows, columns(pair + 2 * PAIRS, 128)]
        g = split_heads(go[rows, columns(pair, 128)])
        weights = probs[index]
        wide = weights.astype(F32)
        inner = dot_nt(g, v)
        inner = wide * (inner - jnp.sum(wide * inner, axis=-1, keepdims=True))
        s = inner.astype(LOW)
        gqkv[rows, columns(pair, 128)] = (join_heads(dot_nn(s, k)) * SCALE).astype(LOW)
        gqkv[rows, columns(pair + PAIRS, 128)] = (dot_tn(s, q) * SCALE).astype(LOW)
        gqkv[rows, columns(pair + 2 * PAIRS, 128)] = dot_tn(weights, g).astype(LOW)
        return carry

    lax.fori_loop(0, 2 * PAIRS, heads, 0)
    gqv[0:1, :] = column_sum(gqkv[:, :WIDTH].astype(F32))
    gqv[1:2, :] = column_sum(gqkv[:, 2 * WIDTH :].astype(F32))
    full = gr1[...] + dot_nt(gqkv[...], wqkv[...])
    row = lax.broadcasted_iota(jnp.int32, (ROWS, 1), 0)
    dropped = row < 0
    for chain in range(2):
        start = spans[chain, 0] + chain * LENGTH
        end = spans[chain, 1] + chain * LENGTH
        dropped = dropped | ((row >= start) & (row < end))
    dropped = dropped & (first[0] > 0)
    zero = jnp.zeros_like(full)
    gh[...] = jnp.where(dropped, zero, full).astype(LOW)
    gmask[...] = column_sum(jnp.where(dropped, full, zero))


VMEM = pl.BlockSpec(memory_space=pltpu.VMEM)
SMEM = pl.BlockSpec(memory_space=pltpu.SMEM)
ANY = pl.BlockSpec(memory_space=pl.ANY)


def shape(dims, kind=LOW):
    return jax.ShapeDtypeStruct(dims, kind)


def kernel_call(body, ins, outs, scratch, flops, moved, name):
    return pl.pallas_call(
        body,
        in_specs=ins,
        out_specs=[VMEM] * len(outs),
        out_shape=outs,
        scratch_shapes=scratch,
        compiler_params=pltpu.CompilerParams(vmem_limit_bytes=VMEM_LIMIT),
        cost_estimate=pl.CostEstimate(flops=flops, bytes_accessed=moved, transcendentals=0),
        name=name,
    )


QKV_SHAPE = (ROWS, 3 * WIDTH)
PROBS_SHAPE = (2 * PAIRS, 2 * LENGTH, LENGTH)
ROW_SHAPE = (ROWS, WIDTH)
MACS = ROWS * WIDTH * WIDTH * 2


def attend(h, half, lens, weights, smalls, save):
    def body(h, half, lens, smalls, qo, qp, oo, op, *rest):
        if save:
            qkv, probs, mixed, normal1, inverse1, u, wqkv, wout, sems = rest
        else:
            u, qkv, mixed, wqkv, wout, sems = rest
            probs = normal1 = inverse1 = None
        first = fetch(half[0], qo, qp, wqkv, sems.at[0])
        second = fetch(half[0], oo, op, wout, sems.at[1])
        wait_all(first)
        wait_all(second)
        attend_body(h, wqkv, wout, smalls, lens, qkv, probs, mixed, normal1, inverse1, u)

    outs = [shape(ROW_SHAPE)]
    scratch = [
        pltpu.VMEM((WIDTH, 3 * WIDTH), LOW),
        pltpu.VMEM((WIDTH, WIDTH), LOW),
        pltpu.SemaphoreType.DMA((2, 2)),
    ]
    if save:
        outs = [
            shape(QKV_SHAPE),
            shape(PROBS_SHAPE),
            shape(ROW_SHAPE),
            shape(ROW_SHAPE, F32),
            shape((ROWS, 1), F32),
        ] + outs
    else:
        scratch = [pltpu.VMEM(QKV_SHAPE, LOW), pltpu.VMEM(ROW_SHAPE, LOW)] + scratch
    return kernel_call(
        body, [VMEM, SMEM, SMEM, VMEM] + [ANY] * 4, outs, scratch, 4 * MACS, 8000000, "attend"
    )(h, half, lens, smalls, *weights[0], *weights[1])


def feed(u, half, weights, smalls, save):
    def body(u, half, smalls, uo, up, do, dp, *rest):
        if save:
            slope, active, normal2, inverse2, y, total, wup, wdown, sems = rest
        else:
            y, total, wup, wdown, sems = rest
            slope = active = normal2 = inverse2 = None
        first = fetch(half[0], uo, up, wup, sems.at[0])
        second = fetch(half[0], do, dp, wdown, sems.at[1])
        wait_all(first)
        wait_all(second)
        feed_body(u, wup, wdown, smalls, slope, active, normal2, inverse2, y, total)

    outs = [shape(ROW_SHAPE)]
    scratch = [
        pltpu.VMEM(ROW_SHAPE, F32),
        pltpu.VMEM((WIDTH, HIDDEN), LOW),
        pltpu.VMEM((HIDDEN, WIDTH), LOW),
        pltpu.SemaphoreType.DMA((2, 2)),
    ]
    if save:
        outs = [
            shape((ROWS, HIDDEN)),
            shape((ROWS, HIDDEN)),
            shape(ROW_SHAPE, F32),
            shape((ROWS, 1), F32),
        ] + outs
    return kernel_call(
        body, [VMEM, SMEM, VMEM] + [ANY] * 4, outs, scratch, 8 * MACS, 14000000, "feed"
    )(u, half, smalls, *weights[2], *weights[3])


def feed_back(gy, half, weights, smalls, slope, normal1, inverse1, normal2, inverse2):
    def body(gy, half, smalls, uo, up, do, dp, slope, n1, i1, n2, i2, *rest):
        gz, ga, gr1, gb, gsmall, total, wup, wdown, sems = rest
        second = fetch(half[0], do, dp, wdown, sems.at[1])
        first = fetch(half[0], uo, up, wup, sems.at[0])
        wait_all(second)
        wait_all(first)
        feed_back_body(
            gy, wup, wdown, smalls, slope, n1, i1, n2, i2, gz, ga, gr1, gb, gsmall, total
        )

    outs = [
        shape(ROW_SHAPE),
        shape((ROWS, HIDDEN)),
        shape(ROW_SHAPE, F32),
        shape(ROW_SHAPE),
        shape((2, SMALL), F32),
    ]
    scratch = [
        pltpu.VMEM(ROW_SHAPE, F32),
        pltpu.VMEM((WIDTH, HIDDEN), LOW),
        pltpu.VMEM((HIDDEN, WIDTH), LOW),
        pltpu.SemaphoreType.DMA((2, 2)),
    ]
    return kernel_call(
        body,
        [VMEM, SMEM, VMEM] + [ANY] * 4 + [VMEM] * 5,
        outs,
        scratch,
        8 * MACS,
        18000000,
        "feed_back",
    )(
        gy,
        half,
        smalls,
        *weights[2],
        *weights[3],
        slope,
        normal1,
        inverse1,
        normal2,
        inverse2,
    )


def attend_back(gb, gr1, half, spans, first, weights, qkv, probs):
    def body(gb, gr1, half, spans, first, qo, qp, oo, op, qkv, probs, *rest):
        gqkv, gh, gqv, gmask, go, wqkv, wout, sems = rest
        second = fetch(half[0], oo, op, wout, sems.at[1])
        start = fetch(half[0], qo, qp, wqkv, sems.at[0])
        wait_all(second)
        wait_all(start)
        attend_back_body(gb, gr1, wqkv, wout, spans, first, qkv, probs, gqkv, gh, gqv, gmask, go)

    outs = [
        shape(QKV_SHAPE),
        shape(ROW_SHAPE),
        shape((2, WIDTH), F32),
        shape((1, WIDTH), F32),
    ]
    scratch = [
        pltpu.VMEM(ROW_SHAPE, LOW),
        pltpu.VMEM((WIDTH, 3 * WIDTH), LOW),
        pltpu.VMEM((WIDTH, WIDTH), LOW),
        pltpu.SemaphoreType.DMA((2, 2)),
    ]
    return kernel_call(
        body,
        [VMEM, VMEM, SMEM, SMEM, SMEM] + [ANY] * 4 + [VMEM] * 2,
        outs,
        scratch,
        4 * MACS,
        12000000,
        "attend_back",
    )(gb, gr1, half, spans, first, *weights[0], *weights[1], qkv, probs)


def partner(x, axis, bit):
    return lax.ppermute(x, axis, [(i, i ^ 1 << bit) for i in range(lax.axis_size(axis))])


def assemble(own_part, partner_part, pair_half):
    lower = jnp.where(pair_half == 0, own_part, partner_part)
    upper = jnp.where(pair_half == 0, partner_part, own_part)
    return jnp.concatenate([lower, upper], axis=0)


def take_half(tensor, which_half):
    half_rows = tensor.shape[0] // 2
    return lax.dynamic_slice_in_dim(tensor, which_half * half_rows, half_rows, 0)


ORDERS = (
    (("zw", "zu", "xw", "xu"), ("zu", "zw", "xu", "xw")),
    (("xw", "xu", "zw", "zu"), ("xu", "xw", "zu", "zw")),
)


def flip_dp(index, bit):
    z, x, y = index // 8, index // 2 % 4, index % 2
    if bit == "zw":
        z ^= 1
    elif bit == "zu":
        z ^= 3
    elif bit == "xw":
        x ^= 1
    elif bit == "xu":
        x ^= 3
    else:
        y ^= 1
    return z * 8 + x * 2 + y


def flip_pairs(bit_of_core):
    pairs = []
    for section in range(4):
        for index in range(32):
            pairs.append(
                (section * 32 + index, section * 32 + flip_dp(index, bit_of_core[section % 2]))
            )
    return pairs


def exchange(value, bit_of_core):
    return lax.ppermute(value, ("section", "dp"), flip_pairs(bit_of_core))


def own_bits():
    index = lax.axis_index("dp")
    z, x, y = index // 8, index // 2 % 4, index % 2
    return {
        "zu": z // 2,
        "zw": (z // 2) ^ (z % 2),
        "xu": x // 2,
        "xw": (x // 2) ^ (x % 2),
        "y": y,
    }


def own_bit(bits, core, part, step):
    return jnp.where(core == 0, bits[ORDERS[0][part][step]], bits[ORDERS[1][part][step]])


def add_low(left_side, right_side):
    return (left_side.astype(jnp.float32) + right_side.astype(jnp.float32)).astype(jnp.bfloat16)


def reduce_rows(pack, extra, bits, core):
    half = pack.shape[0] // 2
    parts = [pack[:half], pack[half:]]
    for step in range(4):
        for part in range(2):
            bit = own_bit(bits, core, part, step)
            rows = parts[part].shape[0] // 2
            keep = lax.dynamic_slice_in_dim(parts[part], bit * rows, rows, 0)
            send = lax.dynamic_slice_in_dim(parts[part], (1 - bit) * rows, rows, 0)
            flips = (ORDERS[0][part][step], ORDERS[1][part][step])
            if part == 0 and extra is not None:
                got = exchange(jnp.concatenate([send, extra], axis=0), flips)
                extra = add_low(extra, got[rows:])
                got = got[:rows]
            else:
                got = exchange(send, flips)
            parts[part] = add_low(keep, got)
    rows = parts[0].shape[0]
    both = jnp.concatenate(parts + ([extra] if extra is not None else []), axis=0)
    both = add_low(both, exchange(both, ("y", "y")))
    parts = [both[:rows], both[rows : 2 * rows]]
    if extra is not None:
        extra = both[2 * rows :]
    for step in reversed(range(4)):
        for part in range(2):
            bit = own_bit(bits, core, part, step)
            flips = (ORDERS[0][part][step], ORDERS[1][part][step])
            got = exchange(parts[part], flips)
            parts[part] = assemble(parts[part], got, bit)
    return jnp.concatenate(parts, axis=0), extra


def fold(tensor):
    return jnp.concatenate(
        [tensor[:, at : at + 768] for at in range(0, tensor.shape[1], 768)], axis=0
    )


def unfold(rows, count):
    return jnp.concatenate(jnp.split(rows, count, axis=0), axis=1)


def per_device(
    inputs,
    cotangent,
    lengths,
    cdr_spans,
    mask_vector,
    w_qkv,
    qv_bias,
    w_out,
    b_out,
    norm1_gain,
    norm1_bias,
    w_up,
    b_up,
    w_down,
    b_down,
    norm2_gain,
    norm2_bias,
):
    section_index = lax.axis_index("section")
    is_first = section_index < 2
    pair_half = section_index % 2
    half = pair_half.astype(jnp.int32).reshape(1)
    first = is_first.astype(jnp.int32).reshape(1)
    big = (w_qkv, w_out, w_up, w_down)
    small = jnp.concatenate(
        [qv_bias, b_out, norm1_gain, norm1_bias, b_up, b_down, norm2_gain, norm2_bias]
    )
    partner_small = partner(small, "section", 0)
    weights = [(tensor, partner(tensor, "section", 0)) for tensor in big]
    smalls = jnp.where(
        pair_half == 0,
        jnp.stack([small, partner_small]),
        jnp.stack([partner_small, small]),
    ).astype(F32)
    my_inputs = lax.dynamic_index_in_dim(inputs, pair_half, 0, keepdims=False)
    my_cotangent = lax.dynamic_index_in_dim(cotangent, pair_half, 0, keepdims=False)
    lens = lax.dynamic_index_in_dim(lengths, pair_half, 0, keepdims=False)
    spans = lax.dynamic_index_in_dim(cdr_spans, pair_half, 0, keepdims=False)
    positions = jnp.arange(LENGTH, dtype=jnp.int32)
    masked = (positions[None, :] >= spans[:, 0:1]) & (positions[None, :] < spans[:, 1:2])
    entered = jnp.where(masked[:, :, None], mask_vector[None, None, :], my_inputs)
    entered = entered.reshape(ROWS, WIDTH)
    my_cotangent = my_cotangent.reshape(ROWS, WIDTH)

    (u,) = attend(entered, half, lens, weights, smalls, False)
    (first_out,) = feed(u, half, weights, smalls, False)
    received = lax.ppermute(first_out, "section", [(0, 2), (1, 3)])
    layer_in = jnp.where(is_first, entered, received)
    qkv, probs, mixed, normal1, inverse1, u = attend(layer_in, half, lens, weights, smalls, True)
    slope, active, normal2, inverse2, output = feed(u, half, weights, smalls, True)

    def back(upstream):
        gz, ga, gr1, gb, gsmall = feed_back(
            upstream, half, weights, smalls, slope, normal1, inverse1, normal2, inverse2
        )
        gqkv, gh, gqv, gmask = attend_back(gb, gr1, half, spans, first, weights, qkv, probs)
        return gz, ga, gb, gsmall, gqkv, gh, gqv, gmask

    upper_grad = back(my_cotangent)[5]
    returned = lax.ppermute(upper_grad, "section", [(2, 0), (3, 1)])
    upstream = jnp.where(is_first, returned, my_cotangent)
    gz, ga, gb, gsmall, gqkv, gh, gqv, gmask = back(upstream)

    def pair_sum(left_side, right_side):
        low = dot_tn(left_side, right_side).astype(LOW)
        got = partner(take_half(low, 1 - pair_half), "section", 0)
        return add_low(take_half(low, pair_half), got)

    bits = own_bits()
    early = jnp.concatenate([pair_sum(active, gz), fold(pair_sum(u, ga))], axis=0)
    gsmall = jnp.concatenate([gqv, gsmall[:, WIDTH:]], axis=1)
    own_small = lax.dynamic_index_in_dim(gsmall, pair_half, 0, keepdims=False)
    other_small = lax.dynamic_index_in_dim(gsmall, 1 - pair_half, 0, keepdims=False)
    summed_small = own_small + partner(other_small.astype(LOW), "section", 0).astype(F32)
    extra = jnp.concatenate(
        [
            summed_small.astype(LOW).reshape(6, WIDTH),
            gmask.astype(LOW),
            jnp.zeros((9, WIDTH), LOW),
        ],
        axis=0,
    )
    late = jnp.concatenate([pair_sum(mixed, gb), fold(pair_sum(layer_in, gqkv))], axis=0)
    early, _ = reduce_rows(early, None, bits, pair_half)
    late, extra = reduce_rows(late, extra, bits, pair_half)
    mask_row = extra[6:7]
    mask_row = mask_row.astype(F32) + partner(mask_row, "section", 0).astype(F32)
    mask_low = mask_row.astype(LOW)
    mask_row = mask_low.astype(F32) + partner(mask_low, "section", 1).astype(F32)
    mask_grad = mask_row[0]

    flat_small = extra[:6].reshape(-1).astype(F32)
    out_small = []
    at = 0
    for size in SIZES:
        out_small.append(flat_small[at : at + size])
        at += size
    g_qv, g_bo, g_n1g, g_n1b, g_bu, g_bd, g_n2g, g_n2b = out_small
    return (
        output.reshape(1, 2, LENGTH, WIDTH),
        gh.reshape(1, 2, LENGTH, WIDTH),
        mask_grad,
        unfold(late[384:], 3).astype(F32),
        g_qv,
        late[:384].astype(F32),
        g_bo,
        g_n1g,
        g_n1b,
        unfold(early[1536:], 4).astype(F32),
        g_bu,
        early[:1536].astype(F32),
        g_bd,
        g_n2g,
        g_n2b,
    )


def solution(mesh):
    in_specs = (
        P(None, "dp", None, None),
        P(None, "dp", None, None),
        P(None, "dp"),
        P(None, "dp", None),
        P(),
        P("section", None),
        P("section"),
        P("section", None),
        P("section"),
        P("section"),
        P("section"),
        P("section", None),
        P("section"),
        P("section", None),
        P("section"),
        P("section"),
        P("section"),
    )
    out_specs = (
        P("section", "dp", None, None),
        P("section", "dp", None, None),
        P(),
        P("section", None),
        P("section"),
        P("section", None),
        P("section"),
        P("section"),
        P("section"),
        P("section", None),
        P("section"),
        P("section", None),
        P("section"),
        P("section"),
        P("section"),
    )
    return jax.shard_map(
        per_device, mesh=mesh, in_specs=in_specs, out_specs=out_specs, check_vma=False
    )
```

time: 460 us -> 380 us (0.83)
  Pallas kernels: 0 us -> 127 us
  matrix products: 111 us -> 9.96 us
  local copies, waits for them, and re-layouts: 102 us -> 24.1 us
  other arithmetic: 66 us -> 34.4 us
    pallas_call x0 -> x8, Pallas kernels: none -> 127 us  [the longest x2 35.7 us: feed(): kernel_call(body, [VMEM, SMEM, VMEM] + [ANY] * 4, outs, scratch, 8 * MACS...]
    dot_general x30 -> x4, matrix products: 111 us -> 9.96 us  [dot_tn(): lax.dot_general(left_side, right_side, (((0,), (0,)), ((), ())), preferre...]
    unnamed x184 -> x57, local copies, waits for them, and re-layouts: 37 us -> 11.8 us
    convert_element_type x9 -> x1, local copies, waits for them, and re-layouts: 18.2 us -> 0.01 us  [per_device(): flat_small = extra[:6].reshape(-1).astype(F32)]
    reshape x7 -> x1, local copies, waits for them, and re-layouts: 17.8 us -> 0.03 us  [per_device(): summed_small.astype(LOW).reshape(6, WIDTH)]
    reduce_sum x15 -> x0, other arithmetic: 14 us -> none  [the longest x4 4.64 us: norm_rows(): center = values - jnp.mean(values, axis=-1, keepdims=True)]
    select_n x17 -> x13, other arithmetic: 14 us -> 2.18 us  [assemble(): lower = jnp.where(pair_half == 0, own_part, partner_part)]
    slice x9 -> x2, local copies, waits for them, and re-layouts: 8.61 us -> 0.17 us  [the longest x1 0.17 us: per_device(): spans[:, 0:1]]
  transfers between devices with their start and end apart: 48 -> 48, of which waited for: 23 -> 22; matrix products, arithmetic and copies ran while one was open for 18% -> 14% of each run, Pallas kernels for 0% -> 4%
where the time goes in v2:
time: 380 us; the launch traced here: 374 us
  Pallas kernels  127 us (33%)
  waiting for transfers between devices  113 us (30%)
  starting transfers between devices  63 us (17%)
  other arithmetic  34.4 us (9%)
  local copies, waits for them, and re-layouts  24.1 us (6%)
  matrix products  9.96 us (3%)
    ppermute x34, waiting for transfers between devices, exchange(): return lax.ppermute(value, ('section', 'dp'), flip_pairs(bit_of_core))  88.7 us
    ppermute x34, starting transfers between devices, exchange(): return lax.ppermute(value, ('section', 'dp'), flip_pairs(bit_of_core))  54.5 us
    pallas_call x2, Pallas kernels, feed(): kernel_call(body, [VMEM, SMEM, VMEM] + [ANY] * 4, outs, scratch, 8 * MACS...  35.7 us
    pallas_call x2, Pallas kernels, feed_back(): kernel_call(body, [VMEM, SMEM, VMEM] + [ANY] * 4 + [VMEM] * 5, outs, scra...  34.5 us
    pallas_call x2, Pallas kernels, attend_back(): kernel_call(body, [VMEM, VMEM, SMEM, SMEM, SMEM] + [ANY] * 4 + [VMEM] * 2...  30.1 us
    pallas_call x2, Pallas kernels, attend(): kernel_call(body, [VMEM, SMEM, SMEM, VMEM] + [ANY] * 4, outs, scratch, 4...  27.2 us
    convert_element_type x26, other arithmetic, add_low(): (left_side.astype(jnp.float32) + right_side.astype(jnp.float32)).astype(j...  14.4 us
    ppermute x1, waiting for transfers between devices, per_device(): returned = lax.ppermute(upper_grad, 'section', [(2, 0), (3, 1)])  13.2 us
  transfers between devices with their start and end apart: 48, of which 22 were waited for; matrix products, arithmetic and copies ran while one was open for 14% of the time, Pallas kernels for 4%

profile of v2, /device:TPU:0, one launch (start us, length us, event | category | flops | bytes accessed | tf_op | source)
XLA Modules:
  0.0 373.9 jit_solution(5332478824394289181)
XLA Ops:
  10.6 1.6 bitcast_select_fusion.h
  14.9 13.2 %attend.2.u = bf16[320,768]{1,0:T(8,128)(2,1)} custom-call(bf16[320,768]{1,0:T(8,128)(2,1)} %bitcast_select_fusion.h, s32[1]{0:T(128)} %bitcast.2.half, s32[2]{0:T(128)} %fusion.9.lens, f32[2,4608]{1,0:T(2,128)} %fusion.6.smalls, bf16[384,2304]{1,0:T(8,128)(2,1)} %qo.7, bf16[384,2304]{1,0:T(8,128)(2,1)} %copy-done.2, bf16[384,768]{1,0:T(8,128)(2,1)} %oo.7, ...), custom_call_target="tpu_custom_call" | custom-call | flops 1509949440 | bytes 8000000 | tf_op jit(solution)/shard_map/attend/pallas_call | solution.py:314
  28.2 17.1 %feed.2 = bf16[320,768]{1,0:T(8,128)(2,1)} custom-call(bf16[320,768]{1,0:T(8,128)(2,1)} %attend.2.u, s32[1]{0:T(128)} %bitcast.2.half, f32[2,4608]{1,0:T(2,128)} %fusion.6.smalls, bf16[384,3072]{1,0:T(8,128)(2,1)} %uo.7, bf16[384,3072]{1,0:T(8,128)(2,1)} %collective-permute-done.3.up, bf16[1536,768]{1,0:T(8,128)(2,1)} %do.7, ...), custom_call_target="tpu_custom_call" | custom-call | flops 3019898880 | bytes 14000000 | tf_op jit(solution)/shard_map/feed/pallas_call | solution.py:346
  45.3 3.9 %collective-permute-start.5 = (bf16[320,768]{1,0:T(8,128)(2,1)}, bf16[320,768]{1,0:T(8,128)(2,1)S(1)}, u32[]{:S(2)}, u32[]{:S(2)}) collective-permute-start(bf16[320,768]{1,0:T(8,128)(2,1)} %feed.2), channel_id=1, source_target_pairs={{0,64},{32,96},{1,65},{33,97},{2,66},{34,98},{3,67},{35,99},{4,68}... | collective-permute-start | bytes 1474568 | tf_op jit(solution)/shard_map/ppermute | solution.py:588
  50.1 10.2 %collective-permute-done.5 = bf16[320,768]{1,0:T(8,128)(2,1)S(1)} collective-permute-done((bf16[320,768]{1,0:T(8,128)(2,1)}, bf16[320,768]{1,0:T(8,128)(2,1)S(1)}, u32[]{:S(2)}, u32[]{:S(2)}) %collective-permute-start.5) | collective-permute-done | bytes 491552 | tf_op jit(solution)/shard_map/ppermute | solution.py:588
  61.2 14.0 %attend.3 = (bf16[320,2304]{1,0:T(8,128)(2,1)}, bf16[12,320,160]{2,1,0:T(8,128)(2,1)}, bf16[320,768]{1,0:T(8,128)(2,1)}, f32[320,768]{1,0:T(8,128)}, f32[320,1]{1,0:T(8,128)}, /*index=5*/bf16[320,768]{1,0:T(8,128)(2,1)}) custom-call(bf16[320,768]{1,0:T(8,128)(2,1)} %broadcast_select_fusion.12.h, s32[1]{0:T(128)} %bitcast.2.half, s32[2]{0:T(128)} %fusion.9.lens, ...), custom_call_target="tpu_custom_call" | custom-call | flops 1509949440 | bytes 8000000 | tf_op jit(solution)/shard_map/attend/pallas_call | solution.py:314
  75.2 18.6 %feed.3 = (bf16[320,3072]{1,0:T(8,128)(2,1)}, bf16[320,3072]{1,0:T(8,128)(2,1)}, f32[320,768]{1,0:T(8,128)}, f32[320,1]{1,0:T(8,128)}, bf16[320,768]{1,0:T(8,128)(2,1)}) custom-call(bf16[320,768]{1,0:T(8,128)(2,1)} %get-tuple-element.38.u, s32[1]{0:T(128)} %bitcast.2.half, f32[2,4608]{1,0:T(2,128)} %fusion.6.smalls, bf16[384,3072]{1,0:T(8,128)(2,1)} %uo.7, ...), custom_call_target="tpu_custom_call" | custom-call | flops 3019898880 | bytes 14000000 | tf_op jit(solution)/shard_map/feed/pallas_call | solution.py:346
  93.8 17.2 %feed_back.2 = (bf16[320,768]{1,0:T(8,128)(2,1)}, bf16[320,3072]{1,0:T(8,128)(2,1)}, f32[320,768]{1,0:T(8,128)}, bf16[320,768]{1,0:T(8,128)(2,1)}, f32[2,4608]{1,0:T(2,128)}) custom-call(bf16[320,768]{1,0:T(8,128)(2,1)} %bitcast.24, s32[1]{0:T(128)} %bitcast.2.half, f32[2,4608]{1,0:T(2,128)} %fusion.6.smalls, bf16[384,3072]{1,0:T(8,128)(2,1)} %uo.7, ...), custom_call_target="tpu_custom_call" | custom-call | flops 3019898880 | bytes 18000000 | tf_op jit(solution)/shard_map/feed_back/pallas_call | solution.py:375
  111.0 15.0 %attend_back.2 = (bf16[320,2304]{1,0:T(8,128)(2,1)}, bf16[320,768]{1,0:T(8,128)(2,1)}, f32[2,768]{1,0:T(2,128)}, f32[1,768]{1,0:T(1,128)}) custom-call(bf16[320,768]{1,0:T(8,128)(2,1)} %get-tuple-element.45.gb, f32[320,768]{1,0:T(8,128)} %get-tuple-element.46.gr1, s32[1]{0:T(128)} %bitcast.2.half, s32[2,2]{1,0:T(2,128)} %copy-done.14, s32[1]{0:T(128)} %bitcast.6.first, ...), custom_call_target="tpu_custom_call" | custom-call | flops 1509949440 | bytes 12000000 | tf_op jit(solution)/shard_map/attend_back/pallas_call | solution.py:418
  127.7 13.2 %collective-permute-done.6 = bf16[320,768]{1,0:T(8,128)(2,1)S(1)} collective-permute-done((bf16[320,768]{1,0:T(8,128)(2,1)}, bf16[320,768]{1,0:T(8,128)(2,1)S(1)}, u32[]{:S(2)}, u32[]{:S(2)}) %collective-permute-start.6) | collective-permute-done | bytes 491552 | tf_op jit(solution)/shard_map/ppermute | solution.py:601
  141.8 17.2 %feed_back.3 = (bf16[320,768]{1,0:T(8,128)(2,1)}, bf16[320,3072]{1,0:T(8,128)(2,1)}, f32[320,768]{1,0:T(8,128)}, bf16[320,768]{1,0:T(8,128)(2,1)}, f32[2,4608]{1,0:T(2,128)}) custom-call(bf16[320,768]{1,0:T(8,128)(2,1)} %broadcast_select_fusion.11.gy, s32[1]{0:T(128)} %bitcast.2.half, f32[2,4608]{1,0:T(2,128)} %fusion.6.smalls, bf16[384,3072]{1,0:T(8,128)(2,1)} %uo.7, ...), custom_call_target="tpu_custom_call" | custom-call | flops 3019898880 | bytes 18000000 | tf_op jit(solution)/shard_map/feed_back/pallas_call | solution.py:375
  159.1 15.0 %attend_back.3 = (bf16[320,2304]{1,0:T(8,128)(2,1)}, bf16[320,768]{1,0:T(8,128)(2,1)}, f32[2,768]{1,0:T(2,128)}, f32[1,768]{1,0:T(1,128)}) custom-call(bf16[320,768]{1,0:T(8,128)(2,1)} %get-tuple-element.50.gb, f32[320,768]{1,0:T(8,128)} %get-tuple-element.51.gr1, s32[1]{0:T(128)} %bitcast.2.half, s32[2,2]{1,0:T(2,128)} %copy-done.14, s32[1]{0:T(128)} %bitcast.6.first, ...), custom_call_target="tpu_custom_call" | custom-call | flops 1509949440 | bytes 12000000 | tf_op jit(solution)/shard_map/attend_back/pallas_call | solution.py:418
  176.2 3.4 convolution_convert_fusion
  183.0 2.9 convolution_convert_fusion.1
  185.9 1.6 constant_dynamic-slice_fusion.4
  187.5 1.6 copy-done.6
  189.3 2.9 convolution_convert_fusion.2
  192.3 1.7 constant_dynamic-slice_fusion.9
  196.0 1.6 fusion
  197.6 4.0 %collective-permute-start.14 = (bf16[384,768]{1,0:T(8,128)(2,1)}, bf16[384,768]{1,0:T(8,128)(2,1)}, u32[]{:S(2)}, u32[]{:S(2)}) collective-permute-start(bf16[384,768]{1,0:T(8,128)(2,1)} %fusion), channel_id=1, source_target_pairs={{0,24},{1,25},{2,26},{3,27},{4,28},{5,29},{6,30},{7,31},{8,16},{9,... | collective-permute-start | bytes 1769480 | tf_op jit(solution)/shard_map/ppermute | solution.py:476
  203.8 6.0 %collective-permute-done.14 = bf16[384,768]{1,0:T(8,128)(2,1)} collective-permute-done((bf16[384,768]{1,0:T(8,128)(2,1)}, bf16[384,768]{1,0:T(8,128)(2,1)}, u32[]{:S(2)}, u32[]{:S(2)}) %collective-permute-start.14) | collective-permute-done | bytes 589856 | tf_op jit(solution)/shard_map/ppermute | solution.py:476
  209.8 1.8 add_convert_fusion.7
  211.9 3.3 add_convert_fusion
  216.7 3.2 collective-permute-start.35
  221.0 2.8 collective-permute-start.16
  223.9 15.4 %collective-permute-done.11 = bf16[208,768]{1,0:T(8,128)(2,1)S(1)} collective-permute-done((bf16[208,768]{1,0:T(8,128)(2,1)S(1)}, bf16[208,768]{1,0:T(8,128)(2,1)S(1)}, u32[]{:S(2)}, u32[]{:S(2)}) %collective-permute-start.11) | collective-permute-done | bytes 319520 | tf_op jit(solution)/shard_map/ppermute | solution.py:476
  239.4 1.6 collective-permute-start.12
  241.7 3.2 collective-permute-done.12
  245.0 2.8 collective-permute-start.13
  247.9 3.0 collective-permute-done.13
  251.0 3.0 collective-permute-start.18
  254.0 2.4 add_convert_fusion.1
  257.5 1.4 collective-permute-start.30
  261.5 2.8 collective-permute-start.21
  264.9 2.2 collective-permute-done.21
  267.1 2.4 collective-permute-done.25
  269.5 1.9 add_convert_fusion.3
  271.8 3.0 collective-permute-done.30
  274.8 1.6 add_convert_fusion.4
  276.4 3.3 collective-permute-start.31
  279.7 2.8 collective-permute-start.26
  283.2 2.4 collective-permute-start.37
  285.6 5.1 %collective-permute-done.31 = bf16[384,768]{1,0:T(8,128)(2,1)S(1)} collective-permute-done((bf16[384,768]{1,0:T(8,128)(2,1)S(1)}, bf16[384,768]{1,0:T(8,128)(2,1)S(1)}, u32[]{:S(2)}, u32[]{:S(2)}) %collective-permute-start.31) | collective-permute-done | bytes 589856 | tf_op jit(solution)/shard_map/ppermute | solution.py:476
  291.4 1.8 collective-permute-start.38
  293.2 4.5 %collective-permute-done.32 = bf16[192,768]{1,0:T(8,128)(2,1)S(1)} collective-permute-done((bf16[192,768]{1,0:T(8,128)(2,1)S(1)}, bf16[192,768]{1,0:T(8,128)(2,1)S(1)}, u32[]{:S(2)}, u32[]{:S(2)}) %collective-permute-start.32) | collective-permute-done | bytes 294944 | tf_op jit(solution)/shard_map/ppermute | solution.py:476
  297.8 2.8 collective-permute-start.33
  300.7 3.5 collective-permute-done.33
  305.9 6.8 %collective-permute-done.39 = bf16[192,768]{1,0:T(8,128)(2,1)S(1)} collective-permute-done((bf16[192,768]{1,0:T(8,128)(2,1)S(1)}, bf16[192,768]{1,0:T(8,128)(2,1)S(1)}, u32[]{:S(2)}, u32[]{:S(2)}) %collective-permute-start.39) | collective-permute-done | bytes 294944 | tf_op jit(solution)/shard_map/ppermute | solution.py:476
  312.8 2.8 collective-permute-start.44
  315.7 3.3 collective-permute-start.23
  319.0 1.8 collective-permute-done.44
  320.8 1.5 collective-permute-done.40
  323.9 3.0 collective-permute-start.28
  327.0 6.6 %collective-permute-done.41 = bf16[192,768]{1,0:T(8,128)(2,1)S(1)} collective-permute-done((bf16[192,768]{1,0:T(8,128)(2,1)S(1)}, bf16[192,768]{1,0:T(8,128)(2,1)S(1)}, u32[]{:S(2)}, u32[]{:S(2)}) %collective-permute-start.41) | collective-permute-done | bytes 294944 | tf_op jit(solution)/shard_map/ppermute | solution.py:476
  334.4 1.7 collective-permute-start.24
  336.3 1.6 collective-permute-start.46
  337.9 5.9 %collective-permute-done.42 = bf16[384,768]{1,0:T(8,128)(2,1)S(1)} collective-permute-done((bf16[384,768]{1,0:T(8,128)(2,1)S(1)}, bf16[384,768]{1,0:T(8,128)(2,1)S(1)}, u32[]{:S(2)}, u32[]{:S(2)}) %collective-permute-start.42) | collective-permute-done | bytes 589856 | tf_op jit(solution)/shard_map/ppermute | solution.py:476
  344.1 1.6 collective-permute-start.43
  345.6 4.5 %collective-permute-done.24 = bf16[384,768]{1,0:T(8,128)(2,1)S(1)} collective-permute-done((bf16[384,768]{1,0:T(8,128)(2,1)S(1)}, bf16[384,768]{1,0:T(8,128)(2,1)S(1)}, u32[]{:S(2)}, u32[]{:S(2)}) %collective-permute-start.24) | collective-permute-done | bytes 589856 | tf_op jit(solution)/shard_map/ppermute | solution.py:476
  352.3 2.0 maximum_convert_fusion.2
  354.3 7.3 %collective-permute-done.43 = bf16[768,768]{1,0:T(8,128)(2,1)S(1)} collective-permute-done((bf16[768,768]{1,0:T(8,128)(2,1)S(1)}, bf16[768,768]{1,0:T(8,128)(2,1)S(1)}, u32[]{:S(2)}, u32[]{:S(2)}) %collective-permute-start.43) | collective-permute-done | bytes 1179680 | tf_op jit(solution)/shard_map/ppermute | solution.py:476
  362.2 5.7 %collective-permute-done.47 = bf16[768,768]{1,0:T(8,128)(2,1)S(1)} collective-permute-done((bf16[768,768]{1,0:T(8,128)(2,1)S(1)}, bf16[768,768]{1,0:T(8,128)(2,1)S(1)}, u32[]{:S(2)}, u32[]{:S(2)}) %collective-permute-start.47) | collective-permute-done | bytes 1179680 | tf_op jit(solution)/shard_map/ppermute | solution.py:476
  368.4 2.5 maximum_convert_fusion.1
  370.9 2.8 maximum_convert_fusion
  (219 shorter events, 44.2 us)
Async XLA Ops:
  0.6 9.1 %copy-start = (bf16[2,2,160,768]{3,2,1,0:T(8,128)(2,1)S(1)}, bf16[2,2,160,768]{3,2,1,0:T(8,128)(2,1)}, u32[]{:S(2)}) copy-start(bf16[2,2,160,768]{3,2,1,0:T(8,128)(2,1)} %param.17) | copy-start | bytes 2949124
  0.7 11.5 %copy-start.19 = (s32[2,2]{1,0:T(2,128)S(1)}, s32[2,2]{1,0:T(2,128)}, u32[]{:S(2)}) copy-start(s32[2,2]{1,0:T(2,128)} %param.19) | copy-start | bytes 52
  0.7 27.5 %collective-permute-start.3 = (bf16[384,3072]{1,0:T(8,128)(2,1)}, bf16[384,3072]{1,0:T(8,128)(2,1)}, u32[]{:S(2)}, u32[]{:S(2)}) collective-permute-start(bf16[384,3072]{1,0:T(8,128)(2,1)} %uo.7), channel_id=1, source_target_pairs={{0,32},{32,0},{64,96},{96,64},{1,33},{33,1},{65,97},{97,65},{2,34}... | collective-permute-start | bytes 7077896 | tf_op jit(solution)/shard_map/ppermute | solution.py:430
  0.8 27.4 %collective-permute-start.4 = (bf16[1536,768]{1,0:T(8,128)(2,1)}, bf16[1536,768]{1,0:T(8,128)(2,1)}, u32[]{:S(2)}, u32[]{:S(2)}) collective-permute-start(bf16[1536,768]{1,0:T(8,128)(2,1)} %do.7), channel_id=1, source_target_pairs={{0,32},{32,0},{64,96},{96,64},{1,33},{33,1},{65,97},{97,65},{2,34}... | collective-permute-start | bytes 7077896 | tf_op jit(solution)/shard_map/ppermute | solution.py:430
  1.3 12.2 %collective-permute-start.1 = (bf16[384,2304]{1,0:T(8,128)(2,1)}, bf16[384,2304]{1,0:T(8,128)(2,1)S(1)}, u32[]{:S(2)}, u32[]{:S(2)}) collective-permute-start(bf16[384,2304]{1,0:T(8,128)(2,1)} %qo.7), channel_id=1, source_target_pairs={{0,32},{32,0},{64,96},{96,64},{1,33},{33,1},{65,97},{97,65},{2,34}... | collective-permute-start | bytes 5308424 | tf_op jit(solution)/shard_map/ppermute | solution.py:430
  8.2 4.5 %collective-permute-start = (bf16[4608]{0:T(1024)(128)(2,1)S(1)}, bf16[4608]{0:T(1024)(128)(2,1)S(1)}, u32[]{:S(2)}, u32[]{:S(2)}) collective-permute-start(bf16[4608]{0:T(1024)(128)(2,1)S(1)} %dynamic-update-slice.7), channel_id=1, source_target_pairs={{0,32},{32,0},{64,96},{96,64},{1,33},{33,1},{65,97},{97,65},{2,34}... | collective-permute-start | bytes 27656 | tf_op jit(solution)/shard_map/ppermute | solution.py:430
  8.7 4.8 %collective-permute-start.2 = (bf16[384,768]{1,0:T(8,128)(2,1)}, bf16[384,768]{1,0:T(8,128)(2,1)S(1)}, u32[]{:S(2)}, u32[]{:S(2)}) collective-permute-start(bf16[384,768]{1,0:T(8,128)(2,1)} %oo.7), channel_id=1, source_target_pairs={{0,32},{32,0},{64,96},{96,64},{1,33},{33,1},{65,97},{97,65},{2,34}... | collective-permute-start | bytes 1769480 | tf_op jit(solution)/shard_map/ppermute | solution.py:430
  9.4 18.7 %copy-start.14 = (s32[2,2]{1,0:T(2,128)}, s32[2,2]{1,0:T(2,128)S(1)}, u32[]{:S(2)}) copy-start(s32[2,2]{1,0:T(2,128)S(1)} %fusion.8.spans) | copy-start | bytes 52
  28.2 21.1 %copy-start.12 = (bf16[2,2,160,768]{3,2,1,0:T(8,128)(2,1)S(1)}, bf16[2,2,160,768]{3,2,1,0:T(8,128)(2,1)}, u32[]{:S(2)}) copy-start(bf16[2,2,160,768]{3,2,1,0:T(8,128)(2,1)} %param.18) | copy-start | bytes 2949124
  28.2 32.1 %copy-start.8 = (bf16[1,2,160,768]{3,2,1,0:T(8,128)(2,1)S(1)}, bf16[1,2,160,768]{3,2,1,0:T(8,128)(2,1)}, u32[]{:S(2)}) copy-start(bf16[1,2,160,768]{3,2,1,0:T(8,128)(2,1)} %copy-done.7) | copy-start | bytes 1474564
  28.2 32.1 %copy-start.16 = (bf16[768]{0:T(1024)(128)(2,1)S(1)}, bf16[768]{0:T(1024)(128)(2,1)}, u32[]{:S(2)}) copy-start(bf16[768]{0:T(1024)(128)(2,1)} %param.21) | copy-start | bytes 4612
  45.3 14.9 %collective-permute-start.5 = (bf16[320,768]{1,0:T(8,128)(2,1)}, bf16[320,768]{1,0:T(8,128)(2,1)S(1)}, u32[]{:S(2)}, u32[]{:S(2)}) collective-permute-start(bf16[320,768]{1,0:T(8,128)(2,1)} %feed.2), channel_id=1, source_target_pairs={{0,64},{32,96},{1,65},{33,97},{2,66},{34,98},{3,67},{35,99},{4,68}... | collective-permute-start | bytes 1474568 | tf_op jit(solution)/shard_map/ppermute | solution.py:588
  111.0 30.0 %copy-start.9 = (bf16[1,2,160,768]{3,2,1,0:T(8,128)(2,1)S(1)}, bf16[1,2,160,768]{3,2,1,0:T(8,128)(2,1)}, u32[]{:S(2)}) copy-start(bf16[1,2,160,768]{3,2,1,0:T(8,128)(2,1)} %constant_dynamic-slice_fusion.18) | copy-start | bytes 1474564
  126.1 14.9 %collective-permute-start.6 = (bf16[320,768]{1,0:T(8,128)(2,1)}, bf16[320,768]{1,0:T(8,128)(2,1)S(1)}, u32[]{:S(2)}, u32[]{:S(2)}) collective-permute-start(bf16[320,768]{1,0:T(8,128)(2,1)} %get-tuple-element.49), channel_id=1, source_target_pairs={{64,0},{96,32},{65,1},{97,33},{66,2},{98,34},{67,3},{99,35},{68,4}... | collective-permute-start | bytes 1474568 | tf_op jit(solution)/shard_map/ppermute | solution.py:601
  159.1 15.8 %copy-start.13 = (f32[2,4608]{1,0:T(2,128)S(1)}, f32[2,4608]{1,0:T(2,128)}, u32[]{:S(2)}) copy-start(f32[2,4608]{1,0:T(2,128)} %get-tuple-element.56) | copy-start | bytes 110596
  159.1 17.2 %copy-start.10 = (bf16[320,768]{1,0:T(8,128)(2,1)S(1)}, bf16[320,768]{1,0:T(8,128)(2,1)}, u32[]{:S(2)}) copy-start(bf16[320,768]{1,0:T(8,128)(2,1)} %broadcast_select_fusion.12.h) | copy-start | bytes 1474564
  175.6 26.0 %collective-permute-start.9 = (bf16[4608]{0:T(1024)(128)(2,1)S(1)}, bf16[4608]{0:T(1024)(128)(2,1)S(1)}, u32[]{:S(2)}, u32[]{:S(2)}) collective-permute-start(bf16[4608]{0:T(1024)(128)(2,1)S(1)} %convert_reduce_fusion), channel_id=1, source_target_pairs={{0,32},{32,0},{64,96},{96,64},{1,33},{33,1},{65,97},{97,65},{2,34}... | collective-permute-start | bytes 27656 | tf_op jit(solution)/shard_map/ppermute | solution.py:430
  179.8 3.2 copy-start.17
  179.8 3.2 copy-start.21
  179.8 15.6 %collective-permute-start.8 = (bf16[384,2304]{1,0:T(8,128)(2,1)S(1)}, bf16[384,2304]{1,0:T(8,128)(2,1)S(1)}, u32[]{:S(2)}, u32[]{:S(2)}) collective-permute-start(bf16[384,2304]{1,0:T(8,128)(2,1)S(1)} %constant_dynamic-slice_fusion.16), channel_id=1, source_target_pairs={{0,32},{32,0},{64,96},{96,64},{1,33},{33,1},{65,97},{97,65},{2,34}... | collective-permute-start | bytes 5308424 | tf_op jit(solution)/shard_map/ppermute | solution.py:430
  182.5 19.2 %collective-permute-start.7 = (bf16[384,768]{1,0:T(8,128)(2,1)}, bf16[384,768]{1,0:T(8,128)(2,1)}, u32[]{:S(2)}, u32[]{:S(2)}) collective-permute-start(bf16[384,768]{1,0:T(8,128)(2,1)} %constant_dynamic-slice_fusion.17), channel_id=1, source_target_pairs={{0,32},{32,0},{64,96},{96,64},{1,33},{33,1},{65,97},{97,65},{2,34}... | collective-permute-start | bytes 1769480 | tf_op jit(solution)/shard_map/ppermute | solution.py:430
  185.9 3.2 copy-start.18
  185.9 3.5 copy-start.22
  189.1 22.9 %collective-permute-start.34 = (bf16[384,3072]{1,0:T(8,128)(2,1)}, bf16[384,3072]{1,0:T(8,128)(2,1)}, u32[]{:S(2)}, u32[]{:S(2)}) collective-permute-start(bf16[384,3072]{1,0:T(8,128)(2,1)} %constant_dynamic-slice_fusion.4), channel_id=1, source_target_pairs={{0,32},{32,0},{64,96},{96,64},{1,33},{33,1},{65,97},{97,65},{2,34}... | collective-permute-start | bytes 7077896 | tf_op jit(solution)/shard_map/ppermute | solution.py:430
  195.1 58.8 %collective-permute-start.29 = (bf16[1536,768]{1,0:T(8,128)(2,1)}, bf16[1536,768]{1,0:T(8,128)(2,1)}, u32[]{:S(2)}, u32[]{:S(2)}) collective-permute-start(bf16[1536,768]{1,0:T(8,128)(2,1)} %constant_dynamic-slice_fusion.9), channel_id=1, source_target_pairs={{0,32},{32,0},{64,96},{96,64},{1,33},{33,1},{65,97},{97,65},{2,34}... | collective-permute-start | bytes 7077896 | tf_op jit(solution)/shard_map/ppermute | solution.py:430
  197.6 12.2 %collective-permute-start.14 = (bf16[384,768]{1,0:T(8,128)(2,1)}, bf16[384,768]{1,0:T(8,128)(2,1)}, u32[]{:S(2)}, u32[]{:S(2)}) collective-permute-start(bf16[384,768]{1,0:T(8,128)(2,1)} %fusion), channel_id=1, source_target_pairs={{0,24},{1,25},{2,26},{3,27},{4,28},{5,29},{6,30},{7,31},{8,16},{9,... | collective-permute-start | bytes 1769480 | tf_op jit(solution)/shard_map/ppermute | solution.py:476
  203.7 16.2 %collective-permute-start.10 = (bf16[400,768]{1,0:T(8,128)(2,1)S(1)}, bf16[400,768]{1,0:T(8,128)(2,1)S(1)}, u32[]{:S(2)}, u32[]{:S(2)}) collective-permute-start(bf16[400,768]{1,0:T(8,128)(2,1)S(1)} %pad_maximum_fusion.3), channel_id=1, source_target_pairs={{0,8},{1,9},{2,10},{3,11},{4,12},{5,13},{6,14},{7,15},{8,0},{9,1},... | collective-permute-start | bytes 1843208 | tf_op jit(solution)/shard_map/ppermute | solution.py:476
  211.7 9.2 %collective-permute-start.15 = (bf16[192,768]{1,0:T(8,128)(2,1)S(1)}, bf16[192,768]{1,0:T(8,128)(2,1)S(1)}, u32[]{:S(2)}, u32[]{:S(2)}) collective-permute-start(bf16[192,768]{1,0:T(8,128)(2,1)S(1)} %constant_dynamic-slice_fusion.12), channel_id=1, source_target_pairs={{0,8},{1,9},{2,10},{3,11},{4,12},{5,13},{6,14},{7,15},{8,0},{9,1},... | collective-permute-start | bytes 884744 | tf_op jit(solution)/shard_map/ppermute | solution.py:476
  215.4 38.6 %slice-start = ((s8[4718592]{0:T(1024)(128)(4,1)}), s8[4194304]{0:T(1024)(128)(4,1)S(1)}, s32[]{:S(2)}) async-start(s8[4718592]{0:T(1024)(128)(4,1)} %bitcast.22), calls=%async_computation | async-start | bytes 8388608
  215.5 5.1 %copy-start.3 = (bf16[1536,768]{1,0:T(8,128)(2,1)}, bf16[1536,768]{1,0:T(8,128)(2,1)S(1)}, u32[]{:S(2)}) copy-start(bf16[1536,768]{1,0:T(8,128)(2,1)S(1)} %pad_maximum_fusion) | copy-start | bytes 7077892
  216.7 37.3 %slice-start.1 = ((s8[4718592]{0:T(1024)(128)(4,1)}), s8[524288]{0:T(1024)(128)(4,1)S(1)}, s32[]{:S(2)}) async-start(s8[4718592]{0:T(1024)(128)(4,1)} %bitcast.22), calls=%async_computation.1 | async-start | bytes 1048576
  216.7 52.8 %collective-permute-start.35 = (bf16[768,768]{1,0:T(8,128)(2,1)}, bf16[768,768]{1,0:T(8,128)(2,1)}, u32[]{:S(2)}, u32[]{:S(2)}) collective-permute-start(bf16[768,768]{1,0:T(8,128)(2,1)} %constant_dynamic-slice_fusion.3), channel_id=1, source_target_pairs={{0,24},{1,25},{2,26},{3,27},{4,28},{5,29},{6,30},{7,31},{8,16},{9,... | collective-permute-start | bytes 3538952 | tf_op jit(solution)/shard_map/ppermute | solution.py:476
  220.8 18.5 %collective-permute-start.11 = (bf16[208,768]{1,0:T(8,128)(2,1)S(1)}, bf16[208,768]{1,0:T(8,128)(2,1)S(1)}, u32[]{:S(2)}, u32[]{:S(2)}) collective-permute-start(bf16[208,768]{1,0:T(8,128)(2,1)S(1)} %pad_maximum_fusion.8), channel_id=1, source_target_pairs={{0,24},{1,25},{2,26},{3,27},{4,28},{5,29},{6,30},{7,31},{8,16},{9,... | collective-permute-start | bytes 958472 | tf_op jit(solution)/shard_map/ppermute | solution.py:476
  221.0 20.0 %collective-permute-start.16 = (bf16[96,768]{1,0:T(8,128)(2,1)S(1)}, bf16[96,768]{1,0:T(8,128)(2,1)S(1)}, u32[]{:S(2)}, u32[]{:S(2)}) collective-permute-start(bf16[96,768]{1,0:T(8,128)(2,1)S(1)} %constant_dynamic-slice_fusion.11), channel_id=1, source_target_pairs={{0,6},{1,7},{2,4},{3,5},{4,2},{5,3},{6,0},{7,1},{8,14},{9,15},{10,... | collective-permute-start | bytes 442376 | tf_op jit(solution)/shard_map/ppermute | solution.py:476
  239.4 5.5 %collective-permute-start.12 = (bf16[112,768]{1,0:T(8,128)(2,1)S(1)}, bf16[112,768]{1,0:T(8,128)(2,1)S(1)}, u32[]{:S(2)}, u32[]{:S(2)}) collective-permute-start(bf16[112,768]{1,0:T(8,128)(2,1)S(1)} %pad_maximum_fusion.14), channel_id=1, source_target_pairs={{0,2},{1,3},{2,0},{3,1},{4,6},{5,7},{6,4},{7,5},{8,10},{9,11},{10,... | collective-permute-start | bytes 516104 | tf_op jit(solution)/shard_map/ppermute | solution.py:476
  241.1 6.8 %collective-permute-start.17 = (bf16[48,768]{1,0:T(8,128)(2,1)S(1)}, bf16[48,768]{1,0:T(8,128)(2,1)S(1)}, u32[]{:S(2)}, u32[]{:S(2)}) collective-permute-start(bf16[48,768]{1,0:T(8,128)(2,1)S(1)} %constant_dynamic-slice_fusion.10), channel_id=1, source_target_pairs={{0,2},{1,3},{2,0},{3,1},{4,6},{5,7},{6,4},{7,5},{8,10},{9,11},{10,... | collective-permute-start | bytes 221192 | tf_op jit(solution)/shard_map/ppermute | solution.py:476
  245.0 5.9 %collective-permute-start.13 = (bf16[64,768]{1,0:T(8,128)(2,1)S(1)}, bf16[64,768]{1,0:T(8,128)(2,1)S(1)}, u32[]{:S(2)}, u32[]{:S(2)}) collective-permute-start(bf16[64,768]{1,0:T(8,128)(2,1)S(1)} %pad_maximum_fusion.18), channel_id=1, source_target_pairs={{0,6},{1,7},{2,4},{3,5},{4,2},{5,3},{6,0},{7,1},{8,14},{9,15},{10,... | collective-permute-start | bytes 294920 | tf_op jit(solution)/shard_map/ppermute | solution.py:476
  251.0 7.9 %collective-permute-start.18 = (bf16[112,768]{1,0:T(8,128)(2,1)S(1)}, bf16[112,768]{1,0:T(8,128)(2,1)S(1)}, u32[]{:S(2)}, u32[]{:S(2)}) collective-permute-start(bf16[112,768]{1,0:T(8,128)(2,1)S(1)} %pad_maximum_fusion.15), channel_id=1, source_target_pairs={{0,1},{1,0},{2,3},{3,2},{4,5},{5,4},{6,7},{7,6},{8,9},{9,8},{10,11... | collective-permute-start | bytes 516104 | tf_op jit(solution)/shard_map/ppermute | solution.py:476
  257.5 17.3 %collective-permute-start.30 = (bf16[768,768]{1,0:T(8,128)(2,1)}, bf16[768,768]{1,0:T(8,128)(2,1)}, u32[]{:S(2)}, u32[]{:S(2)}) collective-permute-start(bf16[768,768]{1,0:T(8,128)(2,1)} %constant_dynamic-slice_fusion.8), channel_id=1, source_target_pairs={{0,8},{1,9},{2,10},{3,11},{4,12},{5,13},{6,14},{7,15},{8,0},{9,1},... | collective-permute-start | bytes 3538952 | tf_op jit(solution)/shard_map/ppermute | solution.py:476
  258.9 1.2 collective-permute-start.19
  260.2 4.1 %collective-permute-start.20 = (bf16[1,768]{1,0:T(2,128)(2,1)S(1)}, bf16[1,768]{1,0:T(2,128)(2,1)S(1)}, u32[]{:S(2)}, u32[]{:S(2)}) collective-permute-start(bf16[1,768]{1,0:T(2,128)(2,1)S(1)} %add_convert_fusion.27), channel_id=1, source_target_pairs={{0,64},{32,96},{64,0},{96,32},{1,65},{33,97},{65,1},{97,33},{2,66}... | collective-permute-start | bytes 4616 | tf_op jit(solution)/shard_map/ppermute | solution.py:430
  261.5 5.6 %collective-permute-start.21 = (bf16[48,768]{1,0:T(8,128)(2,1)S(1)}, bf16[48,768]{1,0:T(8,128)(2,1)S(1)}, u32[]{:S(2)}, u32[]{:S(2)}) collective-permute-start(bf16[48,768]{1,0:T(8,128)(2,1)S(1)} %get-tuple-element.112), channel_id=1, source_target_pairs={{0,6},{1,7},{2,4},{3,5},{4,2},{5,3},{6,0},{7,1},{8,14},{9,15},{10,... | collective-permute-start | bytes 221192 | tf_op jit(solution)/shard_map/ppermute | solution.py:476
  264.2 5.2 %collective-permute-start.25 = (bf16[48,768]{1,0:T(8,128)(2,1)S(1)}, bf16[48,768]{1,0:T(8,128)(2,1)S(1)}, u32[]{:S(2)}, u32[]{:S(2)}) collective-permute-start(bf16[48,768]{1,0:T(8,128)(2,1)S(1)} %get-tuple-element.113), channel_id=1, source_target_pairs={{0,2},{1,3},{2,0},{3,1},{4,6},{5,7},{6,4},{7,5},{8,10},{9,11},{10,... | collective-permute-start | bytes 221192 | tf_op jit(solution)/shard_map/ppermute | solution.py:476
  271.5 11.5 %collective-permute-start.36 = (bf16[384,768]{1,0:T(8,128)(2,1)S(1)}, bf16[384,768]{1,0:T(8,128)(2,1)S(1)}, u32[]{:S(2)}, u32[]{:S(2)}) collective-permute-start(bf16[384,768]{1,0:T(8,128)(2,1)S(1)} %constant_dynamic-slice_fusion.2), channel_id=1, source_target_pairs={{0,8},{1,9},{2,10},{3,11},{4,12},{5,13},{6,14},{7,15},{8,0},{9,1},... | collective-permute-start | bytes 1769480 | tf_op jit(solution)/shard_map/ppermute | solution.py:476
  276.4 14.3 %collective-permute-start.31 = (bf16[384,768]{1,0:T(8,128)(2,1)S(1)}, bf16[384,768]{1,0:T(8,128)(2,1)S(1)}, u32[]{:S(2)}, u32[]{:S(2)}) collective-permute-start(bf16[384,768]{1,0:T(8,128)(2,1)S(1)} %constant_dynamic-slice_fusion.7), channel_id=1, source_target_pairs={{0,24},{1,25},{2,26},{3,27},{4,28},{5,29},{6,30},{7,31},{8,16},{9,... | collective-permute-start | bytes 1769480 | tf_op jit(solution)/shard_map/ppermute | solution.py:476
  279.7 26.0 %collective-permute-start.26 = (bf16[96,768]{1,0:T(8,128)(2,1)S(1)}, bf16[96,768]{1,0:T(8,128)(2,1)S(1)}, u32[]{:S(2)}, u32[]{:S(2)}) collective-permute-start(bf16[96,768]{1,0:T(8,128)(2,1)S(1)} %pad_maximum_fusion.17), channel_id=1, source_target_pairs={{0,6},{1,7},{2,4},{3,5},{4,2},{5,3},{6,0},{7,1},{8,14},{9,15},{10,... | collective-permute-start | bytes 442376 | tf_op jit(solution)/shard_map/ppermute | solution.py:476
  282.6 33.0 %collective-permute-start.22 = (bf16[96,768]{1,0:T(8,128)(2,1)S(1)}, bf16[96,768]{1,0:T(8,128)(2,1)S(1)}, u32[]{:S(2)}, u32[]{:S(2)}) collective-permute-start(bf16[96,768]{1,0:T(8,128)(2,1)S(1)} %pad_maximum_fusion.16), channel_id=1, source_target_pairs={{0,2},{1,3},{2,0},{3,1},{4,6},{5,7},{6,4},{7,5},{8,10},{9,11},{10,... | collective-permute-start | bytes 442376 | tf_op jit(solution)/shard_map/ppermute | solution.py:476
  283.2 8.1 %collective-permute-start.37 = (bf16[192,768]{1,0:T(8,128)(2,1)S(1)}, bf16[192,768]{1,0:T(8,128)(2,1)S(1)}, u32[]{:S(2)}, u32[]{:S(2)}) collective-permute-start(bf16[192,768]{1,0:T(8,128)(2,1)S(1)} %constant_dynamic-slice_fusion.1), channel_id=1, source_target_pairs={{0,6},{1,7},{2,4},{3,5},{4,2},{5,3},{6,0},{7,1},{8,14},{9,15},{10,... | collective-permute-start | bytes 884744 | tf_op jit(solution)/shard_map/ppermute | solution.py:476
  290.9 6.8 %collective-permute-start.32 = (bf16[192,768]{1,0:T(8,128)(2,1)S(1)}, bf16[192,768]{1,0:T(8,128)(2,1)S(1)}, u32[]{:S(2)}, u32[]{:S(2)}) collective-permute-start(bf16[192,768]{1,0:T(8,128)(2,1)S(1)} %constant_dynamic-slice_fusion.6), channel_id=1, source_target_pairs={{0,2},{1,3},{2,0},{3,1},{4,6},{5,7},{6,4},{7,5},{8,10},{9,11},{10,... | collective-permute-start | bytes 884744 | tf_op jit(solution)/shard_map/ppermute | solution.py:476
  291.4 9.3 %collective-permute-start.38 = (bf16[96,768]{1,0:T(8,128)(2,1)S(1)}, bf16[96,768]{1,0:T(8,128)(2,1)S(1)}, u32[]{:S(2)}, u32[]{:S(2)}) collective-permute-start(bf16[96,768]{1,0:T(8,128)(2,1)S(1)} %constant_dynamic-slice_fusion), channel_id=1, source_target_pairs={{0,2},{1,3},{2,0},{3,1},{4,6},{5,7},{6,4},{7,5},{8,10},{9,11},{10,... | collective-permute-start | bytes 442376 | tf_op jit(solution)/shard_map/ppermute | solution.py:476
  297.8 6.4 %collective-permute-start.33 = (bf16[96,768]{1,0:T(8,128)(2,1)S(1)}, bf16[96,768]{1,0:T(8,128)(2,1)S(1)}, u32[]{:S(2)}, u32[]{:S(2)}) collective-permute-start(bf16[96,768]{1,0:T(8,128)(2,1)S(1)} %constant_dynamic-slice_fusion.5), channel_id=1, source_target_pairs={{0,6},{1,7},{2,4},{3,5},{4,2},{5,3},{6,0},{7,1},{8,14},{9,15},{10,... | collective-permute-start | bytes 442376 | tf_op jit(solution)/shard_map/ppermute | solution.py:476
  304.4 8.3 %collective-permute-start.39 = (bf16[192,768]{1,0:T(8,128)(2,1)S(1)}, bf16[192,768]{1,0:T(8,128)(2,1)S(1)}, u32[]{:S(2)}, u32[]{:S(2)}) collective-permute-start(bf16[192,768]{1,0:T(8,128)(2,1)S(1)} %pad_maximum_fusion.11), channel_id=1, source_target_pairs={{0,1},{1,0},{2,3},{3,2},{4,5},{5,4},{6,7},{7,6},{8,9},{9,8},{10,11... | collective-permute-start | bytes 884744 | tf_op jit(solution)/shard_map/ppermute | solution.py:476
  305.8 17.9 %collective-permute-start.27 = (bf16[192,768]{1,0:T(8,128)(2,1)S(1)}, bf16[192,768]{1,0:T(8,128)(2,1)S(1)}, u32[]{:S(2)}, u32[]{:S(2)}) collective-permute-start(bf16[192,768]{1,0:T(8,128)(2,1)S(1)} %pad_maximum_fusion.10), channel_id=1, source_target_pairs={{0,8},{1,9},{2,10},{3,11},{4,12},{5,13},{6,14},{7,15},{8,0},{9,1},... | collective-permute-start | bytes 884744 | tf_op jit(solution)/shard_map/ppermute | solution.py:476
  312.8 8.1 %collective-permute-start.44 = (bf16[96,768]{1,0:T(8,128)(2,1)S(1)}, bf16[96,768]{1,0:T(8,128)(2,1)S(1)}, u32[]{:S(2)}, u32[]{:S(2)}) collective-permute-start(bf16[96,768]{1,0:T(8,128)(2,1)S(1)} %get-tuple-element.100), channel_id=1, source_target_pairs={{0,6},{1,7},{2,4},{3,5},{4,2},{5,3},{6,0},{7,1},{8,14},{9,15},{10,... | collective-permute-start | bytes 442376 | tf_op jit(solution)/shard_map/ppermute | solution.py:476
  315.6 6.7 %collective-permute-start.40 = (bf16[96,768]{1,0:T(8,128)(2,1)S(1)}, bf16[96,768]{1,0:T(8,128)(2,1)S(1)}, u32[]{:S(2)}, u32[]{:S(2)}) collective-permute-start(bf16[96,768]{1,0:T(8,128)(2,1)S(1)} %get-tuple-element.101), channel_id=1, source_target_pairs={{0,2},{1,3},{2,0},{3,1},{4,6},{5,7},{6,4},{7,5},{8,10},{9,11},{10,... | collective-permute-start | bytes 442376 | tf_op jit(solution)/shard_map/ppermute | solution.py:476
  315.7 18.6 %collective-permute-start.23 = (bf16[192,768]{1,0:T(8,128)(2,1)S(1)}, bf16[192,768]{1,0:T(8,128)(2,1)S(1)}, u32[]{:S(2)}, u32[]{:S(2)}) collective-permute-start(bf16[192,768]{1,0:T(8,128)(2,1)S(1)} %pad_maximum_fusion.9), channel_id=1, source_target_pairs={{0,24},{1,25},{2,26},{3,27},{4,28},{5,29},{6,30},{7,31},{8,16},{9,... | collective-permute-start | bytes 884744 | tf_op jit(solution)/shard_map/ppermute | solution.py:476
  322.4 11.2 %collective-permute-start.41 = (bf16[192,768]{1,0:T(8,128)(2,1)S(1)}, bf16[192,768]{1,0:T(8,128)(2,1)S(1)}, u32[]{:S(2)}, u32[]{:S(2)}) collective-permute-start(bf16[192,768]{1,0:T(8,128)(2,1)S(1)} %pad_maximum_fusion.12), channel_id=1, source_target_pairs={{0,6},{1,7},{2,4},{3,5},{4,2},{5,3},{6,0},{7,1},{8,14},{9,15},{10,... | collective-permute-start | bytes 884744 | tf_op jit(solution)/shard_map/ppermute | solution.py:476
  323.9 28.1 %collective-permute-start.28 = (bf16[384,768]{1,0:T(8,128)(2,1)S(1)}, bf16[384,768]{1,0:T(8,128)(2,1)S(1)}, u32[]{:S(2)}, u32[]{:S(2)}) collective-permute-start(bf16[384,768]{1,0:T(8,128)(2,1)S(1)} %pad_maximum_fusion.5), channel_id=1, source_target_pairs={{0,24},{1,25},{2,26},{3,27},{4,28},{5,29},{6,30},{7,31},{8,16},{9,... | collective-permute-start | bytes 1769480 | tf_op jit(solution)/shard_map/ppermute | solution.py:476
  326.9 9.2 %collective-permute-start.45 = (bf16[192,768]{1,0:T(8,128)(2,1)S(1)}, bf16[192,768]{1,0:T(8,128)(2,1)S(1)}, u32[]{:S(2)}, u32[]{:S(2)}) collective-permute-start(bf16[192,768]{1,0:T(8,128)(2,1)S(1)} %pad_maximum_fusion.13), channel_id=1, source_target_pairs={{0,2},{1,3},{2,0},{3,1},{4,6},{5,7},{6,4},{7,5},{8,10},{9,11},{10,... | collective-permute-start | bytes 884744 | tf_op jit(solution)/shard_map/ppermute | solution.py:476
  333.8 10.0 %collective-permute-start.42 = (bf16[384,768]{1,0:T(8,128)(2,1)S(1)}, bf16[384,768]{1,0:T(8,128)(2,1)S(1)}, u32[]{:S(2)}, u32[]{:S(2)}) collective-permute-start(bf16[384,768]{1,0:T(8,128)(2,1)S(1)} %pad_maximum_fusion.6), channel_id=1, source_target_pairs={{0,8},{1,9},{2,10},{3,11},{4,12},{5,13},{6,14},{7,15},{8,0},{9,1},... | collective-permute-start | bytes 1769480 | tf_op jit(solution)/shard_map/ppermute | solution.py:476
  334.4 15.7 %collective-permute-start.24 = (bf16[384,768]{1,0:T(8,128)(2,1)S(1)}, bf16[384,768]{1,0:T(8,128)(2,1)S(1)}, u32[]{:S(2)}, u32[]{:S(2)}) collective-permute-start(bf16[384,768]{1,0:T(8,128)(2,1)S(1)} %pad_maximum_fusion.4), channel_id=1, source_target_pairs={{0,8},{1,9},{2,10},{3,11},{4,12},{5,13},{6,14},{7,15},{8,0},{9,1},... | collective-permute-start | bytes 1769480 | tf_op jit(solution)/shard_map/ppermute | solution.py:476
  336.3 15.0 %collective-permute-start.46 = (bf16[384,768]{1,0:T(8,128)(2,1)S(1)}, bf16[384,768]{1,0:T(8,128)(2,1)S(1)}, u32[]{:S(2)}, u32[]{:S(2)}) collective-permute-start(bf16[384,768]{1,0:T(8,128)(2,1)S(1)} %pad_maximum_fusion.7), channel_id=1, source_target_pairs={{0,24},{1,25},{2,26},{3,27},{4,28},{5,29},{6,30},{7,31},{8,16},{9,... | collective-permute-start | bytes 1769480 | tf_op jit(solution)/shard_map/ppermute | solution.py:476
  344.1 17.5 %collective-permute-start.43 = (bf16[768,768]{1,0:T(8,128)(2,1)S(1)}, bf16[768,768]{1,0:T(8,128)(2,1)S(1)}, u32[]{:S(2)}, u32[]{:S(2)}) collective-permute-start(bf16[768,768]{1,0:T(8,128)(2,1)S(1)} %pad_maximum_fusion.1), channel_id=1, source_target_pairs={{0,24},{1,25},{2,26},{3,27},{4,28},{5,29},{6,30},{7,31},{8,16},{9,... | collective-permute-start | bytes 3538952 | tf_op jit(solution)/shard_map/ppermute | solution.py:476
  351.6 16.3 %collective-permute-start.47 = (bf16[768,768]{1,0:T(8,128)(2,1)S(1)}, bf16[768,768]{1,0:T(8,128)(2,1)S(1)}, u32[]{:S(2)}, u32[]{:S(2)}) collective-permute-start(bf16[768,768]{1,0:T(8,128)(2,1)S(1)} %pad_maximum_fusion.2), channel_id=1, source_target_pairs={{0,8},{1,9},{2,10},{3,11},{4,12},{5,13},{6,14},{7,15},{8,0},{9,1},... | collective-permute-start | bytes 3538952 | tf_op jit(solution)/shard_map/ppermute | solution.py:476
  (9 other events, 17.2 us)

commit v3 on v2

--- a/solution.py
+++ b/solution.py
@@ -181,10 +181,7 @@
     return jnp.sum(values, axis=0, keepdims=True)
 
 
-def feed_back_body(
-    gy, wup, wdown, smalls, slope, normal1, inverse1, normal2, inverse2, gz, ga, gr1, gb, gsmall, total
-):
-    up = gy[...].astype(F32)
+def top_back_body(up, smalls, normal2, inverse2, gr2, gz, gsmall):
     normal = normal2[...]
     put_halves(gsmall, N2G, column_sum(up * normal))
     put_halves(gsmall, N2B, column_sum(up))
@@ -192,7 +189,14 @@
     z = grad.astype(LOW)
     gz[...] = z
     put_halves(gsmall, B_DOWN, column_sum(z.astype(F32)))
-    total[...] = grad
+    gr2[...] = grad
+
+
+def feed_back_body(
+    gr2, gz, wup, wdown, smalls, slope, normal1, inverse1, ga, gr1, gb, gsmall, total
+):
+    z = gz[...]
+    total[...] = gr2[...]
 
     def step(tile, carry):
         place = columns(tile)
@@ -215,6 +219,22 @@
     b = grad.astype(LOW)
     gb[...] = b
     put_halves(gsmall, B_OUT, column_sum(b.astype(F32)))
+
+
+def span_rows(spans):
+    row = lax.broadcasted_iota(jnp.int32, (ROWS, 1), 0)
+    inside = row < 0
+    for chain in range(2):
+        start = spans[chain, 0] + chain * LENGTH
+        end = spans[chain, 1] + chain * LENGTH
+        inside = inside | ((row >= start) & (row < end))
+    return inside
+
+
+def pick_halves(half, own, other, smalls):
+    low = half[0] == 0
+    smalls[0:1, :] = jnp.where(low, own[...], other[...])
+    smalls[1:2, :] = jnp.where(low, other[...], own[...])
 
 
 def attend_back_body(gb, gr1, wqkv, wout, spans, first, qkv, probs, gqkv, gh, gqv, gmask, go):
@@ -242,13 +262,7 @@
     gqv[0:1, :] = column_sum(gqkv[:, :WIDTH].astype(F32))
     gqv[1:2, :] = column_sum(gqkv[:, 2 * WIDTH :].astype(F32))
     full = gr1[...] + dot_nt(gqkv[...], wqkv[...])
-    row = lax.broadcasted_iota(jnp.int32, (ROWS, 1), 0)
-    dropped = row < 0
-    for chain in range(2):
-        start = spans[chain, 0] + chain * LENGTH
-        end = spans[chain, 1] + chain * LENGTH
-        dropped = dropped | ((row >= start) & (row < end))
-    dropped = dropped & (first[0] > 0)
+    dropped = span_rows(spans) & (first[0] > 0)
     zero = jnp.zeros_like(full)
     gh[...] = jnp.where(dropped, zero, full).astype(LOW)
     gmask[...] = column_sum(jnp.where(dropped, full, zero))
@@ -282,60 +296,112 @@
 MACS = ROWS * WIDTH * WIDTH * 2
 
 
-def attend(h, half, lens, weights, smalls, save):
-    def body(h, half, lens, smalls, qo, qp, oo, op, *rest):
-        if save:
-            qkv, probs, mixed, normal1, inverse1, u, wqkv, wout, sems = rest
-        else:
-            u, qkv, mixed, wqkv, wout, sems = rest
-            probs = normal1 = inverse1 = None
+SMALL_SCRATCH = pltpu.VMEM((2, SMALL), F32)
+
+
+def pack_small(vectors):
+    def body(*refs):
+        at = 0
+        for size, ref in zip(SIZES, refs):
+            refs[-1][0:1, at : at + size] = ref[...].astype(F32)
+            at += size
+
+    return kernel_call(body, [VMEM] * 8, [shape((1, SMALL), F32)], [], 1000, 30000, "pack_small")(
+        *[vector.reshape(1, -1) for vector in vectors]
+    )[0]
+
+
+def attend_first(inputs, half, lens, spans, mask_vector, weights, smalls):
+    def body(x, half, lens, spans, mask, so, sp, qo, qp, oo, op, u, h, raw, small, qkv, mixed, wqkv, wout, sems):
+        enter = pltpu.make_async_copy(x.at[half[0]], raw, sems.at[2, 0])
+        enter.start()
         first = fetch(half[0], qo, qp, wqkv, sems.at[0])
         second = fetch(half[0], oo, op, wout, sems.at[1])
+        pick_halves(half, so, sp, small)
+        enter.wait()
+        h[...] = jnp.where(span_rows(spans), mask[...], raw[...].reshape(ROWS, WIDTH))
         wait_all(first)
         wait_all(second)
-        attend_body(h, wqkv, wout, smalls, lens, qkv, probs, mixed, normal1, inverse1, u)
-
-    outs = [shape(ROW_SHAPE)]
-    scratch = [
-        pltpu.VMEM((WIDTH, 3 * WIDTH), LOW),
-        pltpu.VMEM((WIDTH, WIDTH), LOW),
-        pltpu.SemaphoreType.DMA((2, 2)),
-    ]
-    if save:
-        outs = [
+        attend_body(h, wqkv, wout, small, lens, qkv, None, mixed, None, None, u)
+
+    return kernel_call(
+        body,
+        [ANY, SMEM, SMEM, SMEM, VMEM, VMEM, VMEM] + [ANY] * 4,
+        [shape(ROW_SHAPE), shape(ROW_SHAPE)],
+        [
+            pltpu.VMEM((2, LENGTH, WIDTH), LOW),
+            SMALL_SCRATCH,
+            pltpu.VMEM(QKV_SHAPE, LOW),
+            pltpu.VMEM(ROW_SHAPE, LOW),
+            pltpu.VMEM((WIDTH, 3 * WIDTH), LOW),
+            pltpu.VMEM((WIDTH, WIDTH), LOW),
+            pltpu.SemaphoreType.DMA((3, 2)),
+        ],
+        4 * MACS,
+        8000000,
+        "attend_first",
+    )(inputs, half, lens, spans, mask_vector.reshape(1, WIDTH), *smalls, *weights[0], *weights[1])
+
+
+def attend(h0, received, half, first, lens, weights, smalls):
+    def body(h0, received, half, first, lens, so, sp, qo, qp, oo, op, *rest):
+        h, qkv, probs, mixed, normal1, inverse1, u, small, wqkv, wout, sems = rest
+        one = fetch(half[0], qo, qp, wqkv, sems.at[0])
+        two = fetch(half[0], oo, op, wout, sems.at[1])
+        pick_halves(half, so, sp, small)
+        h[...] = jnp.where(first[0] > 0, h0[...], received[...])
+        wait_all(one)
+        wait_all(two)
+        attend_body(h, wqkv, wout, small, lens, qkv, probs, mixed, normal1, inverse1, u)
+
+    return kernel_call(
+        body,
+        [VMEM, VMEM, SMEM, SMEM, SMEM, VMEM, VMEM] + [ANY] * 4,
+        [
+            shape(ROW_SHAPE),
             shape(QKV_SHAPE),
             shape(PROBS_SHAPE),
             shape(ROW_SHAPE),
             shape(ROW_SHAPE, F32),
             shape((ROWS, 1), F32),
-        ] + outs
-    else:
-        scratch = [pltpu.VMEM(QKV_SHAPE, LOW), pltpu.VMEM(ROW_SHAPE, LOW)] + scratch
-    return kernel_call(
-        body, [VMEM, SMEM, SMEM, VMEM] + [ANY] * 4, outs, scratch, 4 * MACS, 8000000, "attend"
-    )(h, half, lens, smalls, *weights[0], *weights[1])
+            shape(ROW_SHAPE),
+        ],
+        [
+            SMALL_SCRATCH,
+            pltpu.VMEM((WIDTH, 3 * WIDTH), LOW),
+            pltpu.VMEM((WIDTH, WIDTH), LOW),
+            pltpu.SemaphoreType.DMA((2, 2)),
+        ],
+        4 * MACS,
+        8000000,
+        "attend",
+    )(h0, received, half, first, lens, *smalls, *weights[0], *weights[1])
+
+
+FEED_SCRATCH = [
+    SMALL_SCRATCH,
+    pltpu.VMEM(ROW_SHAPE, F32),
+    pltpu.VMEM((WIDTH, HIDDEN), LOW),
+    pltpu.VMEM((HIDDEN, WIDTH), LOW),
+    pltpu.SemaphoreType.DMA((2, 2)),
+]
 
 
 def feed(u, half, weights, smalls, save):
-    def body(u, half, smalls, uo, up, do, dp, *rest):
+    def body(u, half, so, sp, uo, up, do, dp, *rest):
         if save:
-            slope, active, normal2, inverse2, y, total, wup, wdown, sems = rest
+            slope, active, normal2, inverse2, y, small, total, wup, wdown, sems = rest
         else:
-            y, total, wup, wdown, sems = rest
+            y, small, total, wup, wdown, sems = rest
             slope = active = normal2 = inverse2 = None
         first = fetch(half[0], uo, up, wup, sems.at[0])
         second = fetch(half[0], do, dp, wdown, sems.at[1])
+        pick_halves(half, so, sp, small)
         wait_all(first)
         wait_all(second)
-        feed_body(u, wup, wdown, smalls, slope, active, normal2, inverse2, y, total)
+        feed_body(u, wup, wdown, small, slope, active, normal2, inverse2, y, total)
 
     outs = [shape(ROW_SHAPE)]
-    scratch = [
-        pltpu.VMEM(ROW_SHAPE, F32),
-        pltpu.VMEM((WIDTH, HIDDEN), LOW),
-        pltpu.VMEM((HIDDEN, WIDTH), LOW),
-        pltpu.SemaphoreType.DMA((2, 2)),
-    ]
     if save:
         outs = [
             shape((ROWS, HIDDEN)),
@@ -344,107 +410,112 @@
             shape((ROWS, 1), F32),
         ] + outs
     return kernel_call(
-        body, [VMEM, SMEM, VMEM] + [ANY] * 4, outs, scratch, 8 * MACS, 14000000, "feed"
-    )(u, half, smalls, *weights[2], *weights[3])
-
-
-def feed_back(gy, half, weights, smalls, slope, normal1, inverse1, normal2, inverse2):
-    def body(gy, half, smalls, uo, up, do, dp, slope, n1, i1, n2, i2, *rest):
-        gz, ga, gr1, gb, gsmall, total, wup, wdown, sems = rest
+        body, [VMEM, SMEM, VMEM, VMEM] + [ANY] * 4, outs, FEED_SCRATCH, 8 * MACS, 14000000, "feed"
+    )(u, half, *smalls, *weights[2], *weights[3])
+
+
+TOP_OUTS = [shape(ROW_SHAPE, F32), shape(ROW_SHAPE), shape((2, SMALL), F32)]
+
+
+def top_back(cotangent, returned, half, first, smalls, normal2, inverse2):
+    def body(cot, returned, half, first, so, sp, n2, i2, gr2, gz, gsmall, raw, small, sem):
+        enter = pltpu.make_async_copy(cot.at[half[0]], raw, sem)
+        enter.start()
+        pick_halves(half, so, sp, small)
+        enter.wait()
+        up = raw[...].reshape(ROWS, WIDTH)
+        if returned is not None:
+            up = jnp.where(first[0] > 0, returned[...], up)
+        top_back_body(up.astype(F32), small, n2, i2, gr2, gz, gsmall)
+
+    scratch = [pltpu.VMEM((2, LENGTH, WIDTH), LOW), SMALL_SCRATCH, pltpu.SemaphoreType.DMA]
+    if returned is None:
+        return kernel_call(
+            lambda cot, *rest: body(cot, None, *rest),
+            [ANY, SMEM, SMEM, VMEM, VMEM, VMEM, VMEM],
+            TOP_OUTS,
+            scratch,
+            1000000,
+            4000000,
+            "top_back",
+        )(cotangent, half, first, *smalls, normal2, inverse2)
+    return kernel_call(
+        body,
+        [ANY, VMEM, SMEM, SMEM, VMEM, VMEM, VMEM, VMEM],
+        TOP_OUTS,
+        scratch,
+        1000000,
+        4000000,
+        "top_back",
+    )(cotangent, returned, half, first, *smalls, normal2, inverse2)
+
+
+def feed_back(gr2, gz, half, weights, smalls, slope, normal1, inverse1, after=()):
+    def body(gr2, gz, half, so, sp, uo, up, do, dp, slope, n1, i1, *rest):
+        ga, gr1, gb, gsmall, small, total, wup, wdown, sems = rest[len(after) :]
         second = fetch(half[0], do, dp, wdown, sems.at[1])
         first = fetch(half[0], uo, up, wup, sems.at[0])
+        pick_halves(half, so, sp, small)
         wait_all(second)
         wait_all(first)
-        feed_back_body(
-            gy, wup, wdown, smalls, slope, n1, i1, n2, i2, gz, ga, gr1, gb, gsmall, total
-        )
-
-    outs = [
-        shape(ROW_SHAPE),
-        shape((ROWS, HIDDEN)),
-        shape(ROW_SHAPE, F32),
-        shape(ROW_SHAPE),
-        shape((2, SMALL), F32),
-    ]
-    scratch = [
-        pltpu.VMEM(ROW_SHAPE, F32),
-        pltpu.VMEM((WIDTH, HIDDEN), LOW),
-        pltpu.VMEM((HIDDEN, WIDTH), LOW),
-        pltpu.SemaphoreType.DMA((2, 2)),
-    ]
+        feed_back_body(gr2, gz, wup, wdown, small, slope, n1, i1, ga, gr1, gb, gsmall, total)
+
     return kernel_call(
         body,
-        [VMEM, SMEM, VMEM] + [ANY] * 4 + [VMEM] * 5,
-        outs,
-        scratch,
+        [VMEM, VMEM, SMEM, VMEM, VMEM] + [ANY] * 4 + [VMEM] * 3 + [ANY] * len(after),
+        [
+            shape((ROWS, HIDDEN)),
+            shape(ROW_SHAPE, F32),
+            shape(ROW_SHAPE),
+            shape((2, SMALL), F32),
+        ],
+        FEED_SCRATCH,
         8 * MACS,
         18000000,
         "feed_back",
-    )(
-        gy,
-        half,
-        smalls,
-        *weights[2],
-        *weights[3],
-        slope,
-        normal1,
-        inverse1,
-        normal2,
-        inverse2,
-    )
-
-
-def attend_back(gb, gr1, half, spans, first, weights, qkv, probs):
+    )(gr2, gz, half, *smalls, *weights[2], *weights[3], slope, normal1, inverse1, *after)
+
+
+def attend_back(gb, gr1, half, spans, first, weights, qkv, probs, after=()):
     def body(gb, gr1, half, spans, first, qo, qp, oo, op, qkv, probs, *rest):
-        gqkv, gh, gqv, gmask, go, wqkv, wout, sems = rest
+        gqkv, gh, gqv, gmask, go, wqkv, wout, sems = rest[len(after) :]
         second = fetch(half[0], oo, op, wout, sems.at[1])
         start = fetch(half[0], qo, qp, wqkv, sems.at[0])
         wait_all(second)
         wait_all(start)
         attend_back_body(gb, gr1, wqkv, wout, spans, first, qkv, probs, gqkv, gh, gqv, gmask, go)
 
-    outs = [
-        shape(QKV_SHAPE),
-        shape(ROW_SHAPE),
-        shape((2, WIDTH), F32),
-        shape((1, WIDTH), F32),
-    ]
-    scratch = [
-        pltpu.VMEM(ROW_SHAPE, LOW),
-        pltpu.VMEM((WIDTH, 3 * WIDTH), LOW),
-        pltpu.VMEM((WIDTH, WIDTH), LOW),
-        pltpu.SemaphoreType.DMA((2, 2)),
-    ]
     return kernel_call(
         body,
-        [VMEM, VMEM, SMEM, SMEM, SMEM] + [ANY] * 4 + [VMEM] * 2,
-        outs,
-        scratch,
+        [VMEM, VMEM, SMEM, SMEM, SMEM] + [ANY] * 4 + [VMEM] * 2 + [ANY] * len(after),
+        [
+            shape(QKV_SHAPE),
+            shape(ROW_SHAPE),
+            shape((2, WIDTH), F32),
+            shape((1, WIDTH), F32),
+        ],
+        [
+            pltpu.VMEM(ROW_SHAPE, LOW),
+            pltpu.VMEM((WIDTH, 3 * WIDTH), LOW),
+            pltpu.VMEM((WIDTH, WIDTH), LOW),
+            pltpu.SemaphoreType.DMA((2, 2)),
+        ],
         4 * MACS,
         12000000,
         "attend_back",
-    )(gb, gr1, half, spans, first, *weights[0], *weights[1], qkv, probs)
+    )(gb, gr1, half, spans, first, *weights[0], *weights[1], qkv, probs, *after)
 
 
 def partner(x, axis, bit):
     return lax.ppermute(x, axis, [(i, i ^ 1 << bit) for i in range(lax.axis_size(axis))])
 
 
-def assemble(own_part, partner_part, pair_half):
-    lower = jnp.where(pair_half == 0, own_part, partner_part)
-    upper = jnp.where(pair_half == 0, partner_part, own_part)
-    return jnp.concatenate([lower, upper], axis=0)
-
-
-def take_half(tensor, which_half):
-    half_rows = tensor.shape[0] // 2
-    return lax.dynamic_slice_in_dim(tensor, which_half * half_rows, half_rows, 0)
-
-
-ORDERS = (
-    (("zw", "zu", "xw", "xu"), ("zu", "zw", "xu", "xw")),
-    (("xw", "xu", "zw", "zu"), ("xu", "xw", "zu", "zw")),
-)
+Z_FIRST = ("zw", "zu", "xw", "xu")
+Z_OTHER = ("zu", "zw", "xu", "xw")
+X_FIRST = ("xw", "xu", "zw", "zu")
+X_OTHER = ("xu", "xw", "zu", "zw")
+ONE = (Z_FIRST, X_FIRST)
+TWO = (Z_OTHER, X_OTHER)
 
 
 def flip_dp(index, bit):
@@ -462,80 +533,61 @@
     return z * 8 + x * 2 + y
 
 
-def flip_pairs(bit_of_core):
+def exchange(value, bit_of_core):
     pairs = []
     for section in range(4):
         for index in range(32):
             pairs.append(
                 (section * 32 + index, section * 32 + flip_dp(index, bit_of_core[section % 2]))
             )
-    return pairs
-
-
-def exchange(value, bit_of_core):
-    return lax.ppermute(value, ("section", "dp"), flip_pairs(bit_of_core))
+    return lax.ppermute(value, ("section", "dp"), pairs)
 
 
 def own_bits():
     index = lax.axis_index("dp")
-    z, x, y = index // 8, index // 2 % 4, index % 2
+    z, x = index // 8, index // 2 % 4
     return {
         "zu": z // 2,
         "zw": (z // 2) ^ (z % 2),
         "xu": x // 2,
         "xw": (x // 2) ^ (x % 2),
-        "y": y,
     }
 
 
-def own_bit(bits, core, part, step):
-    return jnp.where(core == 0, bits[ORDERS[0][part][step]], bits[ORDERS[1][part][step]])
-
-
 def add_low(left_side, right_side):
-    return (left_side.astype(jnp.float32) + right_side.astype(jnp.float32)).astype(jnp.bfloat16)
-
-
-def reduce_rows(pack, extra, bits, core):
-    half = pack.shape[0] // 2
-    parts = [pack[:half], pack[half:]]
-    for step in range(4):
-        for part in range(2):
-            bit = own_bit(bits, core, part, step)
-            rows = parts[part].shape[0] // 2
-            keep = lax.dynamic_slice_in_dim(parts[part], bit * rows, rows, 0)
-            send = lax.dynamic_slice_in_dim(parts[part], (1 - bit) * rows, rows, 0)
-            flips = (ORDERS[0][part][step], ORDERS[1][part][step])
-            if part == 0 and extra is not None:
-                got = exchange(jnp.concatenate([send, extra], axis=0), flips)
-                extra = add_low(extra, got[rows:])
-                got = got[:rows]
-            else:
-                got = exchange(send, flips)
-            parts[part] = add_low(keep, got)
-    rows = parts[0].shape[0]
-    both = jnp.concatenate(parts + ([extra] if extra is not None else []), axis=0)
-    both = add_low(both, exchange(both, ("y", "y")))
-    parts = [both[:rows], both[rows : 2 * rows]]
-    if extra is not None:
-        extra = both[2 * rows :]
-    for step in reversed(range(4)):
-        for part in range(2):
-            bit = own_bit(bits, core, part, step)
-            flips = (ORDERS[0][part][step], ORDERS[1][part][step])
-            got = exchange(parts[part], flips)
-            parts[part] = assemble(parts[part], got, bit)
-    return jnp.concatenate(parts, axis=0), extra
-
-
-def fold(tensor):
-    return jnp.concatenate(
-        [tensor[:, at : at + 768] for at in range(0, tensor.shape[1], 768)], axis=0
-    )
-
-
-def unfold(rows, count):
-    return jnp.concatenate(jnp.split(rows, count, axis=0), axis=1)
+    return (left_side.astype(F32) + right_side.astype(F32)).astype(LOW)
+
+
+class Chain:
+    def __init__(self, value, orders, bits, core):
+        self.value = value
+        self.flips = [(orders[0][step], orders[1][step]) for step in range(4)]
+        self.bits = [jnp.where(core == 0, bits[a], bits[b]) for a, b in self.flips]
+
+    def halve(self, step):
+        bit = self.bits[step]
+        rows = self.value.shape[0] // 2
+        keep = lax.dynamic_slice_in_dim(self.value, bit * rows, rows, 0)
+        send = lax.dynamic_slice_in_dim(self.value, (1 - bit) * rows, rows, 0)
+        self.value = add_low(keep, exchange(send, self.flips[step]))
+
+    def across(self):
+        self.value = add_low(self.value, exchange(self.value, ("y", "y")))
+
+    def double(self, step):
+        got = exchange(self.value, self.flips[step])
+        bit = self.bits[step]
+        lower = jnp.where(bit == 0, self.value, got)
+        upper = jnp.where(bit == 0, got, self.value)
+        self.value = jnp.concatenate([lower, upper], axis=0)
+
+    def run(self):
+        for step in range(4):
+            self.halve(step)
+        self.across()
+        for step in (3, 2, 1, 0):
+            self.double(step)
+        return self.value
 
 
 def per_device(
@@ -558,60 +610,57 @@
     norm2_bias,
 ):
     section_index = lax.axis_index("section")
-    is_first = section_index < 2
-    pair_half = section_index % 2
-    half = pair_half.astype(jnp.int32).reshape(1)
-    first = is_first.astype(jnp.int32).reshape(1)
-    big = (w_qkv, w_out, w_up, w_down)
-    small = jnp.concatenate(
-        [qv_bias, b_out, norm1_gain, norm1_bias, b_up, b_down, norm2_gain, norm2_bias]
-    )
-    partner_small = partner(small, "section", 0)
-    weights = [(tensor, partner(tensor, "section", 0)) for tensor in big]
-    smalls = jnp.where(
-        pair_half == 0,
-        jnp.stack([small, partner_small]),
-        jnp.stack([partner_small, small]),
-    ).astype(F32)
-    my_inputs = lax.dynamic_index_in_dim(inputs, pair_half, 0, keepdims=False)
-    my_cotangent = lax.dynamic_index_in_dim(cotangent, pair_half, 0, keepdims=False)
-    lens = lax.dynamic_index_in_dim(lengths, pair_half, 0, keepdims=False)
-    spans = lax.dynamic_index_in_dim(cdr_spans, pair_half, 0, keepdims=False)
-    positions = jnp.arange(LENGTH, dtype=jnp.int32)
-    masked = (positions[None, :] >= spans[:, 0:1]) & (positions[None, :] < spans[:, 1:2])
-    entered = jnp.where(masked[:, :, None], mask_vector[None, None, :], my_inputs)
-    entered = entered.reshape(ROWS, WIDTH)
-    my_cotangent = my_cotangent.reshape(ROWS, WIDTH)
-
-    (u,) = attend(entered, half, lens, weights, smalls, False)
+    core = section_index % 2
+    half = core.astype(jnp.int32).reshape(1)
+    first = (section_index < 2).astype(jnp.int32).reshape(1)
+    weights = [(tensor, partner(tensor, "section", 0)) for tensor in (w_qkv, w_out, w_up, w_down)]
+    small = pack_small(
+        (qv_bias, b_out, norm1_gain, norm1_bias, b_up, b_down, norm2_gain, norm2_bias)
+    )
+    smalls = (small, partner(small, "section", 0))
+    lens = lax.dynamic_index_in_dim(lengths, core, 0, keepdims=False)
+    spans = lax.dynamic_index_in_dim(cdr_spans, core, 0, keepdims=False)
+
+    u, h0 = attend_first(inputs, half, lens, spans, mask_vector, weights, smalls)
     (first_out,) = feed(u, half, weights, smalls, False)
     received = lax.ppermute(first_out, "section", [(0, 2), (1, 3)])
-    layer_in = jnp.where(is_first, entered, received)
-    qkv, probs, mixed, normal1, inverse1, u = attend(layer_in, half, lens, weights, smalls, True)
+    h, qkv, probs, mixed, normal1, inverse1, u = attend(
+        h0, received, half, first, lens, weights, smalls
+    )
     slope, active, normal2, inverse2, output = feed(u, half, weights, smalls, True)
-
-    def back(upstream):
-        gz, ga, gr1, gb, gsmall = feed_back(
-            upstream, half, weights, smalls, slope, normal1, inverse1, normal2, inverse2
-        )
-        gqkv, gh, gqv, gmask = attend_back(gb, gr1, half, spans, first, weights, qkv, probs)
-        return gz, ga, gb, gsmall, gqkv, gh, gqv, gmask
-
-    upper_grad = back(my_cotangent)[5]
+    gr2, gz, _ = top_back(cotangent, None, half, first, smalls, normal2, inverse2)
+    _, gr1, gb, _ = feed_back(gr2, gz, half, weights, smalls, slope, normal1, inverse1)
+    _, upper_grad, _, _ = attend_back(gb, gr1, half, spans, first, weights, qkv, probs)
     returned = lax.ppermute(upper_grad, "section", [(2, 0), (3, 1)])
-    upstream = jnp.where(is_first, returned, my_cotangent)
-    gz, ga, gb, gsmall, gqkv, gh, gqv, gmask = back(upstream)
-
-    def pair_sum(left_side, right_side):
-        low = dot_tn(left_side, right_side).astype(LOW)
-        got = partner(take_half(low, 1 - pair_half), "section", 0)
-        return add_low(take_half(low, pair_half), got)
 
     bits = own_bits()
-    early = jnp.concatenate([pair_sum(active, gz), fold(pair_sum(u, ga))], axis=0)
-    gsmall = jnp.concatenate([gqv, gsmall[:, WIDTH:]], axis=1)
-    own_small = lax.dynamic_index_in_dim(gsmall, pair_half, 0, keepdims=False)
-    other_small = lax.dynamic_index_in_dim(gsmall, 1 - pair_half, 0, keepdims=False)
+
+    def columns_of(tensor, which):
+        size = tensor.shape[1] // 2
+        return lax.dynamic_slice_in_dim(tensor, which * size, size, 1)
+
+    def weight_grad(left_side, right_side):
+        other = dot_tn(columns_of(left_side, 1 - core), right_side).astype(LOW)
+        got = partner(other, "section", 0)
+        return (dot_tn(columns_of(left_side, core), right_side) + got.astype(F32)).astype(LOW)
+
+    gr2, gz, top_small = top_back(cotangent, returned, half, first, smalls, normal2, inverse2)
+    down = Chain(weight_grad(active, gz), ONE, bits, core)
+    ga, gr1, gb, low_small = feed_back(
+        gr2, gz, half, weights, smalls, slope, normal1, inverse1, (down.value,)
+    )
+    up = Chain(weight_grad(u, ga), TWO, bits, core)
+    gqkv, gh, gqv, gmask = attend_back(
+        gb, gr1, half, spans, first, weights, qkv, probs, (up.value,)
+    )
+    late_qkv = weight_grad(h, gqkv)
+    late_out = weight_grad(mixed, gb)
+    late_one = Chain(late_qkv[:, :1536], ONE, bits, core)
+    gsmall = jnp.concatenate(
+        [gqv, low_small[:, B_OUT:B_DOWN], top_small[:, B_DOWN:]], axis=1
+    )
+    own_small = lax.dynamic_index_in_dim(gsmall, core, 0, keepdims=False)
+    other_small = lax.dynamic_index_in_dim(gsmall, 1 - core, 0, keepdims=False)
     summed_small = own_small + partner(other_small.astype(LOW), "section", 0).astype(F32)
     extra = jnp.concatenate(
         [
@@ -621,9 +670,28 @@
         ],
         axis=0,
     )
-    late = jnp.concatenate([pair_sum(mixed, gb), fold(pair_sum(layer_in, gqkv))], axis=0)
-    early, _ = reduce_rows(early, None, bits, pair_half)
-    late, extra = reduce_rows(late, extra, bits, pair_half)
+    extra = jnp.concatenate([extra[:8], extra[8:]], axis=1)
+    late_two = Chain(jnp.concatenate([late_qkv[:, 1536:], late_out], axis=1), TWO, bits, core)
+
+    for step in range(4):
+        late_one.halve(step)
+        bit = late_two.bits[step]
+        rows = late_two.value.shape[0] // 2
+        keep = lax.dynamic_slice_in_dim(late_two.value, bit * rows, rows, 0)
+        send = lax.dynamic_slice_in_dim(late_two.value, (1 - bit) * rows, rows, 0)
+        got = exchange(jnp.concatenate([send, extra], axis=0), late_two.flips[step])
+        extra = add_low(extra, got[rows:])
+        late_two.value = add_low(keep, got[:rows])
+    rows = late_one.value.shape[0]
+    both = jnp.concatenate([late_one.value, late_two.value, extra], axis=0)
+    both = add_low(both, exchange(both, ("y", "y")))
+    late_one.value = both[:rows]
+    late_two.value = both[rows : 2 * rows]
+    extra = both[2 * rows :]
+    for step in (3, 2, 1, 0):
+        late_one.double(step)
+        late_two.double(step)
+    extra = jnp.concatenate([extra[:, :WIDTH], extra[:, WIDTH:]], axis=0)
     mask_row = extra[6:7]
     mask_row = mask_row.astype(F32) + partner(mask_row, "section", 0).astype(F32)
     mask_low = mask_row.astype(LOW)
@@ -637,19 +705,20 @@
         out_small.append(flat_small[at : at + size])
         at += size
     g_qv, g_bo, g_n1g, g_n1b, g_bu, g_bd, g_n2g, g_n2b = out_small
+    g_qkv = jnp.concatenate([late_one.value, late_two.value[:, :WIDTH]], axis=1)
     return (
         output.reshape(1, 2, LENGTH, WIDTH),
         gh.reshape(1, 2, LENGTH, WIDTH),
         mask_grad,
-        unfold(late[384:], 3).astype(F32),
+        g_qkv.astype(F32),
         g_qv,
-        late[:384].astype(F32),
+        late_two.value[:, WIDTH:].astype(F32),
         g_bo,
         g_n1g,
         g_n1b,
-        unfold(early[1536:], 4).astype(F32),
+        up.run().astype(F32),
         g_bu,
-        early[:1536].astype(F32),
+        down.run().astype(F32),
         g_bd,
         g_n2g,
         g_n2b,

time: 380 us -> 386 us (1.016)
  other arithmetic: 34.4 us -> 20 us
  waiting for transfers between devices: 113 us -> 125 us
  matrix products: 9.96 us -> 21.5 us
  starting transfers between devices: 63 us -> 52.5 us
  Pallas kernels: 127 us -> 136 us
    dot_general x4 -> x8, matrix products: 9.96 us -> 21.5 us  [dot_tn(): lax.dot_general(left_side, right_side, (((0,), (0,)), ((), ())), preferre...]
    reshape x0 -> x9, local copies, waits for them, and re-layouts: none -> 11.3 us  [the longest x8 10 us: pack_small(): vector.reshape(1, -1)]
    convert_element_type x32 -> x27, other arithmetic: 24.4 us -> 13.1 us  [the longest x23 4.64 us: add_low(): return (left_side.astype(F32) + right_side.astype(F32)).astype(LOW)]
    pallas_call x6 -> x9, Pallas kernels: 97.3 us -> 106 us  [the longest x2 35.7 us: feed(): kernel_call(body, [VMEM, SMEM, VMEM, VMEM] + [ANY] * 4, outs, FEED_SCRATC...]
    ppermute x34 -> x35, starting transfers between devices: 54.5 us -> 45.9 us  [exchange(): return lax.ppermute(value, ('section', 'dp'), pairs)]
    unnamed x57 -> x46, local copies, waits for them, and re-layouts: 11.8 us -> 5.58 us
    dynamic_slice x20 -> x16, local copies, waits for them, and re-layouts: 7.68 us -> 1.61 us  [the longest x12 1.49 us: halve(): send = lax.dynamic_slice_in_dim(self.value, (1 - bit) * rows, rows, 0)]
    ppermute x34 -> x35, waiting for transfers between devices: 88.7 us -> 94.5 us  [exchange(): return lax.ppermute(value, ('section', 'dp'), pairs)]
  transfers between devices with their start and end apart: 48 -> 49, of which waited for: 22 -> 28; matrix products, arithmetic and copies ran while one was open for 14% -> 12% of each run, Pallas kernels for 4% -> 12%
where the time goes in v3:
time: 386 us; the launch traced here: 380 us
  Pallas kernels  136 us (35%)
  waiting for transfers between devices  125 us (32%)
  starting transfers between devices  52.5 us (14%)
  local copies, waits for them, and re-layouts  23.1 us (6%)
  matrix products  21.5 us (6%)
  other arithmetic  20 us (5%)
    ppermute x35, waiting for transfers between devices, exchange(): return lax.ppermute(value, ('section', 'dp'), pairs)  94.5 us
    ppermute x35, starting transfers between devices, exchange(): return lax.ppermute(value, ('section', 'dp'), pairs)  45.9 us
    pallas_call x2, Pallas kernels, feed(): kernel_call(body, [VMEM, SMEM, VMEM, VMEM] + [ANY] * 4, outs, FEED_SCRATC...  35.7 us
    pallas_call x2, Pallas kernels, feed_back(): kernel_call(body, [VMEM, VMEM, SMEM, VMEM, VMEM] + [ANY] * 4 + [VMEM] * 3...  33.6 us
    pallas_call x2, Pallas kernels, attend_back(): kernel_call(body, [VMEM, VMEM, SMEM, SMEM, SMEM] + [ANY] * 4 + [VMEM] * 2...  30.1 us
    dot_general x8, matrix products, dot_tn(): lax.dot_general(left_side, right_side, (((0,), (0,)), ((), ())), preferre...  21.5 us
    pallas_call x1, Pallas kernels, attend(): kernel_call(body, [VMEM, VMEM, SMEM, SMEM, SMEM, VMEM, VMEM] + [ANY] * 4,...  13.9 us
    ppermute x1, waiting for transfers between devices, per_device(): returned = lax.ppermute(upper_grad, 'section', [(2, 0), (3, 1)])  13.6 us
  transfers between devices with their start and end apart: 49, of which 28 were waited for; matrix products, arithmetic and copies ran while one was open for 12% of the time, Pallas kernels for 12%

profile of v3, /device:TPU:0, one launch (start us, length us, event | category | flops | bytes accessed | tf_op | source)
XLA Modules:
  0.0 380.0 jit_solution(16815915091945196539)
XLA Ops:
  11.8 1.4 pack_small.1.so.rest_2_
  17.7 13.2 %attend_first.1 = (bf16[320,768]{1,0:T(8,128)(2,1)}, bf16[320,768]{1,0:T(8,128)(2,1)}) custom-call(bf16[2,2,160,768]{3,2,1,0:T(8,128)(2,1)} %x.3, s32[1]{0:T(128)} %bitcast.half.rest_0_, s32[2]{0:T(128)} %fusion.24.lens, s32[2,2]{1,0:T(2,128)} %fusion.23.spans, bf16[1,768]{1,0:T(2,128)(2,1)} %reshape.79.mask, f32[1,4608]{1,0:T(1,128)} %pack_small.1.so.rest_2_, ...), custom_call_target="tpu_custom_call" | custom-call | flops 1509949440 | bytes 8000000 | tf_op jit(solution)/shard_map/attend_first/pallas_call | solution.py:327
  30.9 17.1 %feed.2 = bf16[320,768]{1,0:T(8,128)(2,1)} custom-call(bf16[320,768]{1,0:T(8,128)(2,1)} %get-tuple-element.46.u, s32[1]{0:T(128)} %bitcast.half.rest_0_, f32[1,4608]{1,0:T(1,128)} %pack_small.1.so.rest_2_, f32[1,4608]{1,0:T(1,128)} %copy-done.10, bf16[384,3072]{1,0:T(8,128)(2,1)} %uo.7, bf16[384,3072]{1,0:T(8,128)(2,1)} %collective-permute-done.3.up, ...), custom_call_target="tpu_custom_call" | custom-call | flops 3019898880 | bytes 14000000 | tf_op jit(solution)/shard_map/feed/pallas_call | solution.py:412
  48.0 3.8 collective-permute-start.5
  51.8 11.2 %collective-permute-done.5.received = bf16[320,768]{1,0:T(8,128)(2,1)S(1)} collective-permute-done((bf16[320,768]{1,0:T(8,128)(2,1)}, bf16[320,768]{1,0:T(8,128)(2,1)S(1)}, u32[]{:S(2)}, u32[]{:S(2)}) %collective-permute-start.5) | collective-permute-done | bytes 491552 | tf_op jit(solution)/shard_map/ppermute | solution.py:626
  63.8 13.9 %attend.1 = (bf16[320,768]{1,0:T(8,128)(2,1)}, bf16[320,2304]{1,0:T(8,128)(2,1)}, bf16[12,320,160]{2,1,0:T(8,128)(2,1)}, bf16[320,768]{1,0:T(8,128)(2,1)}, f32[3...) custom-call(bf16[320,768]{1,0:T(8,128)(2,1)} %get-tuple-element.45.h0, bf16[320,768]{1,0:T(8,128)(2,1)} %copy-done.14, ...), custom_call_target="tpu_custom_call" | custom-call | flops 1509949440 | bytes 8000000 | tf_op jit(solution)/shard_map/attend/pallas_call | solution.py:357
  77.7 18.6 %feed.3 = (bf16[320,3072]{1,0:T(8,128)(2,1)}, bf16[320,3072]{1,0:T(8,128)(2,1)}, f32[320,768]{1,0:T(8,128)}, f32[320,1]{1,0:T(8,128)}, bf16[320,768]{1,0:T(8,128)(2,1)}) custom-call(bf16[320,768]{1,0:T(8,128)(2,1)} %get-tuple-element.47.u, s32[1]{0:T(128)} %bitcast.half.rest_0_, f32[1,4608]{1,0:T(1,128)} %pack_small.1.so.rest_2_, f32[1,4608]{1,0:T(1,128)} %copy-done.10, ...), custom_call_target="tpu_custom_call" | custom-call | flops 3019898880 | bytes 14000000 | tf_op jit(solution)/shard_map/feed/pallas_call | solution.py:412
  96.3 4.0 %top_back.2 = (f32[320,768]{1,0:T(8,128)}, bf16[320,768]{1,0:T(8,128)(2,1)}, f32[2,4608]{1,0:T(2,128)}) custom-call(bf16[2,2,160,768]{3,2,1,0:T(8,128)(2,1)} %cot.3, s32[1]{0:T(128)} %bitcast.half.rest_0_, s32[1]{0:T(128)} %bitcast.3.first.rest_1_, f32[1,4608]{1,0:T(1,128)} %pack_small.1.so.rest_2_, f32[1,4608]{1,0:T(1,128)} %copy-done.10, ...), custom_call_target="tpu_custom_call" | custom-call | flops 1000000 | bytes 4000000 | tf_op jit(solution)/shard_map/top_back/pallas_call | solution.py:433
  100.3 16.8 %feed_back.2 = (bf16[320,3072]{1,0:T(8,128)(2,1)}, f32[320,768]{1,0:T(8,128)}, bf16[320,768]{1,0:T(8,128)(2,1)}, f32[2,4608]{1,0:T(2,128)}) custom-call(f32[320,768]{1,0:T(8,128)} %get-tuple-element.51.gr2, bf16[320,768]{1,0:T(8,128)(2,1)} %get-tuple-element.52.gz, s32[1]{0:T(128)} %bitcast.half.rest_0_, f32[1,4608]{1,0:T(1,128)} %pack_small.1.so.rest_2_, ...), custom_call_target="tpu_custom_call" | custom-call | flops 3019898880 | bytes 18000000 | tf_op jit(solution)/shard_map/feed_back/pallas_call | solution.py:463
  117.1 15.0 %attend_back.2 = (bf16[320,2304]{1,0:T(8,128)(2,1)}, bf16[320,768]{1,0:T(8,128)(2,1)}, f32[2,768]{1,0:T(2,128)}, f32[1,768]{1,0:T(1,128)}) custom-call(bf16[320,768]{1,0:T(8,128)(2,1)} %get-tuple-element.56.gb, f32[320,768]{1,0:T(8,128)} %get-tuple-element.57.gr1, s32[1]{0:T(128)} %bitcast.half.rest_0_, s32[2,2]{1,0:T(2,128)} %fusion.23.spans, ...), custom_call_target="tpu_custom_call" | custom-call | flops 1509949440 | bytes 12000000 | tf_op jit(solution)/shard_map/attend_back/pallas_call | solution.py:488
  133.5 13.6 %collective-permute-done.6.returned = bf16[320,768]{1,0:T(8,128)(2,1)S(1)} collective-permute-done((bf16[320,768]{1,0:T(8,128)(2,1)}, bf16[320,768]{1,0:T(8,128)(2,1)S(1)}, u32[]{:S(2)}, u32[]{:S(2)}) %collective-permute-start.6) | collective-permute-done | bytes 491552 | tf_op jit(solution)/shard_map/ppermute | solution.py:634
  147.8 4.2 %top_back.3 = (f32[320,768]{1,0:T(8,128)}, bf16[320,768]{1,0:T(8,128)(2,1)}, f32[2,4608]{1,0:T(2,128)}) custom-call(bf16[2,2,160,768]{3,2,1,0:T(8,128)(2,1)} %cot.3, bf16[320,768]{1,0:T(8,128)(2,1)} %copy-done.11, s32[1]{0:T(128)} %bitcast.half.rest_0_, s32[1]{0:T(128)} %bitcast.3.first.rest_1_, f32[1,4608]{1,0:T(1,128)} %pack_small.1.so.rest_2_, ...), custom_call_target="tpu_custom_call" | custom-call | flops 1000000 | bytes 4000000 | tf_op jit(solution)/shard_map/top_back/pallas_call | solution.py:442
  152.0 3.9 %convolution_convert_fusion.2 = bf16[1536,768]{1,0:T(8,128)(2,1)} fusion(bf16[320,768]{1,0:T(8,128)(2,1)} %get-tuple-element.62.gz, bf16[320,3072]{1,0:T(8,128)(2,1)S(1)} %copy-done.22, s32[]{:T(128)S(6)} %select_n.352), kind=kOutput, calls=%fused_computation.6 | convolution fusion | flops 756154368 | bytes 3833860 | tf_op jit(solution)/shard_map/dot_general | solution.py:38
  156.0 4.9 %collective-permute-done.7 = bf16[1536,768]{1,0:T(8,128)(2,1)} collective-permute-done((bf16[1536,768]{1,0:T(8,128)(2,1)}, bf16[1536,768]{1,0:T(8,128)(2,1)}, u32[]{:S(2)}, u32[]{:S(2)}) %collective-permute-start.7) | collective-permute-done | bytes 2359328 | tf_op jit(solution)/shard_map/ppermute | solution.py:510
  160.8 3.4 add_convert_fusion.1.rest_0_
  164.3 1.3 copy-done.5
  165.6 2.1 collective-permute-start.40
  167.7 16.9 %feed_back.3 = (bf16[320,3072]{1,0:T(8,128)(2,1)}, f32[320,768]{1,0:T(8,128)}, bf16[320,768]{1,0:T(8,128)(2,1)}, f32[2,4608]{1,0:T(2,128)}) custom-call(f32[320,768]{1,0:T(8,128)} %get-tuple-element.61.gr2, bf16[320,768]{1,0:T(8,128)(2,1)} %get-tuple-element.62.gz, s32[1]{0:T(128)} %bitcast.half.rest_0_, f32[1,4608]{1,0:T(1,128)} %pack_small.1.so.rest_2_, ...), custom_call_target="tpu_custom_call" | custom-call | flops 3019898880 | bytes 18000000 | tf_op jit(solution)/shard_map/feed_back/pallas_call | solution.py:463
  184.6 1.7 add_convert_fusion.2
  186.4 2.6 collective-permute-start.41
  189.0 2.8 convolution_convert_fusion.1
  191.9 5.7 %collective-permute-done.41 = bf16[384,768]{1,0:T(8,128)(2,1)S(1)} collective-permute-done((bf16[384,768]{1,0:T(8,128)(2,1)S(1)}, bf16[384,768]{1,0:T(8,128)(2,1)S(1)}, u32[]{:S(2)}, u32[]{:S(2)}) %collective-permute-start.41) | collective-permute-done | bytes 589856 | tf_op jit(solution)/shard_map/ppermute | solution.py:543
  197.8 1.6 collective-permute-start.42
  199.4 1.4 convolution_convert_fusion.3
  200.9 3.7 collective-permute-done.42
  204.7 2.8 collective-permute-start.43
  208.4 2.8 collective-permute-done.43
  211.2 3.0 collective-permute-start.44
  214.7 3.2 collective-permute-done.44
  218.0 2.8 collective-permute-start.45
  220.8 4.5 %add_convert_fusion.rest_0_ = bf16[384,3072]{1,0:T(8,128)(2,1)} fusion(bf16[384,3072]{1,0:T(8,128)(2,1)} %collective-permute-done.8, bf16[320,3072]{1,0:T(8,128)(2,1)S(1)} %copy-done.19, bf16[320,768]{1,0:T(8,128)(2,1)S(1)} %copy-done.21, s32[]{:T(128)S(6)} %select_n.353), kind=kOutput, calls=%fused_computation | convolution fusion | flops 758513664 | bytes 6930436 | tf_op jit(solution)/shard_map/dot_general | solution.py:38
  225.3 15.1 %attend_back.3 = (bf16[320,2304]{1,0:T(8,128)(2,1)}, bf16[320,768]{1,0:T(8,128)(2,1)}, f32[2,768]{1,0:T(2,128)}, f32[1,768]{1,0:T(1,128)}) custom-call(bf16[320,768]{1,0:T(8,128)(2,1)} %get-tuple-element.64.gb, f32[320,768]{1,0:T(8,128)} %get-tuple-element.65.gr1, s32[1]{0:T(128)} %bitcast.half.rest_0_, s32[2,2]{1,0:T(2,128)} %fusion.23.spans, ...), custom_call_target="tpu_custom_call" | custom-call | flops 1509949440 | bytes 12000000 | tf_op jit(solution)/shard_map/attend_back/pallas_call | solution.py:488
  243.2 2.5 collective-permute-start.31
  245.7 2.3 convolution_convert_fusion
  249.4 6.9 %collective-permute-done.46 = bf16[192,768]{1,0:T(8,128)(2,1)} collective-permute-done((bf16[192,768]{1,0:T(8,128)(2,1)}, bf16[192,768]{1,0:T(8,128)(2,1)}, u32[]{:S(2)}, u32[]{:S(2)}) %collective-permute-start.46) | collective-permute-done | bytes 294944 | tf_op jit(solution)/shard_map/ppermute | solution.py:543
  258.2 2.7 collective-permute-done.31
  260.9 1.7 add_convert_fusion.3
  262.7 5.9 %collective-permute-done.47 = bf16[384,768]{1,0:T(8,128)(2,1)S(1)} collective-permute-done((bf16[384,768]{1,0:T(8,128)(2,1)S(1)}, bf16[384,768]{1,0:T(8,128)(2,1)S(1)}, u32[]{:S(2)}, u32[]{:S(2)}) %collective-permute-start.47) | collective-permute-done | bytes 589856 | tf_op jit(solution)/shard_map/ppermute | solution.py:543
  270.3 2.6 fusion
  275.2 2.6 collective-permute-start.16
  277.8 6.6 %collective-permute-done.33 = bf16[48,3072]{1,0:T(8,128)(2,1)S(1)} collective-permute-done((bf16[48,3072]{1,0:T(8,128)(2,1)S(1)}, bf16[48,3072]{1,0:T(8,128)(2,1)S(1)}, u32[]{:S(2)}, u32[]{:S(2)}) %collective-permute-start.33) | collective-permute-done | bytes 294944 | tf_op jit(solution)/shard_map/ppermute | solution.py:543
  284.6 2.2 collective-permute-done.48
  287.3 4.0 %collective-permute-done.34 = bf16[24,3072]{1,0:T(8,128)(2,1)S(1)} collective-permute-done((bf16[24,3072]{1,0:T(8,128)(2,1)S(1)}, bf16[24,3072]{1,0:T(8,128)(2,1)S(1)}, u32[]{:S(2)}, u32[]{:S(2)}) %collective-permute-start.34) | collective-permute-done | bytes 147488 | tf_op jit(solution)/shard_map/ppermute | solution.py:543
  291.4 3.0 collective-permute-start.35
  294.4 2.5 maximum_convert_fusion.1
  298.5 2.1 collective-permute-start.11
  300.9 2.4 collective-permute-done.36
  304.4 4.7 %collective-permute-done.11 = bf16[96,1536]{1,0:T(8,128)(2,1)S(1)} collective-permute-done((bf16[96,1536]{1,0:T(8,128)(2,1)S(1)}, bf16[96,1536]{1,0:T(8,128)(2,1)S(1)}, u32[]{:S(2)}, u32[]{:S(2)}) %collective-permute-start.11) | collective-permute-done | bytes 294944 | tf_op jit(solution)/shard_map/ppermute | solution.py:543
  309.6 2.2 collective-permute-start.18
  311.9 2.5 collective-permute-done.12
  314.9 1.4 collective-permute-done.18
  317.1 3.0 collective-permute-done.13
  320.2 2.0 collective-permute-done.19
  322.3 2.8 collective-permute-start.20
  325.2 4.1 %collective-permute-done.20 = bf16[56,1536]{1,0:T(8,128)(2,1)S(1)} collective-permute-done((bf16[56,1536]{1,0:T(8,128)(2,1)S(1)}, bf16[56,1536]{1,0:T(8,128)(2,1)S(1)}, u32[]{:S(2)}, u32[]{:S(2)}) %collective-permute-start.20) | collective-permute-done | bytes 172064 | tf_op jit(solution)/shard_map/ppermute | solution.py:543
  331.9 2.1 collective-permute-start.23
  334.9 2.6 collective-permute-done.23
  339.9 5.0 %collective-permute-done.28 = bf16[48,1536]{1,0:T(8,128)(2,1)S(1)} collective-permute-done((bf16[48,1536]{1,0:T(8,128)(2,1)S(1)}, bf16[48,1536]{1,0:T(8,128)(2,1)S(1)}, u32[]{:S(2)}, u32[]{:S(2)}) %collective-permute-start.28) | collective-permute-done | bytes 147488 | tf_op jit(solution)/shard_map/ppermute | solution.py:543
  345.2 3.5 collective-permute-start.25
  349.2 2.6 collective-permute-done.29
  352.0 2.6 collective-permute-start.30
  354.8 18.1 %collective-permute-done.30 = bf16[192,1536]{1,0:T(8,128)(2,1)S(1)} collective-permute-done((bf16[192,1536]{1,0:T(8,128)(2,1)S(1)}, bf16[192,1536]{1,0:T(8,128)(2,1)S(1)}, u32[]{:S(2)}, u32[]{:S(2)}) %collective-permute-start.30) | collective-permute-done | bytes 589856 | tf_op jit(solution)/shard_map/ppermute | solution.py:543
  374.4 2.0 maximum_convert_fusion.2
  377.1 2.8 maximum_convert_fusion
  (208 shorter events, 44.7 us)
Async XLA Ops:
  0.6 12.6 %copy-start = (s32[2,2,2]{2,1,0:T(2,128)S(1)}, s32[2,2,2]{2,1,0:T(2,128)}, u32[]{:S(2)}) copy-start(s32[2,2,2]{2,1,0:T(2,128)} %param.20) | copy-start | bytes 100
  0.7 30.2 %collective-permute-start.3 = (bf16[384,3072]{1,0:T(8,128)(2,1)}, bf16[384,3072]{1,0:T(8,128)(2,1)}, u32[]{:S(2)}, u32[]{:S(2)}) collective-permute-start(bf16[384,3072]{1,0:T(8,128)(2,1)} %uo.7), channel_id=1, source_target_pairs={{0,32},{32,0},{64,96},{96,64},{1,33},{33,1},{65,97},{97,65},{2,34}... | collective-permute-start | bytes 7077896 | tf_op jit(solution)/shard_map/ppermute | solution.py:510
  0.8 30.2 %collective-permute-start.4 = (bf16[1536,768]{1,0:T(8,128)(2,1)}, bf16[1536,768]{1,0:T(8,128)(2,1)}, u32[]{:S(2)}, u32[]{:S(2)}) collective-permute-start(bf16[1536,768]{1,0:T(8,128)(2,1)} %do.7), channel_id=1, source_target_pairs={{0,32},{32,0},{64,96},{96,64},{1,33},{33,1},{65,97},{97,65},{2,34}... | collective-permute-start | bytes 7077896 | tf_op jit(solution)/shard_map/ppermute | solution.py:510
  1.3 15.1 %collective-permute-start.1 = (bf16[384,2304]{1,0:T(8,128)(2,1)}, bf16[384,2304]{1,0:T(8,128)(2,1)S(1)}, u32[]{:S(2)}, u32[]{:S(2)}) collective-permute-start(bf16[384,2304]{1,0:T(8,128)(2,1)} %qo.7), channel_id=1, source_target_pairs={{0,32},{32,0},{64,96},{96,64},{1,33},{33,1},{65,97},{97,65},{2,34}... | collective-permute-start | bytes 5308424 | tf_op jit(solution)/shard_map/ppermute | solution.py:510
  1.3 14.9 %collective-permute-start.2 = (bf16[384,768]{1,0:T(8,128)(2,1)}, bf16[384,768]{1,0:T(8,128)(2,1)S(1)}, u32[]{:S(2)}, u32[]{:S(2)}) collective-permute-start(bf16[384,768]{1,0:T(8,128)(2,1)} %oo.7), channel_id=1, source_target_pairs={{0,32},{32,0},{64,96},{96,64},{1,33},{33,1},{65,97},{97,65},{2,34}... | collective-permute-start | bytes 1769480 | tf_op jit(solution)/shard_map/ppermute | solution.py:510
  13.2 3.1 collective-permute-start
  48.0 14.9 %collective-permute-start.5 = (bf16[320,768]{1,0:T(8,128)(2,1)}, bf16[320,768]{1,0:T(8,128)(2,1)S(1)}, u32[]{:S(2)}, u32[]{:S(2)}) collective-permute-start(bf16[320,768]{1,0:T(8,128)(2,1)} %feed.2), channel_id=1, source_target_pairs={{0,64},{32,96},{1,65},{33,97},{2,66},{34,98},{3,67},{35,99},{4,68}... | collective-permute-start | bytes 1474568 | tf_op jit(solution)/shard_map/ppermute | solution.py:626
  132.1 14.9 %collective-permute-start.6 = (bf16[320,768]{1,0:T(8,128)(2,1)}, bf16[320,768]{1,0:T(8,128)(2,1)S(1)}, u32[]{:S(2)}, u32[]{:S(2)}) collective-permute-start(bf16[320,768]{1,0:T(8,128)(2,1)} %get-tuple-element.60), channel_id=1, source_target_pairs={{64,0},{96,32},{65,1},{97,33},{66,2},{98,34},{67,3},{99,35},{68,4}... | collective-permute-start | bytes 1474568 | tf_op jit(solution)/shard_map/ppermute | solution.py:634
  133.4 18.6 %copy-start.22 = (bf16[320,3072]{1,0:T(8,128)(2,1)S(1)}, bf16[320,3072]{1,0:T(8,128)(2,1)}, u32[]{:S(2)}) copy-start(bf16[320,3072]{1,0:T(8,128)(2,1)} %get-tuple-element.63) | copy-start | bytes 5898244
  152.0 8.8 %copy-start.13 = (bf16[320,768]{1,0:T(8,128)(2,1)S(1)}, bf16[320,768]{1,0:T(8,128)(2,1)}, u32[]{:S(2)}) copy-start(bf16[320,768]{1,0:T(8,128)(2,1)} %get-tuple-element.62.gz) | copy-start | bytes 1474564
  155.9 4.9 %collective-permute-start.7 = (bf16[1536,768]{1,0:T(8,128)(2,1)}, bf16[1536,768]{1,0:T(8,128)(2,1)}, u32[]{:S(2)}, u32[]{:S(2)}) collective-permute-start(bf16[1536,768]{1,0:T(8,128)(2,1)} %convolution_convert_fusion.2), channel_id=1, source_target_pairs={{0,32},{32,0},{64,96},{96,64},{1,33},{33,1},{65,97},{97,65},{2,34}... | collective-permute-start | bytes 7077896 | tf_op jit(solution)/shard_map/ppermute | solution.py:510
  165.6 19.0 %collective-permute-start.40 = (bf16[768,768]{1,0:T(8,128)(2,1)S(1)}, bf16[768,768]{1,0:T(8,128)(2,1)}, u32[]{:S(2)}, u32[]{:S(2)}) collective-permute-start(bf16[768,768]{1,0:T(8,128)(2,1)S(1)} %constant_dynamic-slice_fusion.3), channel_id=1, source_target_pairs={{0,8},{1,9},{2,10},{3,11},{4,12},{5,13},{6,14},{7,15},{8,0},{9,1},... | collective-permute-start | bytes 3538952 | tf_op jit(solution)/shard_map/ppermute | solution.py:543
  167.7 16.9 %copy-start.6 = (bf16[1536,768]{1,0:T(8,128)(2,1)S(1)}, bf16[1536,768]{1,0:T(8,128)(2,1)}, u32[]{:S(2)}) copy-start(bf16[1536,768]{1,0:T(8,128)(2,1)} %copy-done.5) | copy-start | bytes 7077892
  184.6 4.4 %copy-start.18 = (bf16[320,3072]{1,0:T(8,128)(2,1)S(1)}, bf16[320,3072]{1,0:T(8,128)(2,1)}, u32[]{:S(2)}) copy-start(bf16[320,3072]{1,0:T(8,128)(2,1)} %get-tuple-element.66) | copy-start | bytes 5898244
  186.4 2.7 copy-start.20
  186.4 11.2 %collective-permute-start.41 = (bf16[384,768]{1,0:T(8,128)(2,1)S(1)}, bf16[384,768]{1,0:T(8,128)(2,1)S(1)}, u32[]{:S(2)}, u32[]{:S(2)}) collective-permute-start(bf16[384,768]{1,0:T(8,128)(2,1)S(1)} %constant_dynamic-slice_fusion.2), channel_id=1, source_target_pairs={{0,24},{1,25},{2,26},{3,27},{4,28},{5,29},{6,30},{7,31},{8,16},{9,... | collective-permute-start | bytes 1769480 | tf_op jit(solution)/shard_map/ppermute | solution.py:543
  191.9 28.9 %collective-permute-start.8 = (bf16[384,3072]{1,0:T(8,128)(2,1)}, bf16[384,3072]{1,0:T(8,128)(2,1)}, u32[]{:S(2)}, u32[]{:S(2)}) collective-permute-start(bf16[384,3072]{1,0:T(8,128)(2,1)} %convolution_convert_fusion.1), channel_id=1, source_target_pairs={{0,32},{32,0},{64,96},{96,64},{1,33},{33,1},{65,97},{97,65},{2,34}... | collective-permute-start | bytes 7077896 | tf_op jit(solution)/shard_map/ppermute | solution.py:510
  191.9 7.5 %copy-start.7 = (bf16[320,768]{1,0:T(8,128)(2,1)S(1)}, bf16[320,768]{1,0:T(8,128)(2,1)}, u32[]{:S(2)}) copy-start(bf16[320,768]{1,0:T(8,128)(2,1)} %get-tuple-element.64.gb) | copy-start | bytes 1474564
  197.8 6.8 %collective-permute-start.42 = (bf16[192,768]{1,0:T(8,128)(2,1)S(1)}, bf16[192,768]{1,0:T(8,128)(2,1)S(1)}, u32[]{:S(2)}, u32[]{:S(2)}) collective-permute-start(bf16[192,768]{1,0:T(8,128)(2,1)S(1)} %constant_dynamic-slice_fusion.1), channel_id=1, source_target_pairs={{0,2},{1,3},{2,0},{3,1},{4,6},{5,7},{6,4},{7,5},{8,10},{9,11},{10,... | collective-permute-start | bytes 884744 | tf_op jit(solution)/shard_map/ppermute | solution.py:543
  199.4 9.0 %copy-start.17 = (f32[2,4608]{1,0:T(2,128)S(1)}, f32[2,4608]{1,0:T(2,128)}, u32[]{:S(2)}) copy-start(f32[2,4608]{1,0:T(2,128)} %get-tuple-element.72) | copy-start | bytes 110596
  200.8 13.4 %copy-start.12 = (bf16[320,768]{1,0:T(8,128)(2,1)S(1)}, bf16[320,768]{1,0:T(8,128)(2,1)}, u32[]{:S(2)}) copy-start(bf16[320,768]{1,0:T(8,128)(2,1)} %get-tuple-element.70) | copy-start | bytes 1474564
  200.8 13.4 %collective-permute-start.14 = (bf16[384,768]{1,0:T(8,128)(2,1)S(1)}, bf16[384,768]{1,0:T(8,128)(2,1)S(1)}, u32[]{:S(2)}, u32[]{:S(2)}) collective-permute-start(bf16[384,768]{1,0:T(8,128)(2,1)S(1)} %convolution_convert_fusion.3), channel_id=1, source_target_pairs={{0,32},{32,0},{64,96},{96,64},{1,33},{33,1},{65,97},{97,65},{2,34}... | collective-permute-start | bytes 1769480 | tf_op jit(solution)/shard_map/ppermute | solution.py:510
  204.7 6.4 %collective-permute-start.43 = (bf16[96,768]{1,0:T(8,128)(2,1)S(1)}, bf16[96,768]{1,0:T(8,128)(2,1)S(1)}, u32[]{:S(2)}, u32[]{:S(2)}) collective-permute-start(bf16[96,768]{1,0:T(8,128)(2,1)S(1)} %constant_dynamic-slice_fusion), channel_id=1, source_target_pairs={{0,6},{1,7},{2,4},{3,5},{4,2},{5,3},{6,0},{7,1},{8,14},{9,15},{10,... | collective-permute-start | bytes 442376 | tf_op jit(solution)/shard_map/ppermute | solution.py:543
  211.1 9.7 %copy-start.21 = (bf16[320,768]{1,0:T(8,128)(2,1)S(1)}, bf16[320,768]{1,0:T(8,128)(2,1)}, u32[]{:S(2)}) copy-start(bf16[320,768]{1,0:T(8,128)(2,1)} %get-tuple-element.47.u) | copy-start | bytes 1474564
  211.2 9.6 %copy-start.19 = (bf16[320,3072]{1,0:T(8,128)(2,1)S(1)}, bf16[320,3072]{1,0:T(8,128)(2,1)}, u32[]{:S(2)}) copy-start(bf16[320,3072]{1,0:T(8,128)(2,1)} %get-tuple-element.66) | copy-start | bytes 5898244
  211.2 6.7 %collective-permute-start.44 = (bf16[96,768]{1,0:T(8,128)(2,1)S(1)}, bf16[96,768]{1,0:T(8,128)(2,1)S(1)}, u32[]{:S(2)}, u32[]{:S(2)}) collective-permute-start(bf16[96,768]{1,0:T(8,128)(2,1)S(1)} %add_convert_fusion.14), channel_id=1, source_target_pairs={{0,1},{1,0},{2,3},{3,2},{4,5},{5,4},{6,7},{7,6},{8,9},{9,8},{10,11... | collective-permute-start | bytes 442376 | tf_op jit(solution)/shard_map/ppermute | solution.py:543
  218.0 30.1 %collective-permute-start.45 = (bf16[96,768]{1,0:T(8,128)(2,1)S(1)}, bf16[96,768]{1,0:T(8,128)(2,1)S(1)}, u32[]{:S(2)}, u32[]{:S(2)}) collective-permute-start(bf16[96,768]{1,0:T(8,128)(2,1)S(1)} %add_convert_fusion.13), channel_id=1, source_target_pairs={{0,6},{1,7},{2,4},{3,5},{4,2},{5,3},{6,0},{7,1},{8,14},{9,15},{10,... | collective-permute-start | bytes 442376 | tf_op jit(solution)/shard_map/ppermute | solution.py:543
  225.3 16.7 %copy-start.3 = (bf16[384,3072]{1,0:T(8,128)(2,1)S(1)}, bf16[384,3072]{1,0:T(8,128)(2,1)}, u32[]{:S(2)}) copy-start(bf16[384,3072]{1,0:T(8,128)(2,1)} %add_convert_fusion.rest_0_) | copy-start | bytes 7077892
  242.0 3.7 copy-start.8
  242.0 3.7 copy-start.15
  242.0 7.3 %collective-permute-start.15 = (bf16[4608]{0:T(1024)(128)(2,1)S(1)}, bf16[4608]{0:T(1024)(128)(2,1)S(1)}, u32[]{:S(2)}, u32[]{:S(2)}) collective-permute-start(bf16[4608]{0:T(1024)(128)(2,1)S(1)} %convert_reduce_fusion), channel_id=1, source_target_pairs={{0,32},{32,0},{64,96},{96,64},{1,33},{33,1},{65,97},{97,65},{2,34}... | collective-permute-start | bytes 27656 | tf_op jit(solution)/shard_map/ppermute | solution.py:510
  243.2 17.7 %collective-permute-start.31 = (bf16[192,3072]{1,0:T(8,128)(2,1)}, bf16[192,3072]{1,0:T(8,128)(2,1)}, u32[]{:S(2)}, u32[]{:S(2)}) collective-permute-start(bf16[192,3072]{1,0:T(8,128)(2,1)} %constant_dynamic-slice_fusion.7), channel_id=1, source_target_pairs={{0,24},{1,25},{2,26},{3,27},{4,28},{5,29},{6,30},{7,31},{8,16},{9,... | collective-permute-start | bytes 3538952 | tf_op jit(solution)/shard_map/ppermute | solution.py:543
  248.0 21.0 %collective-permute-start.9 = (bf16[384,2304]{1,0:T(8,128)(2,1)}, bf16[384,2304]{1,0:T(8,128)(2,1)}, u32[]{:S(2)}, u32[]{:S(2)}) collective-permute-start(bf16[384,2304]{1,0:T(8,128)(2,1)} %convolution_convert_fusion), channel_id=1, source_target_pairs={{0,32},{32,0},{64,96},{96,64},{1,33},{33,1},{65,97},{97,65},{2,34}... | collective-permute-start | bytes 5308424 | tf_op jit(solution)/shard_map/ppermute | solution.py:510
  248.9 7.4 %collective-permute-start.46 = (bf16[192,768]{1,0:T(8,128)(2,1)}, bf16[192,768]{1,0:T(8,128)(2,1)}, u32[]{:S(2)}, u32[]{:S(2)}) collective-permute-start(bf16[192,768]{1,0:T(8,128)(2,1)} %pad_maximum_fusion.12), channel_id=1, source_target_pairs={{0,2},{1,3},{2,0},{3,1},{4,6},{5,7},{6,4},{7,5},{8,10},{9,11},{10,... | collective-permute-start | bytes 884744 | tf_op jit(solution)/shard_map/ppermute | solution.py:543
  257.4 11.2 %collective-permute-start.47 = (bf16[384,768]{1,0:T(8,128)(2,1)S(1)}, bf16[384,768]{1,0:T(8,128)(2,1)S(1)}, u32[]{:S(2)}, u32[]{:S(2)}) collective-permute-start(bf16[384,768]{1,0:T(8,128)(2,1)S(1)} %pad_maximum_fusion.7), channel_id=1, source_target_pairs={{0,24},{1,25},{2,26},{3,27},{4,28},{5,29},{6,30},{7,31},{8,16},{9,... | collective-permute-start | bytes 1769480 | tf_op jit(solution)/shard_map/ppermute | solution.py:543
  262.6 10.4 %collective-permute-start.32 = (bf16[96,3072]{1,0:T(8,128)(2,1)S(1)}, bf16[96,3072]{1,0:T(8,128)(2,1)S(1)}, u32[]{:S(2)}, u32[]{:S(2)}) collective-permute-start(bf16[96,3072]{1,0:T(8,128)(2,1)S(1)} %constant_dynamic-slice_fusion.6), channel_id=1, source_target_pairs={{0,8},{1,9},{2,10},{3,11},{4,12},{5,13},{6,14},{7,15},{8,0},{9,1},... | collective-permute-start | bytes 1769480 | tf_op jit(solution)/shard_map/ppermute | solution.py:543
  268.9 17.9 %collective-permute-start.48 = (bf16[768,768]{1,0:T(8,128)(2,1)S(1)}, bf16[768,768]{1,0:T(8,128)(2,1)S(1)}, u32[]{:S(2)}, u32[]{:S(2)}) collective-permute-start(bf16[768,768]{1,0:T(8,128)(2,1)S(1)} %pad_maximum_fusion.1), channel_id=1, source_target_pairs={{0,8},{1,9},{2,10},{3,11},{4,12},{5,13},{6,14},{7,15},{8,0},{9,1},... | collective-permute-start | bytes 3538952 | tf_op jit(solution)/shard_map/ppermute | solution.py:543
  273.2 11.2 %collective-permute-start.33 = (bf16[48,3072]{1,0:T(8,128)(2,1)S(1)}, bf16[48,3072]{1,0:T(8,128)(2,1)S(1)}, u32[]{:S(2)}, u32[]{:S(2)}) collective-permute-start(bf16[48,3072]{1,0:T(8,128)(2,1)S(1)} %constant_dynamic-slice_fusion.5), channel_id=1, source_target_pairs={{0,6},{1,7},{2,4},{3,5},{4,2},{5,3},{6,0},{7,1},{8,14},{9,15},{10,... | collective-permute-start | bytes 884744 | tf_op jit(solution)/shard_map/ppermute | solution.py:543
  274.2 24.0 %collective-permute-start.10 = (bf16[192,1536]{1,0:T(8,128)(2,1)S(1)}, bf16[192,1536]{1,0:T(8,128)(2,1)S(1)}, u32[]{:S(2)}, u32[]{:S(2)}) collective-permute-start(bf16[192,1536]{1,0:T(8,128)(2,1)S(1)} %constant_dynamic-slice_fusion.14), channel_id=1, source_target_pairs={{0,8},{1,9},{2,10},{3,11},{4,12},{5,13},{6,14},{7,15},{8,0},{9,1},... | collective-permute-start | bytes 1769480 | tf_op jit(solution)/shard_map/ppermute | solution.py:543
  275.2 25.4 %collective-permute-start.16 = (bf16[200,1536]{1,0:T(8,128)(2,1)S(1)}, bf16[200,1536]{1,0:T(8,128)(2,1)S(1)}, u32[]{:S(2)}, u32[]{:S(2)}) collective-permute-start(bf16[200,1536]{1,0:T(8,128)(2,1)S(1)} %pad_maximum_fusion.2), channel_id=1, source_target_pairs={{0,24},{1,25},{2,26},{3,27},{4,28},{5,29},{6,30},{7,31},{8,16},{9,... | collective-permute-start | bytes 1843208 | tf_op jit(solution)/shard_map/ppermute | solution.py:543
  284.5 6.9 %collective-permute-start.34 = (bf16[24,3072]{1,0:T(8,128)(2,1)S(1)}, bf16[24,3072]{1,0:T(8,128)(2,1)S(1)}, u32[]{:S(2)}, u32[]{:S(2)}) collective-permute-start(bf16[24,3072]{1,0:T(8,128)(2,1)S(1)} %constant_dynamic-slice_fusion.4), channel_id=1, source_target_pairs={{0,2},{1,3},{2,0},{3,1},{4,6},{5,7},{6,4},{7,5},{8,10},{9,11},{10,... | collective-permute-start | bytes 442376 | tf_op jit(solution)/shard_map/ppermute | solution.py:543
  291.4 6.7 %collective-permute-start.35 = (bf16[24,3072]{1,0:T(8,128)(2,1)S(1)}, bf16[24,3072]{1,0:T(8,128)(2,1)S(1)}, u32[]{:S(2)}, u32[]{:S(2)}) collective-permute-start(bf16[24,3072]{1,0:T(8,128)(2,1)S(1)} %add_convert_fusion.16), channel_id=1, source_target_pairs={{0,1},{1,0},{2,3},{3,2},{4,5},{5,4},{6,7},{7,6},{8,9},{9,8},{10,11... | collective-permute-start | bytes 442376 | tf_op jit(solution)/shard_map/ppermute | solution.py:543
  298.2 5.2 %collective-permute-start.36 = (bf16[24,3072]{1,0:T(8,128)(2,1)S(1)}, bf16[24,3072]{1,0:T(8,128)(2,1)S(1)}, u32[]{:S(2)}, u32[]{:S(2)}) collective-permute-start(bf16[24,3072]{1,0:T(8,128)(2,1)S(1)} %add_convert_fusion.15), channel_id=1, source_target_pairs={{0,2},{1,3},{2,0},{3,1},{4,6},{5,7},{6,4},{7,5},{8,10},{9,11},{10,... | collective-permute-start | bytes 442376 | tf_op jit(solution)/shard_map/ppermute | solution.py:543
  298.5 10.6 %collective-permute-start.11 = (bf16[96,1536]{1,0:T(8,128)(2,1)S(1)}, bf16[96,1536]{1,0:T(8,128)(2,1)S(1)}, u32[]{:S(2)}, u32[]{:S(2)}) collective-permute-start(bf16[96,1536]{1,0:T(8,128)(2,1)S(1)} %constant_dynamic-slice_fusion.13), channel_id=1, source_target_pairs={{0,24},{1,25},{2,26},{3,27},{4,28},{5,29},{6,30},{7,31},{8,16},{9,... | collective-permute-start | bytes 884744 | tf_op jit(solution)/shard_map/ppermute | solution.py:543
  300.9 8.6 %collective-permute-start.17 = (bf16[104,1536]{1,0:T(8,128)(2,1)S(1)}, bf16[104,1536]{1,0:T(8,128)(2,1)S(1)}, u32[]{:S(2)}, u32[]{:S(2)}) collective-permute-start(bf16[104,1536]{1,0:T(8,128)(2,1)S(1)} %pad_maximum_fusion.8), channel_id=1, source_target_pairs={{0,8},{1,9},{2,10},{3,11},{4,12},{5,13},{6,14},{7,15},{8,0},{9,1},... | collective-permute-start | bytes 958472 | tf_op jit(solution)/shard_map/ppermute | solution.py:543
  303.5 8.4 %collective-permute-start.37 = (bf16[48,3072]{1,0:T(8,128)(2,1)S(1)}, bf16[48,3072]{1,0:T(8,128)(2,1)S(1)}, u32[]{:S(2)}, u32[]{:S(2)}) collective-permute-start(bf16[48,3072]{1,0:T(8,128)(2,1)S(1)} %pad_maximum_fusion.11), channel_id=1, source_target_pairs={{0,6},{1,7},{2,4},{3,5},{4,2},{5,3},{6,0},{7,1},{8,14},{9,15},{10,... | collective-permute-start | bytes 884744 | tf_op jit(solution)/shard_map/ppermute | solution.py:543
  309.2 5.2 %collective-permute-start.12 = (bf16[48,1536]{1,0:T(8,128)(2,1)S(1)}, bf16[48,1536]{1,0:T(8,128)(2,1)S(1)}, u32[]{:S(2)}, u32[]{:S(2)}) collective-permute-start(bf16[48,1536]{1,0:T(8,128)(2,1)S(1)} %constant_dynamic-slice_fusion.12), channel_id=1, source_target_pairs={{0,2},{1,3},{2,0},{3,1},{4,6},{5,7},{6,4},{7,5},{8,10},{9,11},{10,... | collective-permute-start | bytes 442376 | tf_op jit(solution)/shard_map/ppermute | solution.py:543
  309.6 6.7 %collective-permute-start.18 = (bf16[56,1536]{1,0:T(8,128)(2,1)S(1)}, bf16[56,1536]{1,0:T(8,128)(2,1)S(1)}, u32[]{:S(2)}, u32[]{:S(2)}) collective-permute-start(bf16[56,1536]{1,0:T(8,128)(2,1)S(1)} %pad_maximum_fusion.13), channel_id=1, source_target_pairs={{0,6},{1,7},{2,4},{3,5},{4,2},{5,3},{6,0},{7,1},{8,14},{9,15},{10,... | collective-permute-start | bytes 516104 | tf_op jit(solution)/shard_map/ppermute | solution.py:543
  314.5 5.6 %collective-permute-start.13 = (bf16[24,1536]{1,0:T(8,128)(2,1)S(1)}, bf16[24,1536]{1,0:T(8,128)(2,1)S(1)}, u32[]{:S(2)}, u32[]{:S(2)}) collective-permute-start(bf16[24,1536]{1,0:T(8,128)(2,1)S(1)} %constant_dynamic-slice_fusion.11), channel_id=1, source_target_pairs={{0,6},{1,7},{2,4},{3,5},{4,2},{5,3},{6,0},{7,1},{8,14},{9,15},{10,... | collective-permute-start | bytes 221192 | tf_op jit(solution)/shard_map/ppermute | solution.py:543
  316.4 5.8 %collective-permute-start.19 = (bf16[32,1536]{1,0:T(8,128)(2,1)S(1)}, bf16[32,1536]{1,0:T(8,128)(2,1)S(1)}, u32[]{:S(2)}, u32[]{:S(2)}) collective-permute-start(bf16[32,1536]{1,0:T(8,128)(2,1)S(1)} %pad_maximum_fusion.17), channel_id=1, source_target_pairs={{0,2},{1,3},{2,0},{3,1},{4,6},{5,7},{6,4},{7,5},{8,10},{9,11},{10,... | collective-permute-start | bytes 294920 | tf_op jit(solution)/shard_map/ppermute | solution.py:543
  322.3 7.0 %collective-permute-start.20 = (bf16[56,1536]{1,0:T(8,128)(2,1)S(1)}, bf16[56,1536]{1,0:T(8,128)(2,1)S(1)}, u32[]{:S(2)}, u32[]{:S(2)}) collective-permute-start(bf16[56,1536]{1,0:T(8,128)(2,1)S(1)} %pad_maximum_fusion.14), channel_id=1, source_target_pairs={{0,1},{1,0},{2,3},{3,2},{4,5},{5,4},{6,7},{7,6},{8,9},{9,8},{10,11... | collective-permute-start | bytes 516104 | tf_op jit(solution)/shard_map/ppermute | solution.py:543
  325.1 23.6 %collective-permute-start.38 = (bf16[96,3072]{1,0:T(8,128)(2,1)S(1)}, bf16[96,3072]{1,0:T(8,128)(2,1)S(1)}, u32[]{:S(2)}, u32[]{:S(2)}) collective-permute-start(bf16[96,3072]{1,0:T(8,128)(2,1)S(1)} %pad_maximum_fusion.6), channel_id=1, source_target_pairs={{0,8},{1,9},{2,10},{3,11},{4,12},{5,13},{6,14},{7,15},{8,0},{9,1},... | collective-permute-start | bytes 1769480 | tf_op jit(solution)/shard_map/ppermute | solution.py:543
  329.4 1.2 collective-permute-start.21
  330.6 3.7 collective-permute-start.22
  331.9 5.6 %collective-permute-start.23 = (bf16[24,1536]{1,0:T(8,128)(2,1)S(1)}, bf16[24,1536]{1,0:T(8,128)(2,1)S(1)}, u32[]{:S(2)}, u32[]{:S(2)}) collective-permute-start(bf16[24,1536]{1,0:T(8,128)(2,1)S(1)} %get-tuple-element.111), channel_id=1, source_target_pairs={{0,6},{1,7},{2,4},{3,5},{4,2},{5,3},{6,0},{7,1},{8,14},{9,15},{10,... | collective-permute-start | bytes 221192 | tf_op jit(solution)/shard_map/ppermute | solution.py:543
  334.1 4.4 %collective-permute-start.27 = (bf16[24,1536]{1,0:T(8,128)(2,1)S(1)}, bf16[24,1536]{1,0:T(8,128)(2,1)S(1)}, u32[]{:S(2)}, u32[]{:S(2)}) collective-permute-start(bf16[24,1536]{1,0:T(8,128)(2,1)S(1)} %get-tuple-element.112), channel_id=1, source_target_pairs={{0,2},{1,3},{2,0},{3,1},{4,6},{5,7},{6,4},{7,5},{8,10},{9,11},{10,... | collective-permute-start | bytes 221192 | tf_op jit(solution)/shard_map/ppermute | solution.py:543
  338.5 6.4 %collective-permute-start.28 = (bf16[48,1536]{1,0:T(8,128)(2,1)S(1)}, bf16[48,1536]{1,0:T(8,128)(2,1)S(1)}, u32[]{:S(2)}, u32[]{:S(2)}) collective-permute-start(bf16[48,1536]{1,0:T(8,128)(2,1)S(1)} %pad_maximum_fusion.16), channel_id=1, source_target_pairs={{0,6},{1,7},{2,4},{3,5},{4,2},{5,3},{6,0},{7,1},{8,14},{9,15},{10,... | collective-permute-start | bytes 442376 | tf_op jit(solution)/shard_map/ppermute | solution.py:543
  339.8 5.3 %collective-permute-start.24 = (bf16[48,1536]{1,0:T(8,128)(2,1)S(1)}, bf16[48,1536]{1,0:T(8,128)(2,1)S(1)}, u32[]{:S(2)}, u32[]{:S(2)}) collective-permute-start(bf16[48,1536]{1,0:T(8,128)(2,1)S(1)} %pad_maximum_fusion.15), channel_id=1, source_target_pairs={{0,2},{1,3},{2,0},{3,1},{4,6},{5,7},{6,4},{7,5},{8,10},{9,11},{10,... | collective-permute-start | bytes 442376 | tf_op jit(solution)/shard_map/ppermute | solution.py:543
  345.0 6.8 %collective-permute-start.29 = (bf16[96,1536]{1,0:T(8,128)(2,1)S(1)}, bf16[96,1536]{1,0:T(8,128)(2,1)S(1)}, u32[]{:S(2)}, u32[]{:S(2)}) collective-permute-start(bf16[96,1536]{1,0:T(8,128)(2,1)S(1)} %pad_maximum_fusion.10), channel_id=1, source_target_pairs={{0,8},{1,9},{2,10},{3,11},{4,12},{5,13},{6,14},{7,15},{8,0},{9,1},... | collective-permute-start | bytes 884744 | tf_op jit(solution)/shard_map/ppermute | solution.py:543
  345.2 9.3 %collective-permute-start.25 = (bf16[96,1536]{1,0:T(8,128)(2,1)S(1)}, bf16[96,1536]{1,0:T(8,128)(2,1)S(1)}, u32[]{:S(2)}, u32[]{:S(2)}) collective-permute-start(bf16[96,1536]{1,0:T(8,128)(2,1)S(1)} %pad_maximum_fusion.9), channel_id=1, source_target_pairs={{0,24},{1,25},{2,26},{3,27},{4,28},{5,29},{6,30},{7,31},{8,16},{9,... | collective-permute-start | bytes 884744 | tf_op jit(solution)/shard_map/ppermute | solution.py:543
  349.1 27.4 %collective-permute-start.39 = (bf16[192,3072]{1,0:T(8,128)(2,1)S(1)}, bf16[192,3072]{1,0:T(8,128)(2,1)S(1)}, u32[]{:S(2)}, u32[]{:S(2)}) collective-permute-start(bf16[192,3072]{1,0:T(8,128)(2,1)S(1)} %pad_maximum_fusion), channel_id=1, source_target_pairs={{0,24},{1,25},{2,26},{3,27},{4,28},{5,29},{6,30},{7,31},{8,16},{9,... | collective-permute-start | bytes 3538952 | tf_op jit(solution)/shard_map/ppermute | solution.py:543
  352.0 20.9 %collective-permute-start.30 = (bf16[192,1536]{1,0:T(8,128)(2,1)S(1)}, bf16[192,1536]{1,0:T(8,128)(2,1)S(1)}, u32[]{:S(2)}, u32[]{:S(2)}) collective-permute-start(bf16[192,1536]{1,0:T(8,128)(2,1)S(1)} %pad_maximum_fusion.5), channel_id=1, source_target_pairs={{0,24},{1,25},{2,26},{3,27},{4,28},{5,29},{6,30},{7,31},{8,16},{9,... | collective-permute-start | bytes 1769480 | tf_op jit(solution)/shard_map/ppermute | solution.py:543
  354.7 19.5 %collective-permute-start.26 = (bf16[192,1536]{1,0:T(8,128)(2,1)S(1)}, bf16[192,1536]{1,0:T(8,128)(2,1)S(1)}, u32[]{:S(2)}, u32[]{:S(2)}) collective-permute-start(bf16[192,1536]{1,0:T(8,128)(2,1)S(1)} %pad_maximum_fusion.4), channel_id=1, source_target_pairs={{0,8},{1,9},{2,10},{3,11},{4,12},{5,13},{6,14},{7,15},{8,0},{9,1},... | collective-permute-start | bytes 1769480 | tf_op jit(solution)/shard_map/ppermute | solution.py:543
  377.0 2.8 copy-start.1
  (8 other events, 8.6 us)
